TPU v7x, 32 devices: a whole 2x2x4 slice. The times are simulated.
32 devices in a mesh: img: 4 (over y, x), ch: 8 (over z, core).
Axes of the slice: x: 2, y: 2, z: 4, core: 2. Of those that a mesh axis runs over, the one named last changes fastest.
Arguments:
- images_in: bfloat16 [256, 49, 2048], P('img'), may hold values from -6 to 6
- labels: int32 [256], P(('img', 'ch')), may hold values from 0 to 999
- loss_wt: int32 [256], P(('img', 'ch')), may hold values from 1 to 32
- placement: int32 [4, 64], P('img'), may hold values from 0 to 63, each once within a row
- w_one: float32 [2048, 512], P(None, 'ch'), may hold values from -0.125 to 0.125
- mom_one: float32 [2048, 512], P(None, 'ch'), may hold values from -0.0029296875 to 0.0029296875
- avg_one: float32 [2048, 512], P(None, 'ch'), may hold values from -0.125 to 0.125
- mask_one: int32 [2048, 512], P(None, 'ch'), may hold values 0 or 1
- rank_one: int32 [2048, 512], P(None, 'ch'), may hold values from 0 to 99
- first_norm_params: float32 [2, 512], P(None, 'ch'), may hold values from 0.5 to 1.5
- mom_bn_one: float32 [2, 512], P(None, 'ch'), may hold values from -0.001953125 to 0.001953125
- avg_bn_one: float32 [2, 512], P(None, 'ch'), may hold values from 0.5 to 1.5
- w_two: float32 [2359296], P(('img', 'ch')), may hold values from -0.09375 to 0.09375
- mom_two: float32 [2359296], P(('img', 'ch')), may hold values from -0.01171875 to 0.01171875
- avg_two: float32 [2359296], P(('img', 'ch')), may hold values from -0.09375 to 0.09375
- mask_two: int32 [2359296], P(('img', 'ch')), may hold values 0 or 1
- rank_two: int32 [2359296], P(('img', 'ch')), may hold values from 0 to 99
- second_norm_params: float32 [2, 512], replicated, may hold values from 0.5 to 1.5
- mom_bn_two: float32 [2, 512], replicated, may hold values from -0.01953125 to 0.01953125
- avg_bn_two: float32 [2, 512], replicated, may hold values from 0.5 to 1.5
- w_head: float32 [512000], P(('img', 'ch')), may hold values from -0.75 to 0.75
- mom_head: float32 [512000], P(('img', 'ch')), may hold values from -0.0029296875 to 0.0029296875
- avg_head: float32 [512000], P(('img', 'ch')), may hold values from -0.75 to 0.75
Outputs:
- loss: float32 [], replicated
- new_w_one: float32 [2048, 512], P(None, 'ch')
- new_mom_one: float32 [2048, 512], P(None, 'ch')
- new_avg_one: float32 [2048, 512], P(None, 'ch')
- new_mask_one: int32 [2048, 512], P(None, 'ch')
- copy_w_one: bfloat16 [2048, 512], P(None, 'ch')
- new_bn_one: float32 [2, 512], P(None, 'ch')
- new_mom_bn_one: float32 [2, 512], P(None, 'ch')
- new_avg_bn_one: float32 [2, 512], P(None, 'ch')
- new_w_two: float32 [2359296], P(('img', 'ch'))
- new_mom_two: float32 [2359296], P(('img', 'ch'))
- new_avg_two: float32 [2359296], P(('img', 'ch'))
- new_mask_two: int32 [2359296], P(('img', 'ch'))
- copy_w_two: bfloat16 [2359296], P(('img', 'ch'))
- new_bn_two: float32 [2, 512], replicated
- new_mom_bn_two: float32 [2, 512], replicated
- new_avg_bn_two: float32 [2, 512], replicated
- new_w_head: float32 [512000], P(('img', 'ch'))
- new_mom_head: float32 [512000], P(('img', 'ch'))
- new_avg_head: float32 [512000], P(('img', 'ch'))
- copy_w_head: bfloat16 [512000], P(('img', 'ch'))
Inputs may be any that keep to these rules, and one draw needn't show every extreme that they name: `placement`: each row is a permutation of 0 to 63.
All inputs are finite; a program needn't handle non-finite values. No bound on the sum of `mask_one` or of `mask_two` on one device may be relied on, other than what follows from the above.
Results may differ from a plain program's by a relative error of at most 0.013.
Values may be sent and summed in bfloat16 or wider, within the bound.
A program may use at most 512 MiB of HBM per device.

v0:
```python
import math

import jax
import jax.numpy as jnp
from jax import lax
from jax.sharding import PartitionSpec as P

SIDE = 7
PIX = 49
DROP = 10
GROW = 10


EPS = 1e-05
MOMENTUM = 0.5


def advance(weight, grad, velocity, rate):
    velocity = MOMENTUM * velocity + grad
    return (weight - rate * (grad + MOMENTUM * velocity), velocity)


def dense_update(weight, grad, velocity, average, rate):
    moved, velocity = advance(weight, grad, velocity, rate)
    return (moved, velocity, 0.5 * average + 0.5 * moved)


def sparse_update(weight, grad, velocity, average, mask, rank, rate):
    moved, velocity = advance(weight, grad, velocity, rate)
    kept = (mask == 1) & (rank >= DROP)
    grown = (mask == 0) & (rank < GROW)
    new_mask = jnp.where(kept | grown, 1, 0).astype(jnp.int32)
    weight = jnp.where(kept, moved, 0.0)
    velocity = jnp.where(kept, velocity, 0.0)
    average = 0.5 * average + 0.5 * weight
    return (weight, velocity, average, new_mask, weight.astype(jnp.bfloat16))


def silu_slope(value):
    sigma = jax.nn.sigmoid(value)
    return sigma * (1.0 + value * (1.0 - sigma))


def apply_batch_norm(z, sums, squares, element_count):
    mean = sums / element_count
    inverse_deviation = lax.rsqrt(squares / element_count - mean * mean + EPS)
    return ((z - mean) * inverse_deviation, inverse_deviation)


def batch_norm_backward(
    norm_gain,
    inverse_deviation,
    output_gradient,
    standardized_input,
    bias_gradient_sum,
    gain_gradient_sum,
    element_count,
):
    return (
        norm_gain
        * inverse_deviation
        * (
            output_gradient
            - bias_gradient_sum / element_count
            - standardized_input * gain_gradient_sum / element_count
        )
    )


def contract_rows(left, right):
    return jnp.einsum("pk,pc->kc", left, right, preferred_element_type=jnp.float32)


def shards(
    images_in,
    labels,
    loss_wt,
    placement,
    w_one,
    mom_one,
    avg_one,
    mask_one,
    rank_one,
    first_norm_params,
    mom_bn_one,
    avg_bn_one,
    w_two,
    mom_two,
    avg_two,
    mask_two,
    rank_two,
    second_norm_params,
    mom_bn_two,
    avg_bn_two,
    w_head,
    mom_head,
    avg_head,
):
    n_img = lax.axis_size("img")
    n_ch = lax.axis_size("ch")
    group = images_in.shape[0]
    element_count = labels.shape[0]
    width = second_norm_params.shape[1]
    classes = w_head.shape[0] * n_img * n_ch // width
    images = element_count * n_img * n_ch
    weights = loss_wt.astype(jnp.float32)
    local_total = jnp.sum(weights)
    total = lax.psum(local_total, ("img", "ch"))
    kernel_part = (w_two * mask_two.astype(jnp.float32)).astype(jnp.bfloat16)
    kernel, head = (
        lax.all_gather(kernel_part, ("img", "ch"), axis=0, tiled=True),
        lax.all_gather(w_head.astype(jnp.bfloat16), ("img", "ch"), axis=0, tiled=True),
    )
    kernel = kernel.reshape(9 * width, width)
    head = head.reshape(width, classes)
    rows = images_in.reshape(group * PIX, images_in.shape[2])
    filt_one = (w_one * mask_one.astype(jnp.float32)).astype(jnp.bfloat16)
    first_conv_output = jnp.dot(rows, filt_one, preferred_element_type=jnp.float32)
    first_feature_sum, first_squares_sum = lax.psum(
        (
            jnp.sum(first_conv_output, axis=0),
            jnp.sum(first_conv_output * first_conv_output, axis=0),
        ),
        "img",
    )
    first_element_count = group * PIX * n_img
    first_standardized_input, first_inverse_deviation = apply_batch_norm(
        first_conv_output, first_feature_sum, first_squares_sum, first_element_count
    )
    first_norm_output = first_norm_params[0] * first_standardized_input + first_norm_params[1]
    first_activation_map = jax.nn.silu(first_norm_output).astype(jnp.bfloat16)
    ordered = first_activation_map.reshape(group, PIX, first_activation_map.shape[1])[placement[0]]
    act_in = lax.all_to_all(ordered, "ch", split_axis=0, concat_axis=2, tiled=True)
    padded = jnp.pad(
        act_in.reshape(element_count, SIDE, SIDE, width), ((0, 0), (1, 1), (1, 1), (0, 0))
    )
    patches = jnp.concatenate(
        [
            padded[:, tap // 3 : tap // 3 + SIDE, tap % 3 : tap % 3 + SIDE, :].reshape(
                element_count * PIX, width
            )
            for tap in range(9)
        ],
        axis=1,
    )
    second_conv_output = jnp.dot(patches, kernel, preferred_element_type=jnp.float32)
    s_two = jnp.sum(second_conv_output, axis=0)
    q_two = jnp.sum(second_conv_output * second_conv_output, axis=0)
    second_feature_sum, second_squares_sum = lax.psum((s_two, q_two), ("img", "ch"))
    second_element_count = images * PIX
    second_standardized_input, second_inverse_deviation = apply_batch_norm(
        second_conv_output, second_feature_sum, second_squares_sum, second_element_count
    )
    second_norm_output = second_norm_params[0] * second_standardized_input + second_norm_params[1]
    pooled = jnp.mean(jax.nn.silu(second_norm_output).reshape(element_count, PIX, width), axis=1)
    pooled_low = pooled.astype(jnp.bfloat16)
    logits = jnp.dot(pooled_low, head, preferred_element_type=jnp.float32)
    top = jnp.max(logits, axis=1, keepdims=True)
    expd = jnp.exp(logits - top)
    denom = jnp.sum(expd, axis=1, keepdims=True)
    lse = top[:, 0] + jnp.log(denom[:, 0])
    onehot = labels[:, None] == jnp.arange(classes, dtype=jnp.int32)[None, :]
    picked = jnp.sum(jnp.where(onehot, logits, 0.0), axis=1)
    share = weights / total
    partial_loss_value = jnp.sum(share * (lse - picked))
    d_logits = (share[:, None] * (expd / denom - onehot.astype(jnp.float32))).astype(jnp.bfloat16)
    g_head = contract_rows(pooled_low, d_logits)
    d_pooled = jnp.einsum("ic,kc->ik", d_logits, head, preferred_element_type=jnp.float32)
    d_act = jnp.broadcast_to(d_pooled[:, None, :] / PIX, (element_count, PIX, width)).reshape(
        element_count * PIX, width
    )
    second_output_gradient = d_act * silu_slope(second_norm_output)
    second_shift_bias, second_norm_gain, loss = lax.psum(
        (
            jnp.sum(second_output_gradient, axis=0),
            jnp.sum(second_output_gradient * second_standardized_input, axis=0),
            partial_loss_value,
        ),
        ("img", "ch"),
    )
    second_preact_gradient = batch_norm_backward(
        second_norm_params[0],
        second_inverse_deviation,
        second_output_gradient,
        second_standardized_input,
        second_shift_bias,
        second_norm_gain,
        second_element_count,
    ).astype(jnp.bfloat16)
    g_kernel = contract_rows(patches, second_preact_gradient)
    d_patches = jnp.einsum(
        "pc,kc->pk", second_preact_gradient, kernel, preferred_element_type=jnp.float32
    )
    d_pad = jnp.zeros((element_count, SIDE + 2, SIDE + 2, width), jnp.float32)
    for tap in range(9):
        piece = d_patches[:, tap * width : (tap + 1) * width].reshape(
            element_count, SIDE, SIDE, width
        )
        d_pad = d_pad.at[:, tap // 3 : tap // 3 + SIDE, tap % 3 : tap % 3 + SIDE, :].add(piece)
    d_act_in = d_pad[:, 1:-1, 1:-1, :].astype(jnp.bfloat16).reshape(element_count, PIX, width)
    d_ordered = lax.all_to_all(d_act_in, "ch", split_axis=2, concat_axis=0, tiled=True)
    d_act_one = jnp.zeros_like(d_ordered).at[placement[0]].set(d_ordered)
    d_act_one = d_act_one.reshape(group * PIX, d_ordered.shape[2]).astype(jnp.float32)
    first_output_gradient = d_act_one * silu_slope(first_norm_output)
    first_shift_bias, first_norm_gain = lax.psum(
        (
            jnp.sum(first_output_gradient, axis=0),
            jnp.sum(first_output_gradient * first_standardized_input, axis=0),
        ),
        "img",
    )
    first_preact_gradient = batch_norm_backward(
        first_norm_params[0],
        first_inverse_deviation,
        first_output_gradient,
        first_standardized_input,
        first_shift_bias,
        first_norm_gain,
        first_element_count,
    ).astype(jnp.bfloat16)
    g_filt = lax.psum(
        contract_rows(rows, first_preact_gradient).astype(jnp.bfloat16), "img"
    ).astype(jnp.float32)
    g_one = g_filt * mask_one.astype(jnp.float32)
    flat_two = g_kernel.reshape(-1)
    flat_head = g_head.reshape(-1)
    whole_two, whole_head = lax.psum((flat_two, flat_head), ("img", "ch"))
    slot = lax.axis_index(("img", "ch"))
    part_two = lax.dynamic_slice_in_dim(whole_two, slot * w_two.shape[0], w_two.shape[0])
    part_head = lax.dynamic_slice_in_dim(whole_head, slot * w_head.shape[0], w_head.shape[0])
    g_two = part_two * mask_two.astype(jnp.float32)
    root = math.sqrt(images)
    one = sparse_update(w_one, g_one, mom_one, avg_one, mask_one, rank_one, 1.3 * root)
    bno = dense_update(
        first_norm_params,
        jnp.stack([first_norm_gain, first_shift_bias]),
        mom_bn_one,
        avg_bn_one,
        8.0 * root,
    )
    two = sparse_update(w_two, g_two, mom_two, avg_two, mask_two, rank_two, 0.25 * root)
    bnt = dense_update(
        second_norm_params,
        jnp.stack([second_norm_gain, second_shift_bias]),
        mom_bn_two,
        avg_bn_two,
        root,
    )
    top_head = dense_update(w_head, part_head, mom_head, avg_head, 40.0)
    return (
        loss,
        one[0],
        one[1],
        one[2],
        one[3],
        one[4],
        bno[0],
        bno[1],
        bno[2],
        two[0],
        two[1],
        two[2],
        two[3],
        two[4],
        bnt[0],
        bnt[1],
        bnt[2],
        top_head[0],
        top_head[1],
        top_head[2],
        top_head[0].astype(jnp.bfloat16),
    )


def solution(mesh):
    in_specs = (
        P("img", None, None),
        P(("img", "ch")),
        P(("img", "ch")),
        P("img", None),
        P(None, "ch"),
        P(None, "ch"),
        P(None, "ch"),
        P(None, "ch"),
        P(None, "ch"),
        P(None, "ch"),
        P(None, "ch"),
        P(None, "ch"),
        P(("img", "ch")),
        P(("img", "ch")),
        P(("img", "ch")),
        P(("img", "ch")),
        P(("img", "ch")),
        P(),
        P(),
        P(),
        P(("img", "ch")),
        P(("img", "ch")),
        P(("img", "ch")),
    )
    out_specs = (
        P(),
        P(None, "ch"),
        P(None, "ch"),
        P(None, "ch"),
        P(None, "ch"),
        P(None, "ch"),
        P(None, "ch"),
        P(None, "ch"),
        P(None, "ch"),
        P(("img", "ch")),
        P(("img", "ch")),
        P(("img", "ch")),
        P(("img", "ch")),
        P(("img", "ch")),
        P(),
        P(),
        P(),
        P(("img", "ch")),
        P(("img", "ch")),
        P(("img", "ch")),
        P(("img", "ch")),
    )
    return jax.shard_map(shards, mesh=mesh, in_specs=in_specs, out_specs=out_specs, check_vma=False)
```

profile of v0, /device:TPU:1, one launch (start us, length us, event | category | flops | bytes accessed | tf_op | source)
XLA Modules:
  0.0 708.4 jit_solution(10829418269710759824)
XLA Ops:
  9.0 16.3 %copy.114 = bf16[64,49,2048]{2,1,0:T(8,128)(2,1)} copy(bf16[64,49,2048]{2,0,1:T(8,128)(2,1)} %param.41) | data formatting | bytes 25690112 | tf_op args[0]
  25.3 13.4 %reshape.534 = bf16[3136,2048]{1,0:T(8,128)(2,1)} reshape(bf16[64,49,2048]{2,1,0:T(8,128)(2,1)} %copy.114) | data formatting | bytes 25690112 | tf_op jit(solution)/shard_map/reshape | solution.py:116
  38.7 8.9 %fusion.28 = (f32[64]{0:T(128)S(1)}, f32[64]{0:T(128)S(1)}, f32[64,3136]{1,0:T(8,128)S(1)}) fusion(bf16[3136,2048]{1,0:T(8,128)(2,1)} %reshape.534, f32[2048,64]{0,1:T(8,128)S(1)} %copy-done.7, s32[2048,64]{0,1:T(8,128)S(1)} %copy-done), kind=kOutput, calls=%fused_computation.120 | convolution fusion | flops 823078784 | bytes 14696960 | tf_op jit(solution)/shard_map/dot_general | solution.py:118
  47.6 8.6 %all-reduce.6 = (f32[64]{0:T(128)S(1)}, f32[64]{0:T(128)S(1)}) all-reduce(f32[64]{0:T(128)S(1)} %get-tuple-element.132, f32[64]{0:T(128)S(1)} %get-tuple-element.131), channel_id=1, replica_groups=mesh['img'=4,'ch'=8] {'img'}, use_global_device_ids=true, to_apply=%region_5.0 | all-reduce | flops 128 | bytes 1024 | tf_op jit(solution)/shard_map/psum | solution.py:119
  56.6 3.1 reshape.535
  63.1 7.6 %all-to-all-start = ((bf16[8,2,12544]{2,1,0:T(2,128)(2,1)}), bf16[8,2,12544]{2,1,0:T(2,128)(2,1)S(1)}, u32[]{:S(2)}, u32[]{:S(2)}) async-start(bf16[8,2,12544]{2,1,0:T(2,128)(2,1)} %reshape.586), calls=%async_computation | async-start | bytes 802816 | tf_op jit(solution)/shard_map/all_to_all | solution.py:133
  70.8 56.4 %all-gather = bf16[32,1,16000]{2,1,0:T(2,128)(2,1)S(1)} all-gather(bf16[1,1,16000]{2,1,0:T(2,128)(2,1)S(1)} %reshape.582), channel_id=1, replica_groups=mesh['img'=4,'ch'=8] {'img','ch'}, dimensions={0}, use_global_device_ids=true | all-gather | bytes 1056000 | tf_op jit(solution)/shard_map/all_gather | solution.py:112
  127.2 7.2 %reduce.25 = bf16[32,16000]{1,0:T(8,128)(2,1)} reduce(bf16[32,1,16000]{2,1,0:T(2,128)(2,1)S(1)} %all-gather, bf16[]{:T(256)} %constant.355), dimensions={1}, to_apply=%all-gather.reduce_sub_computation | reduce | bytes 2048002 | tf_op jit(solution)/shard_map/all_gather | solution.py:112
  134.4 3.5 reshape.548
  154.7 2.4 reshape.541
  176.7 8.5 %reshape.546 = bf16[4608,512]{1,0:T(8,128)(2,1)} reshape(bf16[2359296]{0:T(1024)(128)(2,1)} %all-gather.3.cloned.1.call-done) | data formatting | bytes 9437184 | tf_op jit(solution)/shard_map/reshape | solution.py:114
  185.3 5.5 fusion.30
  190.8 36.2 %all-reduce.3 = (f32[]{:T(128)}, f32[512]{0:T(512)S(1)}, f32[512]{0:T(512)S(1)}) all-reduce(f32[]{:T(128)} %convert_reduce_fusion, f32[512]{0:T(512)S(1)} %get-tuple-element.136, f32[512]{0:T(512)S(1)} %get-tuple-element.135), channel_id=1, replica_groups=mesh['img'=4,'ch'=8] {'img','ch'}, use_global_device_ids=true, to_apply=%region_1.0 | all-reduce | flops 1025 | bytes 8200 | tf_op jit(solution)/shard_map/psum | solution.py:108
  234.6 42.0 %all-reduce.2 = (f32[]{:T(128)}, f32[512]{0:T(512)S(1)}, f32[512]{0:T(512)S(1)}) all-reduce(f32[]{:T(128)} %get-tuple-element.166, f32[512]{0:T(512)S(1)} %get-tuple-element.134, f32[512]{0:T(512)S(1)} %get-tuple-element.133), channel_id=1, replica_groups=mesh['img'=4,'ch'=8] {'img','ch'}, use_global_device_ids=true, to_apply=%region_15.16 | all-reduce | flops 1025 | bytes 8200 | tf_op jit(solution)/shard_map/psum | solution.py:173
  277.6 4.4 fusion.39
  282.0 3.0 fusion.34
  287.5 2.2 reshape.552
  289.7 2.2 reshape.555
  291.9 3.9 dynamic-slice_add_fusion
  295.8 5.4 scatter-add.31
  301.3 4.4 add_select_fusion
  305.7 5.4 scatter-add.34
  311.1 2.2 reshape.556
  315.5 2.3 slice_add_fusion.5
  317.8 4.1 scatter-add.35
  322.0 2.3 slice_add_fusion.4
  324.3 4.1 scatter-add.36
  330.6 2.2 reshape.559
  332.8 2.4 slice_add_fusion.3
  335.2 4.1 scatter-add.39
  339.3 2.3 slice_add_fusion.2
  341.6 4.1 scatter-add.40
  347.9 2.3 slice_add_fusion.1
  350.2 4.1 scatter-add.41
  356.5 2.4 slice_add_fusion
  359.0 4.3 scatter-add.44
  364.5 2.9 reshape.588
  367.5 4.7 all-to-all-start.1
  372.2 7.4 %convolution_bitcast_fusion = f32[576,4,8,128]{3,2,1,0:T(8,128)} fusion(bf16[392,4608]{1,0:T(8,128)(2,1)} %constant_dynamic-update-slice_fusion, bf16[392,512]{1,0:T(8,128)(2,1)S(1)} %copy-done.4), kind=kOutput, calls=%fused_computation.2 | convolution fusion | flops 1849688064 | bytes 13451264 | tf_op jit(solution)/shard_map/pk,pc->kc/dot_general | solution.py:71
  379.5 9.7 %copy.138 = f32[576,4,8,128]{3,1,2,0:T(4,128)} copy(f32[576,4,8,128]{3,2,1,0:T(8,128)} %convolution_bitcast_fusion) | data formatting | bytes 18874368
  389.2 3.2 reshape.589
  394.8 3.6 scatter_fusion
  399.8 3.2 copy.132
  406.8 8.9 %all-reduce.5 = (f32[64]{0:T(128)S(1)}, f32[64]{0:T(128)S(1)}) all-reduce(f32[64]{0:T(128)S(1)} %get-tuple-element.130, f32[64]{0:T(128)S(1)} %get-tuple-element.129), channel_id=1, replica_groups=mesh['img'=4,'ch'=8] {'img'}, use_global_device_ids=true, to_apply=%region_25.26 | all-reduce | flops 128 | bytes 1024 | tf_op jit(solution)/shard_map/psum | solution.py:205
  415.7 7.8 %fusion = bf16[2048,64]{0,1:T(8,128)(2,1)} fusion(bf16[3136,2048]{1,0:T(8,128)(2,1)} %reshape.534, f32[3136,64]{0,1:T(8,128)S(1)} %get-tuple-element.164, f32[64,3136]{1,0:T(8,128)S(1)} %get-tuple-element.201, f32[64]{0:T(128)S(1)} %get-tuple-element.147, f32[64]{0:T(128)S(1)} %broadcast_multiply_fusion.2, f32[64]{0:T(128)S(1)} %get-tuple-element.192, ...), kind=kOutput, calls=%fused_computation.4 | convolution fusion | flops 823820288 | bytes 14714112 | tf_op jit(solution)/shard_map/pk,pc->kc/dot_general | solution.py:71
  424.1 3.2 reshape.564
  431.6 35.7 %all-reduce.10.cloned.1.call-done = bf16[2048,64]{0,1:T(8,128)(2,1)} async-done(((bf16[2048,64]{0,1:T(8,128)(2,1)}), bf16[2048,64]{0,1:T(8,128)(2,1)}) %all-reduce.10.cloned.1.call-update) | async-done | bytes 262160 | tf_op jit(solution)/shard_map/psum | solution.py:221
  471.4 223.1 %all-reduce.12.cloned.1.call-done = (f32[2359296]{0:T(1024)}, f32[512000]{0:T(1024)}) async-done(((f32[2359296]{0:T(1024)}, f32[512000]{0:T(1024)}), (f32[2359296]{0:T(1024)}, f32[512000]{0:T(1024)})) %all-reduce.12.cloned.1.call-update) | async-done | bytes 11485200 | tf_op jit(solution)/shard_map/psum | solution.py:227
  (167 shorter events, 86.4 us)
Async XLA Ops:
  7.2 169.5 %all-gather.3.cloned.1.call-start = ((), (), s32[]{:S(2)}) async-start(), calls=%async_computation.2 | async-start | bytes 4866048 | tf_op jit(solution)/shard_map/all_gather | solution.py:111
  25.3 13.4 %copy-start = (s32[2048,64]{0,1:T(8,128)S(1)}, s32[2048,64]{0,1:T(8,128)}, u32[]{:S(2)}) copy-start(s32[2048,64]{0,1:T(8,128)} %param.48) | copy-start | bytes 1572868
  25.3 13.4 %copy-start.7 = (f32[2048,64]{0,1:T(8,128)S(1)}, f32[2048,64]{0,1:T(8,128)}, u32[]{:S(2)}) copy-start(f32[2048,64]{0,1:T(8,128)} %param.45) | copy-start | bytes 1572868
  38.7 17.5 %copy-start.21 = (f32[2,64]{1,0:T(2,128)S(1)}, f32[2,64]{1,0:T(2,128)}, u32[]{:S(2)}) copy-start(f32[2,64]{1,0:T(2,128)} %param.50) | copy-start | bytes 1540
  47.5 13.5 %copy-start.34 = (s32[1,64]{1,0:T(1,128)S(1)}, s32[1,64]{1,0:T(1,128)}, u32[]{:S(2)}) copy-start(s32[1,64]{1,0:T(1,128)} %param.44) | copy-start | bytes 772
  56.6 14.1 %copy-start.19 = (f32[16000]{0:T(1024)S(1)}, f32[16000]{0:T(1024)}, u32[]{:S(2)}) copy-start(f32[16000]{0:T(1024)} %param.61) | copy-start | bytes 192004
  61.0 73.3 %copy-start.26 = (s32[64]{0:T(128)}, s32[64]{0:T(128)S(1)}, u32[]{:S(2)}) copy-start(s32[64]{0:T(128)S(1)} %fusion.22) | copy-start | bytes 772
  63.1 77.3 %all-to-all-start = ((bf16[8,2,12544]{2,1,0:T(2,128)(2,1)}), bf16[8,2,12544]{2,1,0:T(2,128)(2,1)S(1)}, u32[]{:S(2)}, u32[]{:S(2)}) async-start(bf16[8,2,12544]{2,1,0:T(2,128)(2,1)} %reshape.586), calls=%async_computation | async-start | bytes 802816 | tf_op jit(solution)/shard_map/all_to_all | solution.py:133
  70.7 67.2 %copy-start.32 = (s32[8]{0:T(128)S(1)}, s32[8]{0:T(128)}, u32[]{:S(2)}) copy-start(s32[8]{0:T(128)} %param.43) | copy-start | bytes 100
  70.7 69.0 %copy-start.33 = (s32[4]{0:T(128)S(1)}, s32[4]{0:T(128)}, u32[]{:S(2)}) copy-start(s32[4]{0:T(128)} %constant.333.clone.1) | copy-start | bytes 52
  70.7 69.7 %copy-start.20 = (f32[2,512]{1,0:T(2,128)S(1)}, f32[2,512]{1,0:T(2,128)}, u32[]{:S(2)}) copy-start(f32[2,512]{1,0:T(2,128)} %param.58) | copy-start | bytes 12292
  153.2 8.0 %copy-start.10 = (bf16[8,7,7,512]{3,0,2,1:T(8,128)(2,1)S(1)}, bf16[8,7,7,512]{3,0,2,1:T(8,128)(2,1)}, u32[]{:S(2)}) copy-start(bf16[8,7,7,512]{3,0,2,1:T(8,128)(2,1)} %get-tuple-element.185) | copy-start | bytes 1204228
  154.7 7.5 %copy-start.9 = (bf16[8,7,7,512]{3,0,2,1:T(8,128)(2,1)S(1)}, bf16[8,7,7,512]{3,0,2,1:T(8,128)(2,1)}, u32[]{:S(2)}) copy-start(bf16[8,7,7,512]{3,0,2,1:T(8,128)(2,1)} %get-tuple-element.179) | copy-start | bytes 1204228
  161.3 11.1 %copy-start.11 = (bf16[392,512]{1,0:T(8,128)(2,1)S(1)}, bf16[392,512]{1,0:T(8,128)(2,1)}, u32[]{:S(2)}) copy-start(bf16[392,512]{1,0:T(8,128)(2,1)} %reshape.542) | copy-start | bytes 1204228
  162.4 12.7 %copy-start.12 = (bf16[392,512]{1,0:T(8,128)(2,1)S(1)}, bf16[392,512]{1,0:T(8,128)(2,1)}, u32[]{:S(2)}) copy-start(bf16[392,512]{1,0:T(8,128)(2,1)} %reshape.544) | copy-start | bytes 1204228
  163.3 12.6 %copy-start.13 = (bf16[392,512]{1,0:T(8,128)(2,1)S(1)}, bf16[392,512]{1,0:T(8,128)(2,1)}, u32[]{:S(2)}) copy-start(bf16[392,512]{1,0:T(8,128)(2,1)} %reshape.545) | copy-start | bytes 1204228
  190.8 41.2 %copy-start.24 = (s32[8]{0:T(128)S(1)}, s32[8]{0:T(128)}, u32[]{:S(2)}) copy-start(s32[8]{0:T(128)} %param.42) | copy-start | bytes 100
  233.5 1.1 copy-start.28
  276.8 0.8 copy-start.3
  363.4 8.8 %copy-start.4 = (bf16[392,512]{1,0:T(8,128)(2,1)S(1)}, bf16[392,512]{1,0:T(8,128)(2,1)}, u32[]{:S(2)}) copy-start(bf16[392,512]{1,0:T(8,128)(2,1)} %copy-done.3) | copy-start | bytes 1204228
  367.5 21.7 %all-to-all-start.1 = ((bf16[8,2,12544]{2,1,0:T(2,128)(2,1)}), bf16[8,2,12544]{2,1,0:T(2,128)(2,1)S(1)}, u32[]{:S(2)}, u32[]{:S(2)}) async-start(bf16[8,2,12544]{2,1,0:T(2,128)(2,1)} %reshape.588), calls=%async_computation.1 | async-start | bytes 802816 | tf_op jit(solution)/shard_map/all_to_all | solution.py:201
  372.2 95.1 %all-reduce.10.cloned.1.call-start = ((), (), s32[]{:S(2)}) async-start(), calls=%async_computation.3 | async-start | bytes 524288 | tf_op jit(solution)/shard_map/psum | solution.py:221
  389.2 5.6 copy-start.27
  415.7 7.9 %copy-start.25 = (s32[8]{0:T(128)S(1)}, s32[8]{0:T(128)}, u32[]{:S(2)}) copy-start(s32[8]{0:T(128)} %param.42) | copy-start | bytes 100
  415.7 7.9 %copy-start.29 = (f32[8]{0:T(128)S(1)}, f32[8]{0:T(128)}, u32[]{:S(2)}) copy-start(f32[8]{0:T(128)} %copy-done.28) | copy-start | bytes 100
  423.6 270.9 %all-reduce.12.cloned.1.call-start = ((), (), s32[]{:S(2)}) async-start(), calls=%async_computation.4 | async-start | bytes 22970368 | tf_op jit(solution)/shard_map/psum | solution.py:227
  427.4 1.0 copy-start.1
  427.4 1.2 copy-start.5
  427.4 2.2 copy-start.2
  427.4 2.2 copy-start.14
  427.4 3.0 copy-start.22
  427.4 3.0 copy-start.23
  427.4 3.6 copy-start.30
  427.4 3.6 copy-start.31
  427.5 39.8 %copy-start.8 = (f32[2048,64]{0,1:T(8,128)S(1)}, f32[2048,64]{0,1:T(8,128)}, u32[]{:S(2)}) copy-start(f32[2048,64]{0,1:T(8,128)} %param.45) | copy-start | bytes 1572868
  427.5 39.8 %copy-start.17 = (f32[2048,64]{0,1:T(8,128)S(1)}, f32[2048,64]{0,1:T(8,128)}, u32[]{:S(2)}) copy-start(f32[2048,64]{0,1:T(8,128)} %param.46) | copy-start | bytes 1572868
  428.6 265.9 %copy-start.16 = (f32[73728]{0:T(1024)S(1)}, f32[73728]{0:T(1024)}, u32[]{:S(2)}) copy-start(f32[73728]{0:T(1024)} %param.53) | copy-start | bytes 884740
  469.4 232.0 %copy-start.6 = (f32[2048,64]{0,1:T(8,128)}, f32[2048,64]{0,1:T(8,128)S(1)}, u32[]{:S(2)}) copy-start(f32[2048,64]{0,1:T(8,128)S(1)} %get-tuple-element.163) | copy-start | bytes 1572868
  696.4 5.0 copy-start.15
  699.9 1.5 copy-start.18
Sparse Core Ops, SparseCore 0:
  11.6 68.5 all-gather.2
  423.7 43.5 all-reduce.9
  474.8 219.6 all-reduce.11
where the time goes:
time: 720 us; the launch traced here: 708 us
  waiting for transfers between devices  259 us (36%)
  local copies, waits for them, and re-layouts  180 us (25%)
  blocking collectives  152 us (21%)
  other arithmetic  54.9 us (8%)
  matrix products  35.2 us (5%)
  between operations  14.8 us (2%)
  starting transfers between devices  12.3 us (2%)
    psum x1, waiting for transfers between devices, shards(): whole_two, whole_head = lax.psum((flat_two, flat_head), ('img', 'ch'))  223 us
    all_gather x1, blocking collectives, shards(): lax.all_gather(w_head.astype(jnp.bfloat16), ('img', 'ch'), axis=0, tiled=...  56.4 us
    unnamed x85, local copies, waits for them, and re-layouts  48.8 us
    psum x1, blocking collectives, shards(): lax.psum((jnp.sum(second_output_gradient, axis=0), jnp.sum(second_output_...  42 us
    scatter-add x9, local copies, waits for them, and re-layouts, shards(): d_pad.at[:, tap // 3:tap // 3 + SIDE, tap % 3:tap % 3 + SIDE, :].add(piece)  37.3 us
    psum x1, blocking collectives, shards(): total = lax.psum(local_total, ('img', 'ch'))  36.2 us
    psum x1, waiting for transfers between devices, shards(): lax.psum(contract_rows(rows, first_preact_gradient).astype(jnp.bfloat16),...  35.7 us
    another operation x11, local copies, waits for them, and re-layouts  18.7 us
  transfers between devices with their start and end apart: 5, of which 2 were waited for; matrix products, arithmetic and copies ran while one was open for 17% of the time, Pallas kernels for 0%

commit v1 on v0

--- a/solution.py
+++ b/solution.py
@@ -103,23 +103,25 @@
     width = second_norm_params.shape[1]
     classes = w_head.shape[0] * n_img * n_ch // width
     images = element_count * n_img * n_ch
-    weights = loss_wt.astype(jnp.float32)
-    local_total = jnp.sum(weights)
-    total = lax.psum(local_total, ("img", "ch"))
+    slot_info = jnp.stack([labels.astype(jnp.float32), loss_wt.astype(jnp.float32)])
+    slot_info = lax.all_gather(slot_info, "ch", axis=1, tiled=True)
+    own = lax.axis_index("ch") * element_count + jnp.arange(element_count, dtype=jnp.int32)
+    fills = placement[0][None, :] == own[:, None]
+    labels_f, weights = jnp.sum(jnp.where(fills[None], slot_info[:, None, :], 0.0), axis=2)
+    labels = labels_f.astype(jnp.int32)
     kernel_part = (w_two * mask_two.astype(jnp.float32)).astype(jnp.bfloat16)
-    kernel, head = (
-        lax.all_gather(kernel_part, ("img", "ch"), axis=0, tiled=True),
-        lax.all_gather(w_head.astype(jnp.bfloat16), ("img", "ch"), axis=0, tiled=True),
-    )
+    kernel = lax.all_gather(kernel_part, ("img", "ch"), axis=0, tiled=True)
+    head = lax.all_gather(w_head.astype(jnp.bfloat16), ("img", "ch"), axis=0, tiled=True)
     kernel = kernel.reshape(9 * width, width)
     head = head.reshape(width, classes)
-    rows = images_in.reshape(group * PIX, images_in.shape[2])
+    rows = images_in.transpose(1, 0, 2).reshape(PIX * group, images_in.shape[2])
     filt_one = (w_one * mask_one.astype(jnp.float32)).astype(jnp.bfloat16)
     first_conv_output = jnp.dot(rows, filt_one, preferred_element_type=jnp.float32)
-    first_feature_sum, first_squares_sum = lax.psum(
+    first_feature_sum, first_squares_sum, total = lax.psum(
         (
             jnp.sum(first_conv_output, axis=0),
             jnp.sum(first_conv_output * first_conv_output, axis=0),
+            jnp.sum(slot_info[1]),
         ),
         "img",
     )
@@ -128,31 +130,34 @@
         first_conv_output, first_feature_sum, first_squares_sum, first_element_count
     )
     first_norm_output = first_norm_params[0] * first_standardized_input + first_norm_params[1]
-    first_activation_map = jax.nn.silu(first_norm_output).astype(jnp.bfloat16)
-    ordered = first_activation_map.reshape(group, PIX, first_activation_map.shape[1])[placement[0]]
-    act_in = lax.all_to_all(ordered, "ch", split_axis=0, concat_axis=2, tiled=True)
+    act = jax.nn.silu(first_norm_output).astype(jnp.bfloat16).reshape(PIX, group, -1)
+    act_in = lax.all_to_all(act, "ch", split_axis=1, concat_axis=2, tiled=True)
     padded = jnp.pad(
-        act_in.reshape(element_count, SIDE, SIDE, width), ((0, 0), (1, 1), (1, 1), (0, 0))
+        act_in.reshape(SIDE, SIDE, element_count, width), ((1, 1), (1, 1), (0, 0), (0, 0))
     )
     patches = jnp.concatenate(
         [
-            padded[:, tap // 3 : tap // 3 + SIDE, tap % 3 : tap % 3 + SIDE, :].reshape(
-                element_count * PIX, width
+            padded[tap // 3 : tap // 3 + SIDE, tap % 3 : tap % 3 + SIDE].reshape(
+                PIX * element_count, width
             )
             for tap in range(9)
         ],
         axis=1,
     )
     second_conv_output = jnp.dot(patches, kernel, preferred_element_type=jnp.float32)
-    s_two = jnp.sum(second_conv_output, axis=0)
-    q_two = jnp.sum(second_conv_output * second_conv_output, axis=0)
-    second_feature_sum, second_squares_sum = lax.psum((s_two, q_two), ("img", "ch"))
+    second_feature_sum, second_squares_sum = lax.psum(
+        (
+            jnp.sum(second_conv_output, axis=0),
+            jnp.sum(second_conv_output * second_conv_output, axis=0),
+        ),
+        ("img", "ch"),
+    )
     second_element_count = images * PIX
     second_standardized_input, second_inverse_deviation = apply_batch_norm(
         second_conv_output, second_feature_sum, second_squares_sum, second_element_count
     )
     second_norm_output = second_norm_params[0] * second_standardized_input + second_norm_params[1]
-    pooled = jnp.mean(jax.nn.silu(second_norm_output).reshape(element_count, PIX, width), axis=1)
+    pooled = jnp.mean(jax.nn.silu(second_norm_output).reshape(PIX, element_count, width), axis=0)
     pooled_low = pooled.astype(jnp.bfloat16)
     logits = jnp.dot(pooled_low, head, preferred_element_type=jnp.float32)
     top = jnp.max(logits, axis=1, keepdims=True)
@@ -166,8 +171,8 @@
     d_logits = (share[:, None] * (expd / denom - onehot.astype(jnp.float32))).astype(jnp.bfloat16)
     g_head = contract_rows(pooled_low, d_logits)
     d_pooled = jnp.einsum("ic,kc->ik", d_logits, head, preferred_element_type=jnp.float32)
-    d_act = jnp.broadcast_to(d_pooled[:, None, :] / PIX, (element_count, PIX, width)).reshape(
-        element_count * PIX, width
+    d_act = jnp.broadcast_to(d_pooled[None] / PIX, (PIX, element_count, width)).reshape(
+        PIX * element_count, width
     )
     second_output_gradient = d_act * silu_slope(second_norm_output)
     second_shift_bias, second_norm_gain, loss = lax.psum(
@@ -187,20 +192,20 @@
         second_norm_gain,
         second_element_count,
     ).astype(jnp.bfloat16)
-    g_kernel = contract_rows(patches, second_preact_gradient)
     d_patches = jnp.einsum(
         "pc,kc->pk", second_preact_gradient, kernel, preferred_element_type=jnp.float32
     )
-    d_pad = jnp.zeros((element_count, SIDE + 2, SIDE + 2, width), jnp.float32)
+    d_pad = 0.0
     for tap in range(9):
         piece = d_patches[:, tap * width : (tap + 1) * width].reshape(
-            element_count, SIDE, SIDE, width
+            SIDE, SIDE, element_count, width
         )
-        d_pad = d_pad.at[:, tap // 3 : tap // 3 + SIDE, tap % 3 : tap % 3 + SIDE, :].add(piece)
-    d_act_in = d_pad[:, 1:-1, 1:-1, :].astype(jnp.bfloat16).reshape(element_count, PIX, width)
-    d_ordered = lax.all_to_all(d_act_in, "ch", split_axis=2, concat_axis=0, tiled=True)
-    d_act_one = jnp.zeros_like(d_ordered).at[placement[0]].set(d_ordered)
-    d_act_one = d_act_one.reshape(group * PIX, d_ordered.shape[2]).astype(jnp.float32)
+        up, left = tap // 3, tap % 3
+        d_pad = d_pad + jnp.pad(piece, ((up, 2 - up), (left, 2 - left), (0, 0), (0, 0)))
+    d_act_in = d_pad[1:-1, 1:-1].astype(jnp.bfloat16).reshape(PIX, element_count, width)
+    d_act_one = lax.all_to_all(d_act_in, "ch", split_axis=2, concat_axis=1, tiled=True)
+    g_kernel = contract_rows(patches, second_preact_gradient)
+    d_act_one = d_act_one.reshape(PIX * group, -1).astype(jnp.float32)
     first_output_gradient = d_act_one * silu_slope(first_norm_output)
     first_shift_bias, first_norm_gain = lax.psum(
         (
@@ -222,12 +227,12 @@
         contract_rows(rows, first_preact_gradient).astype(jnp.bfloat16), "img"
     ).astype(jnp.float32)
     g_one = g_filt * mask_one.astype(jnp.float32)
-    flat_two = g_kernel.reshape(-1)
-    flat_head = g_head.reshape(-1)
-    whole_two, whole_head = lax.psum((flat_two, flat_head), ("img", "ch"))
-    slot = lax.axis_index(("img", "ch"))
-    part_two = lax.dynamic_slice_in_dim(whole_two, slot * w_two.shape[0], w_two.shape[0])
-    part_head = lax.dynamic_slice_in_dim(whole_head, slot * w_head.shape[0], w_head.shape[0])
+    part_two = lax.psum_scatter(
+        g_kernel.reshape(-1), ("img", "ch"), tiled=True
+    )
+    part_head = lax.psum_scatter(
+        g_head.reshape(-1), ("img", "ch"), tiled=True
+    )
     g_two = part_two * mask_two.astype(jnp.float32)
     root = math.sqrt(images)
     one = sparse_update(w_one, g_one, mom_one, avg_one, mask_one, rank_one, 1.3 * root)

time: 720 us -> 582 us (0.81)
  local copies, waits for them, and re-layouts: 180 us -> 55.1 us
  other arithmetic: 54.9 us -> 29.1 us
  blocking collectives: 152 us -> 169 us
    unnamed x3 -> x4, waiting for transfers between devices: 0.05 us -> 223 us
    psum x1 -> x0, waiting for transfers between devices: 223 us -> none  [shards(): whole_two, whole_head = lax.psum((flat_two, flat_head), ('img', 'ch'))]
    scatter-add x9 -> x0, local copies, waits for them, and re-layouts: 37.3 us -> none  [shards(): d_pad.at[:, tap // 3:tap // 3 + SIDE, tap % 3:tap % 3 + SIDE, :].add(piece)]
    reshape x17 -> x6, local copies, waits for them, and re-layouts: 35.6 us -> 7.96 us  [the longest x1 3.22 us: shards(): part_head = lax.psum_scatter(g_head.reshape(-1), ('img', 'ch'), tiled=True)]
    unnamed x85 -> x101, local copies, waits for them, and re-layouts: 48.8 us -> 26.9 us
    another operation x11 -> x0, local copies, waits for them, and re-layouts: 18.7 us -> none
    add x7 -> x2, other arithmetic: 18 us -> 0.36 us  [the longest x1 0.35 us: shards(): d_pad + jnp.pad(piece, ((up, 2 - up), (left, 2 - left), (0, 0), (0, 0)))]
    all_gather x0 -> x1, blocking collectives: none -> 13.3 us  [shards(): slot_info = lax.all_gather(slot_info, 'ch', axis=1, tiled=True)]
  transfers between devices with their start and end apart: 5 -> 5, of which waited for: 2 -> 2; matrix products, arithmetic and copies ran while one was open for 17% -> 12% of each run, Pallas kernels for 0% -> 0%
where the time goes in v1:
time: 582 us; the launch traced here: 575 us
  waiting for transfers between devices  259 us (45%)
  blocking collectives  169 us (29%)
  local copies, waits for them, and re-layouts  55.1 us (9%)
  matrix products  37 us (6%)
  other arithmetic  29.1 us (5%)
  between operations  14.7 us (3%)
  starting transfers between devices  10.7 us (2%)
    unnamed x4, waiting for transfers between devices  223 us
    all_gather x1, blocking collectives, shards(): lax.all_gather(w_head.astype(jnp.bfloat16), ('img', 'ch'), axis=0, tiled=...  60.9 us
    psum x1, blocking collectives, shards(): lax.psum((jnp.sum(second_output_gradient, axis=0), jnp.sum(second_output_...  39.9 us
    psum x1, blocking collectives, shards(): lax.psum((jnp.sum(second_conv_output, axis=0), jnp.sum(second_conv_output...  38.2 us
    psum x1, waiting for transfers between devices, shards(): lax.psum(contract_rows(rows, first_preact_gradient).astype(jnp.bfloat16),...  35.6 us
    unnamed x101, local copies, waits for them, and re-layouts  26.9 us
    dot_general x3, matrix products, contract_rows(): jnp.einsum('pk,pc->kc', left, right, preferred_element_type=jnp.float32)  16.4 us
    all_gather x1, blocking collectives, shards(): slot_info = lax.all_gather(slot_info, 'ch', axis=1, tiled=True)  13.3 us
  transfers between devices with their start and end apart: 5, of which 2 were waited for; matrix products, arithmetic and copies ran while one was open for 12% of the time, Pallas kernels for 0%

profile of v1, /device:TPU:1, one launch (start us, length us, event | category | flops | bytes accessed | tf_op | source)
XLA Modules:
  0.0 574.7 jit_solution(3067732156576850317)
XLA Ops:
  7.2 1.7 multiply_convert_fusion.3
  9.7 13.3 %all-gather = f32[8,8,2]{1,2,0:T(2,128)S(1)} all-gather(f32[1,8,2]{1,2,0:T(2,128)S(1)} %maximum_bitcast_fusion), channel_id=1, replica_groups=mesh['img'=4,'ch'=8] {'ch'}, dimensions={0}, use_global_device_ids=true | all-gather | bytes 576 | tf_op jit(solution)/shard_map/all_gather | solution.py:107
  23.7 9.1 %fusion.29 = (f32[64]{0:T(128)S(1)}, f32[64]{0:T(128)S(1)}, f32[64,3136]{1,0:T(8,128)S(1)}) fusion(bf16[3136,2048]{1,0:T(8,128)(2,1)} %bitcast.114, f32[2048,64]{0,1:T(8,128)} %param.27, s32[2048,64]{0,1:T(8,128)} %param.30), kind=kOutput, calls=%fused_computation.118 | convolution fusion | flops 823078784 | bytes 14696960 | tf_op jit(solution)/shard_map/dot_general | solution.py:119
  32.8 8.5 %all-reduce.16 = (f32[]{:T(128)}, f32[64]{0:T(128)S(1)}, f32[64]{0:T(128)S(1)}) all-reduce(f32[]{:T(128)} %slice_reduce_fusion, f32[64]{0:T(128)S(1)} %get-tuple-element.26, f32[64]{0:T(128)S(1)} %get-tuple-element.25), channel_id=1, replica_groups=mesh['img'=4,'ch'=8] {'img'}, use_global_device_ids=true, to_apply=%region_2.3 | all-reduce | flops 129 | bytes 1032 | tf_op jit(solution)/shard_map/psum | solution.py:120
  42.9 2.4 copy.93
  45.3 1.3 reshape.231
  46.6 5.7 all-to-all-start
  52.3 60.9 %all-gather.1 = bf16[32,1,16000]{2,1,0:T(2,128)(2,1)S(1)} all-gather(bf16[1,1,16000]{2,1,0:T(2,128)(2,1)S(1)} %reshape.227), channel_id=1, replica_groups=mesh['img'=4,'ch'=8] {'img','ch'}, dimensions={0}, use_global_device_ids=true | all-gather | bytes 1056000 | tf_op jit(solution)/shard_map/all_gather | solution.py:114
  113.3 7.2 %reduce.3 = bf16[32,16000]{1,0:T(8,128)(2,1)} reduce(bf16[32,1,16000]{2,1,0:T(2,128)(2,1)S(1)} %all-gather.1, bf16[]{:T(256)} %constant.97), dimensions={1}, to_apply=%all-gather.1.reduce_sub_computation | reduce | bytes 2048002 | tf_op jit(solution)/shard_map/all_gather | solution.py:114
  120.5 3.3 reshape.209
  124.0 1.7 reshape.232
  125.7 1.7 copy.95
  129.4 0.8 constant_dynamic-update-slice_fusion.7
  130.2 0.8 constant_dynamic-update-slice_fusion.6
  132.7 0.8 constant_dynamic-update-slice_fusion.3
  134.3 0.8 constant_dynamic-update-slice_fusion.1
  135.1 0.8 constant_dynamic-update-slice_fusion
  135.9 8.5 %reshape.207 = bf16[4608,512]{1,0:T(8,128)(2,1)} reshape(bf16[2359296]{0:T(1024)(128)(2,1)} %all-gather.4.cloned.1.call-done) | data formatting | bytes 9437184 | tf_op jit(solution)/shard_map/reshape | solution.py:115
  144.4 5.5 fusion.30
  149.9 38.2 %all-reduce.13 = (f32[512]{0:T(512)S(1)}, f32[512]{0:T(512)S(1)}) all-reduce(f32[512]{0:T(512)S(1)} %get-tuple-element.28, f32[512]{0:T(512)S(1)} %get-tuple-element.27), channel_id=1, replica_groups=mesh['img'=4,'ch'=8] {'img','ch'}, use_global_device_ids=true, to_apply=%region_10.11 | all-reduce | flops 1024 | bytes 8192 | tf_op jit(solution)/shard_map/psum | solution.py:148
  189.1 1.3 multiply_reduce_fusion.3
  190.3 1.0 convolution_multiply_fusion
  191.8 39.9 %all-reduce.12 = (f32[]{:T(128)}, f32[512]{0:T(512)S(1)}, f32[512]{0:T(512)S(1)}) all-reduce(f32[]{:T(128)} %get-tuple-element.57, f32[512]{0:T(512)S(1)} %get-tuple-element.22, f32[512]{0:T(512)S(1)} %get-tuple-element.21), channel_id=1, replica_groups=mesh['img'=4,'ch'=8] {'img','ch'}, use_global_device_ids=true, to_apply=%region_16.17 | all-reduce | flops 1025 | bytes 8200 | tf_op jit(solution)/shard_map/psum | solution.py:178
  231.8 4.7 fusion.27
  236.5 0.9 fusion.34
  238.3 1.0 copy.97
  239.3 2.9 reshape.233
  242.2 4.7 all-to-all-start.1
  246.9 8.0 %convolution_bitcast_fusion = f32[576,4,8,128]{3,2,1,0:T(8,128)} fusion(bf16[392,4608]{1,0:T(8,128)(2,1)} %constant_dynamic-update-slice_fusion, f32[392,512]{1,0:T(8,128)S(1)} %get-tuple-element.89, f32[512]{0:T(512)S(1)} %get-tuple-element.32, f32[512]{0:T(512)S(1)} %broadcast_multiply_fusion, f32[512]{0:T(512)S(1)} %copy-done.39, ...), kind=kOutput, calls=%fused_computation | convolution fusion | flops 1853300736 | bytes 13883392 | tf_op jit(solution)/shard_map/pk,pc->kc/dot_general | solution.py:71
  254.9 9.8 %copy.105 = f32[576,4,8,128]{3,1,2,0:T(4,128)} copy(f32[576,4,8,128]{3,2,1,0:T(8,128)} %convolution_bitcast_fusion) | data formatting | bytes 18874368
  264.7 3.2 reshape.234
  267.9 1.1 copy.98
  269.4 1.5 copy.99
  270.9 1.9 copy.100
  273.4 8.5 %all-reduce.15 = (f32[64]{0:T(128)S(1)}, f32[64]{0:T(128)S(1)}) all-reduce(f32[64]{0:T(128)S(1)} %get-tuple-element.24, f32[64]{0:T(128)S(1)} %get-tuple-element.23), channel_id=1, replica_groups=mesh['img'=4,'ch'=8] {'img'}, use_global_device_ids=true, to_apply=%region_24.25 | all-reduce | flops 128 | bytes 1024 | tf_op jit(solution)/shard_map/psum | solution.py:210
  281.9 7.8 %fusion = bf16[2048,64]{0,1:T(8,128)(2,1)} fusion(bf16[3136,2048]{1,0:T(8,128)(2,1)} %bitcast.115, f32[3136,64]{0,1:T(8,128)S(1)} %get-tuple-element.56, f32[64,3136]{1,0:T(8,128)S(1)} %get-tuple-element.88, f32[64]{0:T(128)S(1)} %get-tuple-element.38, f32[64]{0:T(128)S(1)} %broadcast_multiply_fusion.2, f32[64]{0:T(128)S(1)} %copy-done.25, ...), kind=kOutput, calls=%fused_computation.2 | convolution fusion | flops 823820288 | bytes 14714112 | tf_op jit(solution)/shard_map/pk,pc->kc/dot_general | solution.py:71
  290.6 3.2 reshape.222
  294.0 0.9 copy-done
  295.1 1.0 or_select_fusion
  296.1 0.8 or_select_fusion.1
  298.1 35.6 %all-reduce.20.cloned.1.call-done = bf16[2048,64]{0,1:T(8,128)(2,1)} async-done(((bf16[2048,64]{0,1:T(8,128)(2,1)}), bf16[2048,64]{0,1:T(8,128)(2,1)}) %all-reduce.20.cloned.1.call-update) | async-done | bytes 262160 | tf_op jit(solution)/shard_map/psum | solution.py:226
  333.7 2.1 fusion.33
  335.8 2.1 add_multiply_fusion
  337.9 223.1 %all-reduce.22.cloned.1.call-done = (f32[2359296]{0:T(1024)}, f32[512000]{0:T(1024)}) async-done(((f32[2359296]{0:T(1024)}, f32[512000]{0:T(1024)}), (f32[2359296]{0:T(1024)}, f32[512000]{0:T(1024)})) %all-reduce.22.cloned.1.call-update) | async-done | bytes 11485200
  561.0 1.9 fusion.32
  562.9 1.8 add_multiply_fusion.1
  564.7 1.6 fusion.31
  566.4 1.5 add_multiply_fusion.2
  (131 shorter events, 13.1 us)
Async XLA Ops:
  7.2 128.7 %all-gather.4.cloned.1.call-start = ((), (), s32[]{:S(2)}) async-start(), calls=%async_computation.2 | async-start | bytes 4866048 | tf_op jit(solution)/shard_map/all_gather | solution.py:113
  23.7 17.6 %copy-start.21 = (f32[2,64]{1,0:T(2,128)S(1)}, f32[2,64]{1,0:T(2,128)}, u32[]{:S(2)}) copy-start(f32[2,64]{1,0:T(2,128)} %param.32) | copy-start | bytes 1540
  32.8 19.5 %copy-start.10 = (f32[16000]{0:T(1024)S(1)}, f32[16000]{0:T(1024)}, u32[]{:S(2)}) copy-start(f32[16000]{0:T(1024)} %param.43) | copy-start | bytes 192004
  41.3 0.9 copy-start.26
  41.3 0.9 copy-start.28
  41.9 0.5 copy-start.13
  41.9 0.6 copy-start.15
  46.6 77.4 %all-to-all-start = ((bf16[8,2,12544]{2,1,0:T(2,128)(2,1)}), bf16[8,2,12544]{2,1,0:T(2,128)(2,1)S(1)}, u32[]{:S(2)}, u32[]{:S(2)}) async-start(bf16[8,2,12544]{2,1,0:T(2,128)(2,1)} %reshape.231), calls=%async_computation | async-start | bytes 802816 | tf_op jit(solution)/shard_map/all_to_all | solution.py:134
  52.3 71.5 %copy-start.42 = (s32[1,64]{1,0:T(1,128)S(1)}, s32[1,64]{1,0:T(1,128)}, u32[]{:S(2)}) copy-start(s32[1,64]{1,0:T(1,128)} %param.26) | copy-start | bytes 772
  52.3 71.6 %copy-start.11 = (f32[2,512]{1,0:T(2,128)S(1)}, f32[2,512]{1,0:T(2,128)}, u32[]{:S(2)}) copy-start(f32[2,512]{1,0:T(2,128)} %param.40) | copy-start | bytes 12292
  124.0 64.9 %copy-start.32 = (s32[8]{0:T(128)}, s32[8]{0:T(128)S(1)}, u32[]{:S(2)}) copy-start(s32[8]{0:T(128)S(1)} %convert_bitcast_fusion) | copy-start | bytes 100
  188.2 48.3 %copy-start.38 = (f32[512]{0:T(512)}, f32[512]{0:T(512)S(1)}, u32[]{:S(2)}) copy-start(f32[512]{0:T(512)S(1)} %get-tuple-element.78) | copy-start | bytes 6148
  188.8 2.6 copy-start.17
  189.1 2.8 copy-start.23
  190.3 1.5 copy-start.34
  231.8 4.7 copy-start.19
  231.8 15.1 %copy-start.36 = (f32[512]{0:T(512)}, f32[512]{0:T(512)S(1)}, u32[]{:S(2)}) copy-start(f32[512]{0:T(512)S(1)} %get-tuple-element.32) | copy-start | bytes 6148
  237.8 9.1 %copy-start.39 = (f32[512]{0:T(512)S(1)}, f32[512]{0:T(512)}, u32[]{:S(2)}) copy-start(f32[512]{0:T(512)} %copy-done.38) | copy-start | bytes 6148
  242.2 22.5 %all-to-all-start.1 = ((bf16[8,2,12544]{2,1,0:T(2,128)(2,1)}), bf16[8,2,12544]{2,1,0:T(2,128)(2,1)S(1)}, u32[]{:S(2)}, u32[]{:S(2)}) async-start(bf16[8,2,12544]{2,1,0:T(2,128)(2,1)} %reshape.233), calls=%async_computation.1 | async-start | bytes 802816 | tf_op jit(solution)/shard_map/all_to_all | solution.py:206
  246.9 86.8 %all-reduce.20.cloned.1.call-start = ((), (), s32[]{:S(2)}) async-start(), calls=%async_computation.3 | async-start | bytes 524288 | tf_op jit(solution)/shard_map/psum | solution.py:226
  269.0 3.8 copy-start.14
  269.0 3.8 copy-start.16
  269.0 3.8 copy-start.27
  269.0 3.8 copy-start.29
  269.4 12.5 %copy-start.25 = (f32[64]{0:T(128)S(1)}, f32[64]{0:T(128)}, u32[]{:S(2)}) copy-start(f32[64]{0:T(128)} %get-tuple-element.83) | copy-start | bytes 772
  281.9 8.2 %copy-start.18 = (f32[8]{0:T(128)S(1)}, f32[8]{0:T(128)}, u32[]{:S(2)}) copy-start(f32[8]{0:T(128)} %copy-done.17) | copy-start | bytes 100
  281.9 8.3 %copy-start.24 = (f32[8]{0:T(128)S(1)}, f32[8]{0:T(128)}, u32[]{:S(2)}) copy-start(f32[8]{0:T(128)} %copy-done.23) | copy-start | bytes 100
  281.9 8.2 %copy-start.33 = (s32[8]{0:T(128)S(1)}, s32[8]{0:T(128)}, u32[]{:S(2)}) copy-start(s32[8]{0:T(128)} %copy-done.32) | copy-start | bytes 100
  281.9 8.2 %copy-start.35 = (f32[8]{0:T(128)S(1)}, f32[8]{0:T(128)}, u32[]{:S(2)}) copy-start(f32[8]{0:T(128)} %copy-done.34) | copy-start | bytes 100
  289.8 271.2 %all-reduce.22.cloned.1.call-start = ((), (), s32[]{:S(2)}) async-start(), calls=%async_computation.4 | async-start | bytes 22970368
  293.9 1.0 copy-start
  293.9 1.2 copy-start.2
  293.9 2.2 copy-start.1
  293.9 2.2 copy-start.5
  293.9 3.0 copy-start.12
  293.9 3.0 copy-start.20
  293.9 3.0 copy-start.30
  293.9 3.0 copy-start.31
  293.9 3.0 copy-start.37
  293.9 3.6 copy-start.22
  293.9 3.6 copy-start.40
  294.0 3.6 copy-start.41
  294.0 39.7 %copy-start.4 = (f32[2048,64]{0,1:T(8,128)S(1)}, f32[2048,64]{0,1:T(8,128)}, u32[]{:S(2)}) copy-start(f32[2048,64]{0,1:T(8,128)} %param.27) | copy-start | bytes 1572868
  294.0 39.7 %copy-start.8 = (f32[2048,64]{0,1:T(8,128)S(1)}, f32[2048,64]{0,1:T(8,128)}, u32[]{:S(2)}) copy-start(f32[2048,64]{0,1:T(8,128)} %param.28) | copy-start | bytes 1572868
  295.1 265.9 %copy-start.7 = (f32[73728]{0:T(1024)S(1)}, f32[73728]{0:T(1024)}, u32[]{:S(2)}) copy-start(f32[73728]{0:T(1024)} %param.35) | copy-start | bytes 884740
  335.8 232.1 %copy-start.3 = (f32[2048,64]{0,1:T(8,128)}, f32[2048,64]{0,1:T(8,128)S(1)}, u32[]{:S(2)}) copy-start(f32[2048,64]{0,1:T(8,128)S(1)} %get-tuple-element.55) | copy-start | bytes 1572868
  562.9 5.0 copy-start.6
  566.4 1.5 copy-start.9
Sparse Core Ops, SparseCore 0:
  11.6 73.3 all-gather.3
  289.9 43.7 all-reduce.19
  341.3 219.6 all-reduce.21

commit v2 on v1

--- a/solution.py
+++ b/solution.py
@@ -1,8 +1,12 @@
+import functools
+import itertools
 import math
 
 import jax
 import jax.numpy as jnp
 from jax import lax
+from jax.experimental import pallas as pl
+from jax.experimental.pallas import tpu as pltpu
 from jax.sharding import PartitionSpec as P
 
 SIDE = 7
@@ -277,6 +281,908 @@
     )
 
 
+F32, BF16 = jnp.float32, jnp.bfloat16
+MESH = pl.DeviceIdType.MESH
+TAPS = 9
+UPPER = (SIDE + 1) // 2
+PITCH = SIDE + 1
+FRONT = 2 * PITCH
+
+
+def silu_pair(value):
+    sigma = 1.0 / (1.0 + jnp.exp(-value))
+    return value * sigma, sigma * (1.0 + value * (1.0 - sigma))
+
+
+def matmul_nt(left, right):
+    return lax.dot_general(left, right, (((1,), (1,)), ((), ())), preferred_element_type=F32)
+
+
+def matmul_tn(left, right):
+    return lax.dot_general(left, right, (((0,), (0,)), ((), ())), preferred_element_type=F32)
+
+
+def rank_one(row, other):
+    first = other.astype(BF16)
+    rest = other - first.astype(F32)
+    second = rest.astype(BF16)
+    third = (rest - second.astype(F32)).astype(BF16)
+    place = lax.broadcasted_iota(jnp.int32, (16, other.shape[1]), 0)
+    parts = jnp.where(place == 0, first.astype(F32), 0.0)
+    parts = jnp.where(place == 1, second.astype(F32), parts)
+    parts = jnp.where(place == 2, third.astype(F32), parts)
+    rows = jnp.broadcast_to(row, (16, row.shape[1])).astype(BF16)
+    return matmul_tn(rows, parts.astype(BF16))
+
+
+def step_kernel(
+    sizes,
+    images,
+    place,
+    labels,
+    loss_wt,
+    w_one,
+    mask_one,
+    norm_one,
+    w_two,
+    mask_two,
+    head_part,
+    norm_two,
+    g_one,
+    g_two,
+    g_head,
+    g_bn_one,
+    g_bn_two,
+    loss,
+    feats,
+    filt,
+    kern,
+    head,
+    act_in,
+    act_out,
+    z_one,
+    z_two,
+    slope,
+    d_pad,
+    act_t,
+    d_act,
+    d_send,
+    d_recv,
+    d_one,
+    early,
+    info,
+    tile_sib,
+    tile_plane,
+    wide_plane,
+    wide_z,
+    wide_sib,
+    logit,
+    gh_half,
+    gk,
+    gh,
+    rk_one,
+    rh_one,
+    rk_two,
+    rh_two,
+    rk_z,
+    rh_z,
+    last_send,
+    last_recv,
+    edge_rows,
+    ranked,
+    grad_t,
+    g_acc,
+    go_send,
+    go_recv,
+    ga_send,
+    ga_recv,
+    image_sem,
+    local_sem,
+    send,
+    recv,
+):
+    group, per_chip, classes, images_in_all = sizes
+    width = norm_two.shape[1]
+    half = width // 2
+    own_ch = w_one.shape[0]
+    chip_ch = 2 * own_ch
+    block = w_two.shape[0] * 128 // width
+    chunk = 2 * block
+    rows_a = SIDE * group
+    rows_c = PITCH * per_chip
+    count_all = float(images_in_all * PIX)
+
+    i, c = lax.axis_index("img"), lax.axis_index("ch")
+    z, k = lax.div(c, 2), lax.rem(c, 2)
+    sib = c + 1 - 2 * k
+    xn, yn, dg = i + 1 - 2 * lax.rem(i, 2), lax.rem(i + 2, 4), 3 - i
+    lines = (xn, yn, dg)
+    h0 = (SIDE - UPPER) * k
+
+    def chip(dz):
+        return lax.rem(z + dz, 4)
+
+    def zdev(dz):
+        return 2 * chip(dz) + k
+
+    next_send, next_recv = itertools.count(), itertools.count()
+    sent = []
+
+    def new_recv(n=1):
+        first = next(next_recv)
+        for _ in range(n - 1):
+            next(next_recv)
+        return first
+
+    def push(src, dst, device, to):
+        copy = pltpu.make_async_remote_copy(
+            src_ref=src,
+            dst_ref=dst,
+            send_sem=send.at[next(next_send)],
+            recv_sem=recv.at[to],
+            device_id=device,
+            device_id_type=MESH,
+        )
+        copy.start()
+        sent.append(copy)
+        return copy
+
+    def arrived(dst, at):
+        pltpu.make_async_remote_copy(
+            src_ref=dst,
+            dst_ref=dst,
+            send_sem=send.at[0],
+            recv_sem=recv.at[at],
+            device_id=(i, sib),
+            device_id_type=MESH,
+        ).wait_recv()
+
+    def image_copy(r):
+        return pltpu.make_async_copy(
+            images.at[pl.ds(SIDE * (h0 + r), SIDE)], feats.at[pl.ds(SIDE * r, SIDE)], image_sem.at[r]
+        )
+
+    for r in range(UPPER):
+        image_copy(r).start()
+
+    act_in[0] = jnp.zeros(act_in.shape[1:], BF16)
+    for r in range(SIDE + 1, act_in.shape[0]):
+        act_in[r] = jnp.zeros(act_in.shape[1:], BF16)
+    for r in range(1, SIDE + 1):
+        act_in[r, 0] = jnp.zeros(act_in.shape[2:], BF16)
+    chunk_at = pl.multiple_of(chunk * (i * 4 + z), 32)
+    block_at = pl.multiple_of(chunk_at + block * k, 16)
+    parts = [
+        w_two[pl.ds(j, block, stride=4), :] * mask_two[pl.ds(j, block, stride=4), :].astype(F32)
+        for j in range(4)
+    ]
+    low = jnp.concatenate(parts[:2], axis=1).astype(BF16)
+    high = jnp.concatenate(parts[2:], axis=1).astype(BF16)
+    kern[pl.ds(block_at, block), :] = jnp.where(k == 0, low.astype(F32), high.astype(F32)).astype(BF16)
+    gk[pl.ds(0, block), :] = jnp.where(k == 0, high.astype(F32), low.astype(F32)).astype(BF16)
+    own_at = pl.multiple_of(own_ch * k, 16)
+    filt[pl.ds(own_at, own_ch), :] = (w_one[...] * mask_one[...].astype(F32)).astype(BF16)
+    head[i, z, k] = head_part[...]
+    lane = lax.broadcasted_iota(jnp.int32, (1, 128), 1)
+    norms = norm_one[...]
+    nothing = jnp.zeros_like(norms)
+    placed = jnp.where(
+        k == 0, jnp.concatenate([norms, nothing], axis=1), jnp.concatenate([nothing, norms], axis=1)
+    )
+    label_row, weight_row = jnp.zeros((1, 128), F32), jnp.zeros((1, 128), F32)
+    for j in range(labels.shape[0]):
+        here = lane == labels.shape[0] * c + j
+        label_row = jnp.where(here, labels[j].astype(F32), label_row)
+        weight_row = jnp.where(here, loss_wt[j].astype(F32), weight_row)
+    early[0] = jnp.concatenate(
+        [placed, label_row, weight_row, jnp.zeros((4, 128), F32)], axis=0
+    )
+
+    barrier = pltpu.get_barrier_semaphore()
+    others = [(i, sib)] + [(o, c) for o in lines] + [(i, zdev(dz)) for dz in (1, 2, 3)]
+    for device in others:
+        pl.semaphore_signal(barrier, inc=1, device_id=device, device_id_type=MESH)
+    pl.semaphore_wait(barrier, len(others))
+
+    k_sib, f_sib, e_sib = new_recv(), new_recv(), new_recv()
+    push(gk.at[pl.ds(0, block)], kern.at[pl.ds(block_at, block)], (i, sib), k_sib)
+    push(filt.at[pl.ds(own_at, own_ch)], filt.at[pl.ds(own_at, own_ch)], (i, sib), f_sib)
+    push(early.at[0], early.at[1], (i, sib), e_sib)
+
+    k_recv, h_recv = new_recv(16), new_recv(16)
+
+    def kern_at(line, dz):
+        return kern.at[pl.ds(pl.multiple_of(chunk * (line * 4 + chip(dz)), 32), chunk)]
+
+    def head_at(line, dz):
+        return head.at[line, chip(dz), k]
+
+    def number(line, dz):
+        return line * 4 + chip(dz)
+
+    def forward(line, dz, device):
+        push(kern_at(line, dz), kern_at(line, dz), device, k_recv + number(line, dz))
+        push(head_at(line, dz), head_at(line, dz), device, h_recv + number(line, dz))
+
+    def landed(line, dz):
+        arrived(kern_at(line, dz), k_recv + number(line, dz))
+        arrived(head_at(line, dz), h_recv + number(line, dz))
+
+    other_block_at = pl.multiple_of(chunk_at + block * (1 - k), 16)
+    arrived(kern.at[pl.ds(other_block_at, block)], k_sib)
+    for dz in (1, 2, 3):
+        forward(i, 0, (i, zdev(dz)))
+    forward(i, 0, (xn, c))
+    forward(i, 0, (yn, c))
+    arrived(early.at[1], e_sib)
+    both = early[0] + early[1]
+    info[z] = both
+    i_recv = new_recv(4)
+    for dz in (1, 2, 3):
+        push(info.at[z], info.at[z], (i, zdev(dz)), i_recv + z)
+    other_at = pl.multiple_of(own_ch * (1 - k), 16)
+    arrived(filt.at[pl.ds(other_at, own_ch)], f_sib)
+
+    def first_conv(r, carry):
+        sums, squares = carry
+        image_copy(r).wait()
+        rows = feats[pl.ds(SIDE * r, SIDE)].reshape(rows_a, feats.shape[2])
+        out = matmul_nt(rows, filt[...])
+        z_one[pl.ds(pl.multiple_of(rows_a * r, 64), rows_a), :] = out
+        counted = jnp.where((r == 0) & (k == 1), 0.0, 1.0)
+        return (
+            sums + counted * jnp.sum(out, axis=0, keepdims=True),
+            squares + counted * jnp.sum(out * out, axis=0, keepdims=True),
+        )
+
+    zero_row = jnp.zeros((1, chip_ch), F32)
+    sums, squares = lax.fori_loop(0, UPPER, first_conv, (zero_row, zero_row))
+
+    for dz in (1, 2, 3):
+        arrived(info.at[chip(dz)], i_recv + chip(dz))
+    slots = info[0] + info[1] + info[2] + info[3]
+    lane_in = lane < group
+    group_weight = jnp.sum(jnp.where(lane_in, slots[3:4], 0.0), axis=1, keepdims=True)
+
+    def small_sum(turn, rows):
+        tile_sib[turn, 0] = rows
+        at = new_recv()
+        push(tile_sib.at[turn, 0], tile_sib.at[turn, 1], (i, sib), at)
+        arrived(tile_sib.at[turn, 1], at)
+        tile_plane[turn, i] = tile_sib[turn, 0] + tile_sib[turn, 1]
+        at = new_recv(4)
+        for line in lines:
+            push(tile_plane.at[turn, i], tile_plane.at[turn, i], (line, c), at + i)
+
+        def finish():
+            for line in lines:
+                arrived(tile_plane.at[turn, line], at + line)
+            return (
+                tile_plane[turn, 0] + tile_plane[turn, 1] + tile_plane[turn, 2] + tile_plane[turn, 3]
+            )
+
+        return finish
+
+    half_weight = jnp.broadcast_to(0.5 * group_weight, (1, 128))
+    finish = small_sum(
+        0, jnp.concatenate([sums, squares, half_weight, jnp.zeros((5, 128), F32)], axis=0)
+    )
+    for dz in (1, 2, 3):
+        landed(i, dz)
+        forward(i, dz, (xn, c))
+        forward(i, dz, (yn, c))
+    totals = finish()
+    total = totals[2:3, 0:1]
+    mean_one = totals[0:1] / count_all
+    inv_one = lax.rsqrt(totals[1:2] / count_all - mean_one * mean_one + EPS)
+    gain_one, bias_one = both[0:1], both[1:2]
+
+    def first_act(r, carry):
+        at = pl.ds(pl.multiple_of(rows_a * r, 64), rows_a)
+        hat = (z_one[at, :] - mean_one) * inv_one
+        value, grade = silu_pair(gain_one * hat + bias_one)
+        act_out[r] = value.astype(BF16).reshape(SIDE, group, chip_ch)
+        return carry
+
+    lax.fori_loop(0, UPPER, first_act, 0)
+
+    a_recv = new_recv(4)
+    into = act_in.at[
+        pl.ds(1 + h0, UPPER), pl.ds(1, SIDE), :, pl.ds(pl.multiple_of(chip_ch * z, 128), chip_ch)
+    ]
+
+    def images_of(ref, dz):
+        return ref.at[:, :, pl.ds(pl.multiple_of(per_chip * chip(dz), 16), per_chip), :]
+
+    out_copies = [push(images_of(act_out, dz), into, (i, zdev(dz)), a_recv + z) for dz in (1, 2, 3)]
+    keep = pltpu.make_async_copy(images_of(act_out, 0), into, local_sem.at[0])
+    keep.start()
+
+    for dz in (0, 1):
+        landed(xn, dz)
+        forward(xn, dz, (yn, c))
+    for dz in (2, 3):
+        landed(yn, dz)
+        forward(yn, dz, (xn, c))
+
+    keep.wait()
+    for dz in (1, 2, 3):
+        arrived(
+            act_in.at[
+                pl.ds(1 + h0, UPPER),
+                pl.ds(1, SIDE),
+                :,
+                pl.ds(pl.multiple_of(chip_ch * chip(dz), 128), chip_ch),
+            ],
+            a_recv + chip(dz),
+        )
+    a_sib = new_recv()
+    mine = act_in.at[pl.ds(1 + UPPER * k, SIDE - UPPER), pl.ds(1, SIDE)]
+    push(mine, mine, (i, sib), a_sib)
+
+    for dz in (0, 1):
+        landed(yn, dz)
+    for dz in (2, 3):
+        landed(xn, dz)
+    for dz in (0, 1, 2, 3):
+        landed(dg, dz)
+    hd_sib = new_recv()
+    theirs = head.at[pl.ds(2 * (1 - k), 2), :, k]
+    push(theirs, theirs, (i, sib), hd_sib)
+    arrived(act_in.at[pl.ds(1 + UPPER * (1 - k), SIDE - UPPER), pl.ds(1, SIDE)], a_sib)
+
+    def tap_of(t):
+        return t // 3, t % 3
+
+    def second_conv(h, carry):
+        sums, squares = carry
+        out = jnp.zeros((rows_c, half), F32)
+        for t in range(TAPS):
+            up, left = tap_of(t)
+            wide = act_in[pl.ds(h + up, 2)].reshape(2 * PITCH, per_chip, width)
+            rows = wide[left : left + PITCH].reshape(rows_c, width)
+            out = out + jnp.dot(
+                rows, kern[pl.ds(width * t, width), :], preferred_element_type=F32
+            )
+        z_two[h] = out.reshape(PITCH, per_chip, half)
+        real = out[: SIDE * per_chip]
+        return (
+            sums + jnp.sum(real, axis=0, keepdims=True),
+            squares + jnp.sum(real * real, axis=0, keepdims=True),
+        )
+
+    zero_half = jnp.zeros((1, half), F32)
+    sums, squares = lax.fori_loop(0, SIDE, second_conv, (zero_half, zero_half))
+
+    def act_sum(h, carry):
+        rows = act_in[h + 1].reshape(rows_c, width).astype(F32)
+        return carry + jnp.sum(rows, axis=0, keepdims=True)
+
+    act_sums = lax.fori_loop(0, SIDE, act_sum, jnp.zeros((1, width), F32))
+
+    def wide_sum(turn, rows, between=None, size=8):
+        wide_plane[turn, i, pl.ds(0, size)] = rows
+        at = new_recv(4)
+        for line in lines:
+            push(
+                wide_plane.at[turn, i, pl.ds(0, size)],
+                wide_plane.at[turn, i, pl.ds(0, size)],
+                (line, c),
+                at + i,
+            )
+        if between is not None:
+            between()
+        for line in lines:
+            arrived(wide_plane.at[turn, line, pl.ds(0, size)], at + line)
+        wide_z[turn, z, pl.ds(0, size)] = (
+            wide_plane[turn, 0, pl.ds(0, size)]
+            + wide_plane[turn, 1, pl.ds(0, size)]
+            + wide_plane[turn, 2, pl.ds(0, size)]
+            + wide_plane[turn, 3, pl.ds(0, size)]
+        )
+        at_z = new_recv(4)
+        for dz in (1, 2, 3):
+            push(
+                wide_z.at[turn, z, pl.ds(0, size)],
+                wide_z.at[turn, z, pl.ds(0, size)],
+                (i, zdev(dz)),
+                at_z + z,
+            )
+
+        def finish():
+            for dz in (1, 2, 3):
+                arrived(wide_z.at[turn, chip(dz), pl.ds(0, size)], at_z + chip(dz))
+            return (
+                wide_z[turn, 0, pl.ds(0, size)]
+                + wide_z[turn, 1, pl.ds(0, size)]
+                + wide_z[turn, 2, pl.ds(0, size)]
+                + wide_z[turn, 3, pl.ds(0, size)]
+            )
+
+        return finish
+
+    finish = wide_sum(
+        0,
+        jnp.concatenate(
+            [sums, squares, act_sums[:, :half], act_sums[:, half:], jnp.zeros((4, half), F32)], axis=0
+        ),
+    )
+    inner = act_in[pl.ds(1, SIDE + 1)].reshape((SIDE + 1) * PITCH, per_chip, width)
+    inner = inner[1 : 1 + SIDE * PITCH].reshape(SIDE * rows_c, width)
+    act_t[pl.ds(0, width), :] = inner.T
+    column = lax.broadcasted_iota(jnp.int32, (16, SIDE * rows_c), 1)
+    is_real = lax.rem(lax.div(column, per_chip), PITCH) < SIDE
+    act_t[pl.ds(width, 16), :] = jnp.where(is_real, 1.0, 0.0).astype(BF16)
+    d_pad[pl.ds(0, FRONT)] = jnp.zeros((FRONT, per_chip, half), BF16)
+    d_pad[pl.ds(FRONT + SIDE * PITCH, FRONT)] = jnp.zeros((FRONT, per_chip, half), BF16)
+    totals_two = finish()
+    mean_two = totals_two[0:1] / count_all
+    inv_two = lax.rsqrt(totals_two[1:2] / count_all - mean_two * mean_two + EPS)
+    centre = jnp.concatenate([totals_two[2:3], totals_two[3:4]], axis=1) / count_all
+    centre = centre.astype(BF16).astype(F32)
+    norms_two = jnp.where(k == 0, norm_two[:, :half], norm_two[:, half:])
+    gain_two, bias_two = norms_two[0:1], norms_two[1:2]
+
+    def second_act(h, pooled):
+        hat = (z_two[h] - mean_two) * inv_two
+        z_two[h] = hat
+        value, grade = silu_pair(gain_two * hat + bias_two)
+        slope[h] = grade
+        return pooled + jnp.sum(value[:SIDE], axis=0)
+
+    pooled = lax.fori_loop(0, SIDE, second_act, jnp.zeros((per_chip, half), F32)) / PIX
+    pooled_low = pooled.astype(BF16)
+
+    arrived(head.at[pl.ds(2 * k, 2), :, 1 - k], hd_sib)
+    head_half = head[pl.ds(2 * k, 2)].reshape(half, head.shape[4])
+    logit[0] = jnp.dot(pooled_low, head_half, preferred_element_type=F32)
+    at = new_recv()
+    push(logit.at[0], logit.at[1], (i, sib), at)
+    image_id = per_chip * z + lax.broadcasted_iota(jnp.int32, (per_chip, group), 0)
+    fills = place[...] == image_id
+    label = jnp.sum(jnp.where(fills, slots[2:3, :group], 0.0), axis=1, keepdims=True).astype(jnp.int32)
+    weight = jnp.sum(jnp.where(fills, slots[3:4, :group], 0.0), axis=1, keepdims=True)
+    share = weight / total
+    arrived(logit.at[1], at)
+    logits = logit[0] + logit[1]
+    klass = lax.broadcasted_iota(jnp.int32, logits.shape, 1)
+    inside = klass < classes
+    top = jnp.max(jnp.where(inside, logits, -jnp.inf), axis=1, keepdims=True)
+    expd = jnp.where(inside, jnp.exp(jnp.where(inside, logits - top, 0.0)), 0.0)
+    denom = jnp.sum(expd, axis=1, keepdims=True)
+    onehot = klass == label
+    picked = jnp.sum(jnp.where(onehot, logits, 0.0), axis=1, keepdims=True)
+    partial = jnp.sum(share * (top + jnp.log(denom) - picked), axis=0, keepdims=True)
+    d_logits = (share * (expd / denom - jnp.where(onehot, 1.0, 0.0))).astype(BF16)
+    d_pooled = matmul_nt(d_logits, head_half) / PIX
+
+    def second_back(h, carry):
+        sums, products = carry
+        d_y = d_pooled[None] * slope[h]
+        slope[h] = d_y
+        d_y = d_y[:SIDE].reshape(SIDE * per_chip, half)
+        hat = z_two[h][:SIDE].reshape(SIDE * per_chip, half)
+        return (
+            sums + jnp.sum(d_y, axis=0, keepdims=True),
+            products + jnp.sum(d_y * hat, axis=0, keepdims=True),
+        )
+
+    d_bias, d_gain = lax.fori_loop(0, SIDE, second_back, (zero_half, zero_half))
+
+    gh_swap = new_recv()
+
+    def head_gradient():
+        gh_half[...] = matmul_tn(pooled_low, d_logits).astype(BF16).reshape(gh_half.shape)
+        push(gh_half.at[:, :, 1 - k], gh.at[pl.ds(2 * k, 2)], (i, sib), gh_swap)
+
+    finish = wide_sum(
+        1,
+        jnp.concatenate(
+            [d_gain, d_bias, jnp.broadcast_to(partial, (1, half)), jnp.zeros((5, half), F32)], axis=0
+        ),
+        head_gradient,
+    )
+    totals_back = finish()
+    loss[...] = totals_back[2:3, :128]
+    wide_sib[0] = totals_back
+    bn_at = new_recv()
+    push(wide_sib.at[0], wide_sib.at[1], (i, sib), bn_at)
+    scale = gain_two * inv_two
+    shift_two, lean_two = totals_back[1:2] / count_all, totals_back[0:1] / count_all
+
+    def second_grad(h, carry):
+        grad = scale * (slope[h] - shift_two - z_two[h] * lean_two)
+        pixel = lax.broadcasted_iota(jnp.int32, grad.shape, 0)
+        grad = jnp.where(pixel < SIDE, grad, 0.0)
+        d_pad[pl.ds(FRONT + PITCH * h, PITCH)] = grad.astype(BF16)
+        return carry
+
+    lax.fori_loop(0, SIDE, second_grad, 0)
+
+    def back_conv(h, carry):
+        out = jnp.zeros((rows_c, width), F32)
+        for t in range(TAPS):
+            up, left = tap_of(t)
+            rows = d_pad[pl.ds(PITCH * h + FRONT + PITCH + 1 - PITCH * up - left, PITCH)]
+            out = out + matmul_nt(rows.reshape(rows_c, half), kern[pl.ds(width * t, width), :])
+        d_act[h] = out.reshape(PITCH, per_chip, width)
+        return carry
+
+    lax.fori_loop(0, SIDE, back_conv, 0)
+    s0 = (SIDE - UPPER) * (1 - k)
+    for r in range(UPPER):
+        d_send[r] = d_act[s0 + r][:SIDE].astype(BF16)
+    d_at = new_recv()
+    push(d_send, d_recv, (i, sib), d_at)
+
+    def kernel_gradient(t, carry):
+        rows = d_pad[pl.ds(FRONT + PITCH + 1 - PITCH * lax.div(t, 3) - lax.rem(t, 3), SIDE * PITCH)]
+        out = jnp.dot(
+            act_t[...], rows.reshape(SIDE * rows_c, half), preferred_element_type=F32
+        )
+        edge = out[width : width + 1]
+        edge_rows[pl.ds(t, 1)] = edge
+        gk[pl.ds(pl.multiple_of(width * t, 32), width), :] = (
+            out[:width] - rank_one(centre, edge)
+        ).astype(BF16)
+        return carry
+
+    arrived(d_recv, d_at)
+    for r in range(UPPER):
+        d_send_r = d_act[h0 + r][:SIDE] + d_recv[r].astype(F32)
+        d_recv[r] = d_send_r.astype(BF16)
+    b_recv = new_recv(4)
+    back_into = images_of(d_one, 0)
+
+    def channels_of(dz):
+        return d_recv.at[:, :, :, pl.ds(pl.multiple_of(chip_ch * chip(dz), 128), chip_ch)]
+
+    for dz in (1, 2, 3):
+        push(channels_of(dz), back_into, (i, zdev(dz)), b_recv + z)
+    keep = pltpu.make_async_copy(channels_of(0), back_into, local_sem.at[1])
+    keep.start()
+
+    sent.pop(0).wait_send()
+    edge_rows[...] = jnp.zeros(edge_rows.shape, F32)
+    lax.fori_loop(0, TAPS, kernel_gradient, 0)
+    arrived(gh.at[pl.ds(2 * (1 - k), 2)], gh_swap)
+    gh[pl.ds(2 * k, 2)] = jnp.where(
+        k == 0, gh_half[:, :, 0].astype(F32), gh_half[:, :, 1].astype(F32)
+    ).astype(BF16)
+
+    def gk_at(line, dz):
+        return gk.at[pl.ds(pl.multiple_of(chunk * (line * 4 + chip(dz)), 32), chunk)]
+
+    def gh_at(line, dz):
+        return gh.at[line, chip(dz)]
+
+    order = (1, 2, 3, 0)
+    ways = {1: (xn, yn), 2: (yn, xn), 3: (xn, yn), 0: (yn, xn)}
+    one_at = {dz: new_recv(4) for dz in order}
+    two_at = {dz: new_recv(2) for dz in order}
+    z_at = new_recv(8)
+
+    def start_one(dz):
+        first, second = ways[dz]
+        push(gk_at(dg, dz), rk_one.at[dz, 1], (first, c), one_at[dz] + 1)
+        push(gh_at(dg, dz), rh_one.at[dz, 1], (first, c), one_at[dz] + 3)
+        push(gk_at(first, dz), rk_one.at[dz, 0], (first, c), one_at[dz])
+        push(gh_at(first, dz), rh_one.at[dz, 0], (first, c), one_at[dz] + 2)
+
+    def start_two(dz):
+        first, second = ways[dz]
+        arrived(rk_one.at[dz, 1], one_at[dz] + 1)
+        arrived(rh_one.at[dz, 1], one_at[dz] + 3)
+        into_k, into_h = gk_at(second, dz), gh_at(second, dz)
+        into_k[...] = (into_k[...].astype(F32) + rk_one[dz, 1].astype(F32)).astype(BF16)
+        into_h[...] = (into_h[...].astype(F32) + rh_one[dz, 1].astype(F32)).astype(BF16)
+        push(into_k, rk_two.at[dz], (second, c), two_at[dz])
+        push(into_h, rh_two.at[dz], (second, c), two_at[dz] + 1)
+
+    def plane_done(dz):
+        arrived(rk_one.at[dz, 0], one_at[dz])
+        arrived(rh_one.at[dz, 0], one_at[dz] + 2)
+        arrived(rk_two.at[dz], two_at[dz])
+        arrived(rh_two.at[dz], two_at[dz] + 1)
+        into_k, into_h = gk_at(i, dz), gh_at(i, dz)
+        sum_k = into_k[...].astype(F32) + rk_one[dz, 0].astype(F32) + rk_two[dz].astype(F32)
+        sum_h = into_h[...].astype(F32) + rh_one[dz, 0].astype(F32) + rh_two[dz].astype(F32)
+        if dz == 0:
+            return sum_k, sum_h
+        into_k[...] = sum_k.astype(BF16)
+        into_h[...] = sum_h.astype(BF16)
+        push(into_k, rk_z.at[z], (i, zdev(dz)), z_at + z)
+        push(into_h, rh_z.at[z], (i, zdev(dz)), z_at + 4 + z)
+        return None
+
+    for dz in order:
+        start_one(dz)
+    finish_edges = wide_sum(2, edge_rows[...], size=edge_rows.shape[0])
+
+    keep.wait()
+    for dz in (1, 2, 3):
+        arrived(images_of(d_one, dz), b_recv + chip(dz))
+
+    def first_back(r, carry):
+        sums, products = carry
+        at = pl.ds(pl.multiple_of(rows_a * r, 64), rows_a)
+        hat = (z_one[at, :] - mean_one) * inv_one
+        z_one[at, :] = hat
+        _, grade = silu_pair(gain_one * hat + bias_one)
+        d_y = d_one[r].reshape(rows_a, chip_ch).astype(F32) * grade
+        counted = jnp.where((r == 0) & (k == 1), 0.0, 1.0)
+        return (
+            sums + counted * jnp.sum(d_y, axis=0, keepdims=True),
+            products + counted * jnp.sum(d_y * hat, axis=0, keepdims=True),
+        )
+
+    d_bias, d_gain = lax.fori_loop(0, UPPER, first_back, (zero_row, zero_row))
+    finish = small_sum(
+        1, jnp.concatenate([d_gain, d_bias, jnp.zeros((6, 128), F32)], axis=0)
+    )
+    start_two(1)
+    start_two(2)
+    totals_one = finish()
+    g_bn_one[...] = jnp.where(k == 0, totals_one[0:2, :own_ch], totals_one[0:2, own_ch:])
+    scale_one = gain_one * inv_one
+    shift_one, lean_one = totals_one[1:2] / count_all, totals_one[0:1] / count_all
+
+    def first_grad(r, carry):
+        at = pl.ds(pl.multiple_of(rows_a * r, 64), rows_a)
+        hat = z_one[at, :]
+        _, grade = silu_pair(gain_one * hat + bias_one)
+        d_y = d_one[r].reshape(rows_a, chip_ch).astype(F32) * grade
+        counted = jnp.where((r == 0) & (k == 1), 0.0, 1.0)
+        grad = (counted * scale_one) * (d_y - shift_one - hat * lean_one)
+        act_out[r] = grad.astype(BF16).reshape(SIDE, group, chip_ch)
+        return carry
+
+    for copy in out_copies:
+        copy.wait_send()
+    sent[:] = [copy for copy in sent if all(copy is not done for done in out_copies)]
+    lax.fori_loop(0, UPPER, first_grad, 0)
+
+    grad_t[...] = act_out[...].reshape(UPPER * rows_a, chip_ch).T
+
+    def first_weights(n, carry):
+        at = pl.ds(pl.multiple_of(256 * n, 256), 256)
+        rows = feats[:, :, at].reshape(UPPER * rows_a, 256)
+        g_acc[:, at] = jnp.dot(grad_t[...], rows, preferred_element_type=F32)
+        return carry
+
+    lax.fori_loop(0, feats.shape[2] // 256, first_weights, 0)
+    low, high = g_acc[:own_ch], g_acc[own_ch:]
+    go_send[...] = jnp.where(k == 0, high, low).astype(BF16)
+    g_at = new_recv()
+    push(go_send, go_recv, (i, sib), g_at)
+    g_one[...] = jnp.where(k == 0, low, high)
+    plane_done(1)
+    plane_done(2)
+    start_two(3)
+    start_two(0)
+    arrived(go_recv, g_at)
+    part = own_ch // 2
+    ga_send[0] = (g_one[...] + go_recv[...].astype(F32)).astype(BF16)
+    first_at, second_at = new_recv(2), new_recv(2)
+    upper, lower = pl.ds(0, part), pl.ds(part, part)
+    push(ga_send.at[0, upper], ga_recv.at[0, upper], (xn, c), first_at)
+    push(ga_send.at[0, lower], ga_recv.at[0, lower], (yn, c), first_at + 1)
+    arrived(ga_recv.at[0, upper], first_at)
+    arrived(ga_recv.at[0, lower], first_at + 1)
+    ga_send[1] = (ga_send[0].astype(F32) + ga_recv[0].astype(F32)).astype(BF16)
+    push(ga_send.at[1, upper], ga_recv.at[1, upper], (yn, c), second_at)
+    push(ga_send.at[1, lower], ga_recv.at[1, lower], (xn, c), second_at + 1)
+
+    edges = finish_edges()
+    plane_done(3)
+    sum_k, sum_h = plane_done(0)
+
+    arrived(ga_recv.at[1, upper], second_at)
+    arrived(ga_recv.at[1, lower], second_at + 1)
+    g_one[...] = ga_send[1].astype(F32) + ga_recv[1].astype(F32)
+
+    row_at = chunk * (i * 4 + z)
+    tap = lax.div(row_at, width)
+    edge_rows[...] = edges
+    for step in range(2):
+        ranked[pl.ds(width * step, width), :] = rank_one(
+            centre, edge_rows[pl.ds(lax.rem(tap + step, TAPS), 1)]
+        )
+    offset = pl.multiple_of(row_at - width * tap, 32)
+    sum_k = sum_k + ranked[pl.ds(offset, chunk), :]
+    for dz in (1, 2, 3):
+        arrived(rk_z.at[chip(dz)], z_at + chip(dz))
+        arrived(rh_z.at[chip(dz)], z_at + 4 + chip(dz))
+        sum_k = sum_k + rk_z[chip(dz)].astype(F32)
+        sum_h = sum_h + rh_z[chip(dz)].astype(F32)
+    g_head[...] = sum_h
+    last_send[...] = sum_k
+    l_at = new_recv()
+    theirs = last_send.at[pl.ds(pl.multiple_of(block * (1 - k), 16), block)]
+    push(theirs, last_recv, (i, sib), l_at)
+    mine = last_send[pl.ds(pl.multiple_of(block * k, 16), block), :]
+    arrived(last_recv, l_at)
+    other = last_recv[...]
+    for j in range(4):
+        lanes = slice(128 * (j % 2), 128 * (j % 2) + 128)
+        g_two[pl.ds(j, block, stride=4), :] = jnp.where(
+            k == j // 2, mine[:, lanes], other[:, lanes]
+        )
+
+    arrived(wide_sib.at[1], bn_at)
+    own_bn, other_bn = wide_sib[0], wide_sib[1]
+    g_bn_two[...] = jnp.where(
+        k == 0,
+        jnp.concatenate([own_bn[0:2], other_bn[0:2]], axis=1),
+        jnp.concatenate([other_bn[0:2], own_bn[0:2]], axis=1),
+    )
+    for copy in sent:
+        copy.wait_send()
+
+
+def update_kernel(rates, *refs):
+    take, give = refs[:20], refs[20:]
+    rate_one, rate_bn_one, rate_two, rate_bn_two = rates
+    w, g, m, v, mask, rank = (r[...] for r in take[:6])
+    results = sparse_update(w, g * mask.astype(F32), m, v, mask, rank, rate_one)
+    for ref, value in zip(give[:5], results):
+        ref[...] = value
+    w, g, m, v, mask, rank = (r[...] for r in take[6:12])
+    results = sparse_update(w, g * mask.astype(F32), m, v, mask, rank, rate_two)
+    for ref, value in zip(give[5:10], results):
+        ref[...] = value
+    w, g, m, v = (r[...] for r in take[12:16])
+    for ref, value in zip(give[10:13], dense_update(w, g, m, v, rate_bn_one)):
+        ref[...] = value
+    w, g, m, v = (r[...] for r in take[16:20])
+    for ref, value in zip(give[13:16], dense_update(w, g, m, v, rate_bn_two)):
+        ref[...] = value
+
+
+def fast_shards(
+    images_in, labels, loss_wt, placement,
+    w_one, mom_one, avg_one, mask_one, rank_one_in, first_norm_params, mom_bn_one, avg_bn_one,
+    w_two, mom_two, avg_two, mask_two, rank_two, second_norm_params, mom_bn_two, avg_bn_two,
+    w_head, mom_head, avg_head,
+):
+    n_img, n_ch = lax.axis_size("img"), lax.axis_size("ch")
+    group, cin = images_in.shape[0], images_in.shape[2]
+    per_core = labels.shape[0]
+    per_chip = 2 * per_core
+    width = second_norm_params.shape[1]
+    half = width // 2
+    own_ch = w_one.shape[1]
+    chip_ch = 2 * own_ch
+    classes = w_head.shape[0] * n_img * n_ch // width
+    images = per_core * n_img * n_ch
+    head_rows = w_head.shape[0] // classes
+    lanes = -(-classes // 512) * 512
+    block = w_two.shape[0] // width
+    chunk = 2 * block
+    flat = (w_two.shape[0] // 128, 128)
+    headp = jnp.pad(
+        w_head.astype(BF16).reshape(head_rows, classes), ((0, 0), (0, lanes - classes))
+    )
+    one = [a.T for a in (w_one, mom_one, avg_one, mask_one, rank_one_in)]
+    two = [a.reshape(flat) for a in (w_two, mom_two, avg_two, mask_two, rank_two)]
+    vmem = pl.BlockSpec(memory_space=pltpu.VMEM)
+    smem = pl.BlockSpec(memory_space=pltpu.SMEM)
+    hbm = pl.BlockSpec(memory_space=pl.ANY)
+    v = pltpu.VMEM
+    shape = jax.ShapeDtypeStruct
+    g_one, g_two, g_head, g_bn_one, g_bn_two, loss = pl.pallas_call(
+        functools.partial(step_kernel, (group, per_chip, classes, images)),
+        out_shape=(
+            shape((own_ch, cin), F32),
+            shape(flat, F32),
+            shape((head_rows, lanes), F32),
+            shape((2, own_ch), F32),
+            shape((2, width), F32),
+            shape((1, 128), F32),
+        ),
+        in_specs=[hbm, vmem, smem, smem, vmem, vmem, vmem, vmem, vmem, vmem, vmem],
+        out_specs=[vmem] * 6,
+        scratch_shapes=[
+            v((UPPER * SIDE, group, cin), BF16),
+            v((chip_ch, cin), BF16),
+            v((TAPS * width, half), BF16),
+            v((4, 4, 2, head_rows, lanes), BF16),
+            v((SIDE + 3, PITCH, per_chip, width), BF16),
+            v((UPPER, SIDE, group, chip_ch), BF16),
+            v((UPPER * SIDE * group, chip_ch), F32),
+            v((SIDE, PITCH, per_chip, half), F32),
+            v((SIDE, PITCH, per_chip, half), F32),
+            v((2 * FRONT + SIDE * PITCH, per_chip, half), BF16),
+            v((width + 16, SIDE * PITCH * per_chip), BF16),
+            v((SIDE, PITCH, per_chip, width), F32),
+            v((UPPER, SIDE, per_chip, width), BF16),
+            v((UPPER, SIDE, per_chip, width), BF16),
+            v((UPPER, SIDE, group, chip_ch), BF16),
+            v((2, 8, 128), F32),
+            v((4, 8, 128), F32),
+            v((2, 2, 8, 128), F32),
+            v((2, 4, 8, 128), F32),
+            v((3, 4, 16, half), F32),
+            v((3, 4, 16, half), F32),
+            v((2, 8, half), F32),
+            v((2, per_chip, lanes), F32),
+            v((2, 4, 2, head_rows, lanes), BF16),
+            v((TAPS * width, half), BF16),
+            v((4, 4, head_rows, lanes), BF16),
+            v((4, 2, chunk, half), BF16),
+            v((4, 2, head_rows, lanes), BF16),
+            v((4, chunk, half), BF16),
+            v((4, head_rows, lanes), BF16),
+            v((4, chunk, half), BF16),
+            v((4, head_rows, lanes), BF16),
+            v((chunk, half), F32),
+            v((block, half), F32),
+            v((16, half), F32),
+            v((2 * width, half), F32),
+            v((chip_ch, UPPER * SIDE * group), BF16),
+            v((chip_ch, cin), F32),
+            v((own_ch, cin), BF16),
+            v((own_ch, cin), BF16),
+            v((2, own_ch, cin), BF16),
+            v((2, own_ch, cin), BF16),
+            pltpu.SemaphoreType.DMA((UPPER,)),
+            pltpu.SemaphoreType.DMA((2,)),
+            pltpu.SemaphoreType.DMA((150,)),
+            pltpu.SemaphoreType.DMA((150,)),
+        ],
+        compiler_params=pltpu.CompilerParams(
+            collective_id=0, has_side_effects=True, vmem_limit_bytes=56 << 20
+        ),
+        name="step",
+    )(
+        images_in.transpose(1, 0, 2),
+        placement,
+        labels,
+        loss_wt,
+        one[0],
+        one[3],
+        first_norm_params,
+        two[0],
+        two[3],
+        headp,
+        second_norm_params,
+    )
+    root = math.sqrt(images)
+    steps = 4
+    one_spec = pl.BlockSpec((own_ch // steps, cin), lambda n: (n, 0))
+    two_spec = pl.BlockSpec((flat[0] // steps, 128), lambda n: (n, 0))
+    bno_spec = pl.BlockSpec((2, own_ch), lambda n: (0, 0))
+    bnt_spec = pl.BlockSpec((2, width), lambda n: (0, 0))
+    f_one, f_two = shape(one[0].shape, F32), shape(flat, F32)
+    new = pl.pallas_call(
+        functools.partial(update_kernel, (1.3 * root, 8.0 * root, 0.25 * root, root)),
+        grid=(steps,),
+        in_specs=[one_spec] * 6 + [two_spec] * 6 + [bno_spec] * 4 + [bnt_spec] * 4,
+        out_specs=[one_spec] * 5 + [two_spec] * 5 + [bno_spec] * 3 + [bnt_spec] * 3,
+        out_shape=[f_one] * 3 + [shape(f_one.shape, jnp.int32), shape(f_one.shape, BF16)]
+        + [f_two] * 3 + [shape(flat, jnp.int32), shape(flat, BF16)]
+        + [shape((2, own_ch), F32)] * 3 + [shape((2, width), F32)] * 3,
+        compiler_params=pltpu.CompilerParams(vmem_limit_bytes=32 << 20),
+        name="update",
+    )(
+        one[0], g_one, one[1], one[2], one[3], one[4],
+        two[0], g_two, two[1], two[2], two[3], two[4],
+        first_norm_params, g_bn_one, mom_bn_one, avg_bn_one,
+        second_norm_params, g_bn_two, mom_bn_two, avg_bn_two,
+    )
+    g_head = g_head[:, :classes].reshape(-1)
+    top_head = dense_update(w_head, g_head, mom_head, avg_head, 40.0)
+    return (
+        loss[0, 0],
+        *(a.T for a in new[:5]),
+        *new[10:13],
+        *(a.reshape(-1) for a in new[5:10]),
+        *new[13:16],
+        *top_head,
+        top_head[0].astype(BF16),
+    )
+
+
 def solution(mesh):
     in_specs = (
         P("img", None, None),
@@ -326,4 +1232,5 @@
         P(("img", "ch")),
         P(("img", "ch")),
     )
-    return jax.shard_map(shards, mesh=mesh, in_specs=in_specs, out_specs=out_specs, check_vma=False)
+    fast = mesh.shape["img"] == 4 and mesh.shape["ch"] == 8
+    return jax.shard_map(fast_shards if fast else shards, mesh=mesh, in_specs=in_specs, out_specs=out_specs, check_vma=False)

time: 582 us -> 147 us (0.25); the launches traced: 575 us -> 146 us
  waiting for transfers between devices: 259 us -> 0 us
  blocking collectives: 169 us -> 0 us
  Pallas kernels: 0 us -> 132 us
  local copies, waits for them, and re-layouts: 55.1 us -> 7.3 us
  matrix products: 37 us -> 0 us
  other arithmetic: 29.1 us -> 4.63 us
  between operations: 14.7 us -> 2.69 us
  starting transfers between devices: 10.7 us -> 0 us
    unnamed x4 -> x0, waiting for transfers between devices: 223 us -> none
    pallas_call x0 -> x2, Pallas kernels: none -> 132 us  [the longest x1 129 us: fast_shards(): pl.pallas_call(functools.partial(step_kernel, (group, per_chip, classes,...]
    psum x4 -> x0, blocking collectives: 95.2 us -> none  [the longest x1 39.9 us: shards(): lax.psum((jnp.sum(second_output_gradient, axis=0), jnp.sum(second_output_...]
    all_gather x2 -> x0, blocking collectives: 74.3 us -> none  [the longest x1 60.9 us: shards(): lax.all_gather(w_head.astype(jnp.bfloat16), ('img', 'ch'), axis=0, tiled=...]
    dot_general x8 -> x0, matrix products: 37 us -> none  [the longest x3 16.4 us: contract_rows(): jnp.einsum('pk,pc->kc', left, right, preferred_element_type=jnp.float32)]
    psum x1 -> x0, waiting for transfers between devices: 35.6 us -> none  [shards(): lax.psum(contract_rows(rows, first_preact_gradient).astype(jnp.bfloat16),...]
    unnamed x101 -> x42, local copies, waits for them, and re-layouts: 26.9 us -> 3.43 us
    reshape x8 -> x2, local copies, waits for them, and re-layouts: 19.7 us -> 2.43 us  [the longest x1 1.49 us: fast_shards(): w_head.astype(BF16).reshape(head_rows, classes)]
  transfers between devices with their start and end apart: 5 -> 0, of which waited for: 2 -> 0; matrix products, arithmetic and copies ran while one was open for 12% -> 0% of each run, Pallas kernels for 0% -> 0%
where the time goes in v2:
time: 147 us; the launch traced here: 146 us
  Pallas kernels  132 us (90%)
  local copies, waits for them, and re-layouts  7.3 us (5%)
  other arithmetic  4.63 us (3%)
  between operations  2.69 us (2%)
    pallas_call x1, Pallas kernels, fast_shards(): pl.pallas_call(functools.partial(step_kernel, (group, per_chip, classes,...  129 us
    unnamed x42, local copies, waits for them, and re-layouts  3.43 us

profile of v2, /device:TPU:1, one launch (start us, length us, event | category | flops | bytes accessed | tf_op | source)
XLA Modules:
  0.0 146.2 jit_solution(789803465112121047)
XLA Ops:
  0.7 0.0 copy-start
  0.7 0.0 copy-start.1
  0.7 0.0 copy-start.2
  0.7 0.0 copy-start.3
  0.7 0.0 copy-start.16
  0.7 0.0 copy-start.12
  0.7 0.0 copy-start.4
  0.7 0.0 copy-start.5
  0.8 0.0 copy-start.6
  0.8 0.0 copy-start.8
  0.8 0.0 copy-start.17
  0.8 0.0 copy-start.18
  0.8 0.0 copy-start.13
  0.8 0.0 copy-start.14
  0.8 1.6 %convert_element_type.8 = bf16[16000]{0:T(1024)(128)(2,1)} convert(f32[16000]{0:T(1024)} %param.43) | non-fusion elementwise | flops 16000 | bytes 96000 | tf_op jit(solution)/shard_map/convert_element_type | solution.py:1064
  2.4 1.5 %reshape.80 = bf16[16,1000]{1,0:T(8,128)(2,1)} reshape(bf16[16000]{0:T(1024)(128)(2,1)} %convert_element_type.8) | data formatting | bytes 64000 | tf_op jit(solution)/shard_map/reshape | solution.py:1064
  3.9 0.0 copy-start.9
  3.9 0.0 copy-start.10
  3.9 1.4 pad.4.head_part
  5.4 129.2 %step.1 = (f32[64,2048]{1,0:T(8,128)}, f32[576,128]{1,0:T(8,128)}, f32[16,1024]{1,0:T(8,128)}, f32[2,64]{1,0:T(2,128)}, f32[2,512]{1,0:T(2,128)}, /*index=5*/f32[1,128]{1,0:T(1,128)}) custom-call(bf16[49,64,2048]{2,1,0:T(8,128)(2,1)} %bitcast.38, s32[1,64]{1,0:T(1,128)} %place.1, s32[8]{0:T(128)} %labels.1, s32[8]{0:T(128)} %loss_wt.1, f32[64,2048]{1,0:T(8,128)} %bitcast.24, ...), custom_call_target="tpu_custom_call" | custom-call | tf_op jit(solution)/shard_map/step/pallas_call | solution.py:1073
  134.5 0.0 copy-done
  134.5 0.0 copy-done.1
  134.5 0.0 copy-done.2
  134.6 0.0 copy-done.3
  134.6 0.0 copy-done.16
  134.6 0.0 copy-done.12
  134.6 0.0 copy-done.4
  134.6 0.0 copy-done.5
  134.6 0.0 copy-done.6
  134.6 0.0 copy-done.8
  134.6 0.0 copy-done.17
  134.6 0.0 copy-done.18
  134.6 0.0 copy-done.13
  134.7 0.0 copy-done.14
  134.7 0.0 copy-done.9
  134.7 0.0 copy-done.10
  134.7 0.0 copy-start.7
  134.7 1.0 copy-done.7
  135.7 0.0 copy-start.11
  135.7 1.0 copy-done.11
  136.7 0.0 copy-start.15
  136.7 0.7 copy-done.15
  137.4 0.7 copy-done.19
  138.0 2.4 %update.1 = (f32[64,2048]{1,0:T(8,128)}, f32[64,2048]{1,0:T(8,128)}, f32[64,2048]{1,0:T(8,128)}, s32[64,2048]{1,0:T(8,128)}, bf16[64,2048]{1,0:T(8,128)(2,1)}, /...) custom-call(f32[64,2048]{1,0:T(8,128)S(1)} %bitcast.25, ...), custom_call_target="tpu_custom_call" | custom-call | tf_op jit(solution)/shard_map/update/pallas_call | solution.py:1157
  140.5 0.9 reshape.89
  141.4 1.5 %fusion = (bf16[16000]{0:T(1024)(128)(2,1)}, f32[16000]{0:T(1024)S(1)}, f32[16000]{0:T(1024)}) fusion(f32[16000]{0:T(1024)} %param.43, f32[16000]{0:T(1024)S(1)} %reshape.89, f32[16000]{0:T(1024)} %param.44), kind=kLoop, calls=%fused_computation.3 | loop fusion | flops 112000 | bytes 352000 | tf_op jit(solution)/shard_map/convert_element_type | solution.py:1182
  142.9 1.5 %add_multiply_fusion = f32[16000]{0:T(1024)} fusion(f32[16000]{0:T(1024)} %param.45, f32[16000]{0:T(1024)S(1)} %get-tuple-element.106), kind=kLoop, calls=%fused_computation | loop fusion | flops 32000 | bytes 192000 | tf_op jit(solution)/shard_map/add | solution.py:29
  145.1 0.0 copy-done.20
  (2 shorter events, 0.0 us)
Async XLA Ops:
  0.7 133.9 %copy-start = (f32[2048,64]{0,1:T(8,128)S(1)}, f32[2048,64]{0,1:T(8,128)}, u32[]{:S(2)}) copy-start(f32[2048,64]{0,1:T(8,128)} %param.27) | copy-start | bytes 1572868
  0.7 133.9 %copy-start.1 = (s32[2048,64]{0,1:T(8,128)S(1)}, s32[2048,64]{0,1:T(8,128)}, u32[]{:S(2)}) copy-start(s32[2048,64]{0,1:T(8,128)} %param.30) | copy-start | bytes 1572868
  0.7 133.9 %copy-start.2 = (f32[73728]{0:T(1024)S(1)}, f32[73728]{0:T(1024)}, u32[]{:S(2)}) copy-start(f32[73728]{0:T(1024)} %param.35) | copy-start | bytes 884740
  0.7 133.9 %copy-start.3 = (s32[73728]{0:T(1024)S(1)}, s32[73728]{0:T(1024)}, u32[]{:S(2)}) copy-start(s32[73728]{0:T(1024)} %param.38) | copy-start | bytes 884740
  0.7 133.9 %copy-start.16 = (f32[2,64]{1,0:T(2,128)S(1)}, f32[2,64]{1,0:T(2,128)}, u32[]{:S(2)}) copy-start(f32[2,64]{1,0:T(2,128)} %refs_12_.1) | copy-start | bytes 1540
  0.7 133.9 %copy-start.12 = (f32[2,512]{1,0:T(2,128)S(1)}, f32[2,512]{1,0:T(2,128)}, u32[]{:S(2)}) copy-start(f32[2,512]{1,0:T(2,128)} %refs_16_.1) | copy-start | bytes 12292
  0.7 133.9 %copy-start.4 = (f32[2048,64]{0,1:T(8,128)S(1)}, f32[2048,64]{0,1:T(8,128)}, u32[]{:S(2)}) copy-start(f32[2048,64]{0,1:T(8,128)} %param.28) | copy-start | bytes 1572868
  0.7 133.9 %copy-start.5 = (f32[2048,64]{0,1:T(8,128)S(1)}, f32[2048,64]{0,1:T(8,128)}, u32[]{:S(2)}) copy-start(f32[2048,64]{0,1:T(8,128)} %param.29) | copy-start | bytes 1572868
  0.8 133.9 %copy-start.6 = (s32[2048,64]{0,1:T(8,128)S(1)}, s32[2048,64]{0,1:T(8,128)}, u32[]{:S(2)}) copy-start(s32[2048,64]{0,1:T(8,128)} %param.31) | copy-start | bytes 1572868
  0.8 133.9 %copy-start.8 = (f32[73728]{0:T(1024)S(1)}, f32[73728]{0:T(1024)}, u32[]{:S(2)}) copy-start(f32[73728]{0:T(1024)} %param.36) | copy-start | bytes 884740
  0.8 133.9 %copy-start.17 = (f32[2,64]{1,0:T(2,128)S(1)}, f32[2,64]{1,0:T(2,128)}, u32[]{:S(2)}) copy-start(f32[2,64]{1,0:T(2,128)} %refs_14_.1) | copy-start | bytes 1540
  0.8 133.9 %copy-start.18 = (f32[2,64]{1,0:T(2,128)S(1)}, f32[2,64]{1,0:T(2,128)}, u32[]{:S(2)}) copy-start(f32[2,64]{1,0:T(2,128)} %refs_15_.1) | copy-start | bytes 1540
  0.8 133.9 %copy-start.13 = (f32[2,512]{1,0:T(2,128)S(1)}, f32[2,512]{1,0:T(2,128)}, u32[]{:S(2)}) copy-start(f32[2,512]{1,0:T(2,128)} %refs_18_.1) | copy-start | bytes 12292
  0.8 133.9 %copy-start.14 = (f32[2,512]{1,0:T(2,128)S(1)}, f32[2,512]{1,0:T(2,128)}, u32[]{:S(2)}) copy-start(f32[2,512]{1,0:T(2,128)} %refs_19_.1) | copy-start | bytes 12292
  3.9 130.8 %copy-start.9 = (f32[73728]{0:T(1024)S(1)}, f32[73728]{0:T(1024)}, u32[]{:S(2)}) copy-start(f32[73728]{0:T(1024)} %param.37) | copy-start | bytes 884740
  3.9 130.8 %copy-start.10 = (s32[73728]{0:T(1024)S(1)}, s32[73728]{0:T(1024)}, u32[]{:S(2)}) copy-start(s32[73728]{0:T(1024)} %param.39) | copy-start | bytes 884740
  134.7 1.0 copy-start.7
  135.7 1.0 copy-start.11
  136.7 0.7 copy-start.15
  137.4 0.7 copy-start.19
  142.9 2.1 %copy-start.20 = (f32[16000]{0:T(1024)}, f32[16000]{0:T(1024)S(1)}, u32[]{:S(2)}) copy-start(f32[16000]{0:T(1024)S(1)} %get-tuple-element.106) | copy-start | bytes 192004

commit v3 on v2

--- a/solution.py
+++ b/solution.py
@@ -287,6 +287,7 @@
 UPPER = (SIDE + 1) // 2
 PITCH = SIDE + 1
 FRONT = 2 * PITCH
+SEMS = 240
 
 
 def silu_pair(value):
@@ -326,7 +327,7 @@
     norm_one,
     w_two,
     mask_two,
-    head_part,
+    w_head,
     norm_two,
     g_one,
     g_two,
@@ -351,10 +352,8 @@
     d_one,
     early,
     info,
-    tile_sib,
-    tile_plane,
-    wide_plane,
-    wide_z,
+    tiles,
+    wide,
     wide_sib,
     logit,
     gh_half,
@@ -366,6 +365,8 @@
     rh_two,
     rk_z,
     rh_z,
+    h_sum,
+    head_flat,
     last_send,
     last_recv,
     edge_rows,
@@ -388,6 +389,7 @@
     chip_ch = 2 * own_ch
     block = w_two.shape[0] * 128 // width
     chunk = 2 * block
+    head_rows = head.shape[3]
     rows_a = SIDE * group
     rows_c = PITCH * per_chip
     count_all = float(images_in_all * PIX)
@@ -397,10 +399,11 @@
     sib = c + 1 - 2 * k
     xn, yn, dg = i + 1 - 2 * lax.rem(i, 2), lax.rem(i + 2, 4), 3 - i
     lines = (xn, yn, dg)
+    near = (z, z + 1 - 2 * lax.rem(z, 2), 2 - lax.div(z, 2), 3 - 3 * lax.div(z, 2))
     h0 = (SIDE - UPPER) * k
 
     def chip(dz):
-        return lax.rem(z + dz, 4)
+        return near[dz]
 
     def zdev(dz):
         return 2 * chip(dz) + k
@@ -462,8 +465,20 @@
     gk[pl.ds(0, block), :] = jnp.where(k == 0, high.astype(F32), low.astype(F32)).astype(BF16)
     own_at = pl.multiple_of(own_ch * k, 16)
     filt[pl.ds(own_at, own_ch), :] = (w_one[...] * mask_one[...].astype(F32)).astype(BF16)
-    head[i, z, k] = head_part[...]
     lane = lax.broadcasted_iota(jnp.int32, (1, 128), 1)
+    for r in range(head_rows):
+        first, shift = divmod(classes * r, 128)
+        taken = -(-(shift + classes) // 128)
+        rows = w_head[first : first + taken, :]
+        if taken < 9:
+            rows = jnp.concatenate([rows, jnp.zeros((9 - taken, 128), F32)], axis=0)
+        if shift:
+            rows = pltpu.roll(rows, 128 - shift, 1)
+            rows = jnp.where(lane < 128 - shift, rows[:8], rows[1:9])
+        for j in range(8):
+            head_flat[r : r + 1, 128 * j : 128 * j + 128] = rows[j : j + 1]
+    head_lane = lax.broadcasted_iota(jnp.int32, (head_rows, 1024), 1)
+    head[i, z, k] = jnp.where(head_lane < classes, head_flat[...], 0.0).astype(BF16)
     norms = norm_one[...]
     nothing = jnp.zeros_like(norms)
     placed = jnp.where(
@@ -479,7 +494,9 @@
     )
 
     barrier = pltpu.get_barrier_semaphore()
-    others = [(i, sib)] + [(o, c) for o in lines] + [(i, zdev(dz)) for dz in (1, 2, 3)]
+    same_core = [(o, zdev(dz)) for o in (i, *lines) for dz in (0, 1, 2, 3)][1:]
+    plane = [(i, sib)] + [(o, d) for o in lines for d in (c, sib)]
+    others = same_core + [plane[0]] + [p for p in plane[1:] if p[1] is sib]
     for device in others:
         pl.semaphore_signal(barrier, inc=1, device_id=device, device_id_type=MESH)
     pl.semaphore_wait(barrier, len(others))
@@ -502,18 +519,22 @@
 
     def forward(line, dz, device):
         push(kern_at(line, dz), kern_at(line, dz), device, k_recv + number(line, dz))
-        push(head_at(line, dz), head_at(line, dz), device, h_recv + number(line, dz))
 
     def landed(line, dz):
         arrived(kern_at(line, dz), k_recv + number(line, dz))
+
+    def head_forward(line, dz, device):
+        push(head_at(line, dz), head_at(line, dz), device, h_recv + number(line, dz))
+
+    def head_landed(line, dz):
         arrived(head_at(line, dz), h_recv + number(line, dz))
 
     other_block_at = pl.multiple_of(chunk_at + block * (1 - k), 16)
     arrived(kern.at[pl.ds(other_block_at, block)], k_sib)
+    forward(i, 0, (xn, c))
+    forward(i, 0, (yn, c))
     for dz in (1, 2, 3):
         forward(i, 0, (i, zdev(dz)))
-    forward(i, 0, (xn, c))
-    forward(i, 0, (yn, c))
     arrived(early.at[1], e_sib)
     both = early[0] + early[1]
     info[z] = both
@@ -538,97 +559,93 @@
     zero_row = jnp.zeros((1, chip_ch), F32)
     sums, squares = lax.fori_loop(0, UPPER, first_conv, (zero_row, zero_row))
 
-    for dz in (1, 2, 3):
-        arrived(info.at[chip(dz)], i_recv + chip(dz))
-    slots = info[0] + info[1] + info[2] + info[3]
-    lane_in = lane < group
-    group_weight = jnp.sum(jnp.where(lane_in, slots[3:4], 0.0), axis=1, keepdims=True)
-
     def small_sum(turn, rows):
-        tile_sib[turn, 0] = rows
-        at = new_recv()
-        push(tile_sib.at[turn, 0], tile_sib.at[turn, 1], (i, sib), at)
-        arrived(tile_sib.at[turn, 1], at)
-        tile_plane[turn, i] = tile_sib[turn, 0] + tile_sib[turn, 1]
-        at = new_recv(4)
-        for line in lines:
-            push(tile_plane.at[turn, i], tile_plane.at[turn, i], (line, c), at + i)
+        own = 2 * i + k
+        tiles[turn, own] = rows
+        at = new_recv(8)
+        for device in plane:
+            push(tiles.at[turn, own], tiles.at[turn, own], device, at + own)
 
         def finish():
-            for line in lines:
-                arrived(tile_plane.at[turn, line], at + line)
-            return (
-                tile_plane[turn, 0] + tile_plane[turn, 1] + tile_plane[turn, 2] + tile_plane[turn, 3]
-            )
+            for line in (i, *lines):
+                arrived(tiles.at[turn, 2 * line + 1 - k], at + 2 * line + 1 - k)
+                if line is not i:
+                    arrived(tiles.at[turn, 2 * line + k], at + 2 * line + k)
+            result = tiles[turn, 0]
+            for n in range(1, 8):
+                result = result + tiles[turn, n]
+            return result
 
         return finish
 
-    half_weight = jnp.broadcast_to(0.5 * group_weight, (1, 128))
-    finish = small_sum(
-        0, jnp.concatenate([sums, squares, half_weight, jnp.zeros((5, 128), F32)], axis=0)
-    )
-    for dz in (1, 2, 3):
-        landed(i, dz)
-        forward(i, dz, (xn, c))
-        forward(i, dz, (yn, c))
+    finish = small_sum(0, jnp.concatenate([sums, squares, jnp.zeros((6, 128), F32)], axis=0))
+    landed(i, 1)
+    forward(i, 1, (xn, c))
+    forward(i, 1, (yn, c))
+    landed(xn, 0)
+    forward(xn, 0, (yn, c))
     totals = finish()
-    total = totals[2:3, 0:1]
     mean_one = totals[0:1] / count_all
     inv_one = lax.rsqrt(totals[1:2] / count_all - mean_one * mean_one + EPS)
     gain_one, bias_one = both[0:1], both[1:2]
 
-    def first_act(r, carry):
-        at = pl.ds(pl.multiple_of(rows_a * r, 64), rows_a)
+    def first_act(r):
+        at = slice(rows_a * r, rows_a * r + rows_a)
         hat = (z_one[at, :] - mean_one) * inv_one
         value, grade = silu_pair(gain_one * hat + bias_one)
         act_out[r] = value.astype(BF16).reshape(SIDE, group, chip_ch)
-        return carry
-
-    lax.fori_loop(0, UPPER, first_act, 0)
-
-    a_recv = new_recv(4)
-    into = act_in.at[
-        pl.ds(1 + h0, UPPER), pl.ds(1, SIDE), :, pl.ds(pl.multiple_of(chip_ch * z, 128), chip_ch)
-    ]
+
+    a_recv = new_recv(4 * UPPER)
+
+    def into(r, chip_id):
+        return act_in.at[
+            1 + h0 + r, pl.ds(1, SIDE), :, pl.ds(pl.multiple_of(chip_ch * chip_id, 128), chip_ch)
+        ]
 
     def images_of(ref, dz):
         return ref.at[:, :, pl.ds(pl.multiple_of(per_chip * chip(dz), 16), per_chip), :]
 
-    out_copies = [push(images_of(act_out, dz), into, (i, zdev(dz)), a_recv + z) for dz in (1, 2, 3)]
-    keep = pltpu.make_async_copy(images_of(act_out, 0), into, local_sem.at[0])
-    keep.start()
-
-    for dz in (0, 1):
-        landed(xn, dz)
-        forward(xn, dz, (yn, c))
-    for dz in (2, 3):
-        landed(yn, dz)
-        forward(yn, dz, (xn, c))
-
-    keep.wait()
+    def images_in_row(ref, r, dz):
+        return ref.at[r, :, pl.ds(pl.multiple_of(per_chip * chip(dz), 16), per_chip), :]
+
+    out_copies, kept = [], []
+    for r in range(UPPER):
+        first_act(r)
+        for dz in (3, 2, 1):
+            out_copies.append(
+                push(images_in_row(act_out, r, dz), into(r, z), (i, zdev(dz)), a_recv + 4 * r + z)
+            )
+        kept.append(
+            pltpu.make_async_copy(images_in_row(act_out, r, 0), into(r, z), local_sem.at[r])
+        )
+        kept[-1].start()
+    landed(i, 2)
+    forward(i, 2, (xn, c))
+    forward(i, 2, (yn, c))
+    landed(xn, 1)
+    forward(xn, 1, (yn, c))
+    landed(i, 3)
+    forward(i, 3, (xn, c))
+    forward(i, 3, (yn, c))
+    landed(yn, 2)
+    forward(yn, 2, (xn, c))
+    landed(yn, 3)
+    forward(yn, 3, (xn, c))
+    head_forward(i, 0, (xn, c))
+    head_forward(i, 0, (yn, c))
     for dz in (1, 2, 3):
-        arrived(
-            act_in.at[
-                pl.ds(1 + h0, UPPER),
-                pl.ds(1, SIDE),
-                :,
-                pl.ds(pl.multiple_of(chip_ch * chip(dz), 128), chip_ch),
-            ],
-            a_recv + chip(dz),
-        )
+        head_forward(i, 0, (i, zdev(dz)))
+
+    for copy in kept:
+        copy.wait()
+    for r in range(UPPER):
+        for dz in (1, 2, 3):
+            arrived(into(r, chip(dz)), a_recv + 4 * r + chip(dz))
     a_sib = new_recv()
     mine = act_in.at[pl.ds(1 + UPPER * k, SIDE - UPPER), pl.ds(1, SIDE)]
     push(mine, mine, (i, sib), a_sib)
-
-    for dz in (0, 1):
-        landed(yn, dz)
-    for dz in (2, 3):
-        landed(xn, dz)
-    for dz in (0, 1, 2, 3):
-        landed(dg, dz)
-    hd_sib = new_recv()
-    theirs = head.at[pl.ds(2 * (1 - k), 2), :, k]
-    push(theirs, theirs, (i, sib), hd_sib)
+    for line, dz in ((yn, 0), (yn, 1), (xn, 2), (xn, 3), (dg, 0), (dg, 1), (dg, 2), (dg, 3)):
+        landed(line, dz)
     arrived(act_in.at[pl.ds(1 + UPPER * (1 - k), SIDE - UPPER), pl.ds(1, SIDE)], a_sib)
 
     def tap_of(t):
@@ -660,53 +677,48 @@
 
     act_sums = lax.fori_loop(0, SIDE, act_sum, jnp.zeros((1, width), F32))
 
-    def wide_sum(turn, rows, between=None, size=8):
-        wide_plane[turn, i, pl.ds(0, size)] = rows
-        at = new_recv(4)
-        for line in lines:
-            push(
-                wide_plane.at[turn, i, pl.ds(0, size)],
-                wide_plane.at[turn, i, pl.ds(0, size)],
-                (line, c),
-                at + i,
-            )
-        if between is not None:
-            between()
-        for line in lines:
-            arrived(wide_plane.at[turn, line, pl.ds(0, size)], at + line)
-        wide_z[turn, z, pl.ds(0, size)] = (
-            wide_plane[turn, 0, pl.ds(0, size)]
-            + wide_plane[turn, 1, pl.ds(0, size)]
-            + wide_plane[turn, 2, pl.ds(0, size)]
-            + wide_plane[turn, 3, pl.ds(0, size)]
-        )
-        at_z = new_recv(4)
-        for dz in (1, 2, 3):
-            push(
-                wide_z.at[turn, z, pl.ds(0, size)],
-                wide_z.at[turn, z, pl.ds(0, size)],
-                (i, zdev(dz)),
-                at_z + z,
-            )
+    def wide_sum(turn, rows):
+        own, size = 4 * i + z, rows.shape[0]
+        wide[turn, own, pl.ds(0, size)] = rows
+        at = new_recv(16)
+
+        def tile(number):
+            return wide.at[turn, number, pl.ds(0, size)]
+
+        for device in same_core[::-1]:
+            push(tile(own), tile(own), device, at + own)
 
         def finish():
-            for dz in (1, 2, 3):
-                arrived(wide_z.at[turn, chip(dz), pl.ds(0, size)], at_z + chip(dz))
-            return (
-                wide_z[turn, 0, pl.ds(0, size)]
-                + wide_z[turn, 1, pl.ds(0, size)]
-                + wide_z[turn, 2, pl.ds(0, size)]
-                + wide_z[turn, 3, pl.ds(0, size)]
-            )
+            for line in (i, *lines):
+                for dz in (0, 1, 2, 3):
+                    if not (line is i and dz == 0):
+                        arrived(tile(4 * line + chip(dz)), at + 4 * line + chip(dz))
+            result = wide[turn, 0, pl.ds(0, size)]
+            for n in range(1, 16):
+                result = result + wide[turn, n, pl.ds(0, size)]
+            return result
 
         return finish
 
+    chip_weight = jnp.sum(both[3:4], axis=1, keepdims=True)
     finish = wide_sum(
         0,
         jnp.concatenate(
-            [sums, squares, act_sums[:, :half], act_sums[:, half:], jnp.zeros((4, half), F32)], axis=0
+            [
+                sums,
+                squares,
+                act_sums[:, :half],
+                act_sums[:, half:],
+                jnp.broadcast_to(chip_weight, (1, half)),
+                jnp.zeros((3, half), F32),
+            ],
+            axis=0,
         ),
     )
+    for dz in (1, 2, 3):
+        head_landed(i, dz)
+        head_forward(i, dz, (xn, c))
+        head_forward(i, dz, (yn, c))
     inner = act_in[pl.ds(1, SIDE + 1)].reshape((SIDE + 1) * PITCH, per_chip, width)
     inner = inner[1 : 1 + SIDE * PITCH].reshape(SIDE * rows_c, width)
     act_t[pl.ds(0, width), :] = inner.T
@@ -715,7 +727,14 @@
     act_t[pl.ds(width, 16), :] = jnp.where(is_real, 1.0, 0.0).astype(BF16)
     d_pad[pl.ds(0, FRONT)] = jnp.zeros((FRONT, per_chip, half), BF16)
     d_pad[pl.ds(FRONT + SIDE * PITCH, FRONT)] = jnp.zeros((FRONT, per_chip, half), BF16)
+    for dz in (0, 1):
+        head_landed(xn, dz)
+        head_forward(xn, dz, (yn, c))
+    for dz in (2, 3):
+        head_landed(yn, dz)
+        head_forward(yn, dz, (xn, c))
     totals_two = finish()
+    total = totals_two[4:5, 0:1]
     mean_two = totals_two[0:1] / count_all
     inv_two = lax.rsqrt(totals_two[1:2] / count_all - mean_two * mean_two + EPS)
     centre = jnp.concatenate([totals_two[2:3], totals_two[3:4]], axis=1) / count_all
@@ -733,6 +752,14 @@
     pooled = lax.fori_loop(0, SIDE, second_act, jnp.zeros((per_chip, half), F32)) / PIX
     pooled_low = pooled.astype(BF16)
 
+    for line, dz in ((yn, 0), (yn, 1), (xn, 2), (xn, 3), (dg, 0), (dg, 1), (dg, 2), (dg, 3)):
+        head_landed(line, dz)
+    hd_sib = new_recv()
+    theirs = head.at[pl.ds(2 * (1 - k), 2), :, k]
+    push(theirs, theirs, (i, sib), hd_sib)
+    for dz in (1, 2, 3):
+        arrived(info.at[chip(dz)], i_recv + chip(dz))
+    slots = info[0] + info[1] + info[2] + info[3]
     arrived(head.at[pl.ds(2 * k, 2), :, 1 - k], hd_sib)
     head_half = head[pl.ds(2 * k, 2)].reshape(half, head.shape[4])
     logit[0] = jnp.dot(pooled_low, head_half, preferred_element_type=F32)
@@ -769,19 +796,24 @@
 
     d_bias, d_gain = lax.fori_loop(0, SIDE, second_back, (zero_half, zero_half))
 
-    gh_swap = new_recv()
-
-    def head_gradient():
-        gh_half[...] = matmul_tn(pooled_low, d_logits).astype(BF16).reshape(gh_half.shape)
-        push(gh_half.at[:, :, 1 - k], gh.at[pl.ds(2 * k, 2)], (i, sib), gh_swap)
-
     finish = wide_sum(
         1,
         jnp.concatenate(
             [d_gain, d_bias, jnp.broadcast_to(partial, (1, half)), jnp.zeros((5, half), F32)], axis=0
         ),
-        head_gradient,
-    )
+    )
+    gh_swap = new_recv()
+    gh_half[...] = matmul_tn(pooled_low, d_logits).astype(BF16).reshape(gh_half.shape)
+    push(gh_half.at[:, :, 1 - k], gh.at[pl.ds(2 * k, 2)], (i, sib), gh_swap)
+    gh[pl.ds(2 * k, 2)] = jnp.where(
+        k == 0, gh_half[:, :, 0].astype(F32), gh_half[:, :, 1].astype(F32)
+    ).astype(BF16)
+    arrived(gh.at[pl.ds(2 * (1 - k), 2)], gh_swap)
+    h_one, h_two, h_z = new_recv(4), new_recv(2), new_recv(4)
+    for way, first in enumerate((xn, yn)):
+        part = pl.ds(2 * way, 2)
+        push(gh.at[dg, part], rh_one.at[way, 1], (first, c), h_one + 2 * way + 1)
+        push(gh.at[first, part], rh_one.at[way, 0], (first, c), h_one + 2 * way)
     totals_back = finish()
     loss[...] = totals_back[2:3, :128]
     wide_sib[0] = totals_back
@@ -799,21 +831,35 @@
 
     lax.fori_loop(0, SIDE, second_grad, 0)
 
-    def back_conv(h, carry):
+    def back_conv(h):
         out = jnp.zeros((rows_c, width), F32)
         for t in range(TAPS):
             up, left = tap_of(t)
             rows = d_pad[pl.ds(PITCH * h + FRONT + PITCH + 1 - PITCH * up - left, PITCH)]
             out = out + matmul_nt(rows.reshape(rows_c, half), kern[pl.ds(width * t, width), :])
-        d_act[h] = out.reshape(PITCH, per_chip, width)
+        return out.reshape(PITCH, per_chip, width)
+
+    s0 = (SIDE - UPPER) * (1 - k)
+
+    def back_theirs(r, carry):
+        out = back_conv(s0 + r)
+        d_act[s0 + r] = out
+        d_send[r] = out[:SIDE].astype(BF16)
         return carry
 
-    lax.fori_loop(0, SIDE, back_conv, 0)
-    s0 = (SIDE - UPPER) * (1 - k)
-    for r in range(UPPER):
-        d_send[r] = d_act[s0 + r][:SIDE].astype(BF16)
+    def back_mine(r, carry):
+        d_act[UPPER * k + r] = back_conv(UPPER * k + r)
+        return carry
+
+    lax.fori_loop(0, UPPER, back_theirs, 0)
     d_at = new_recv()
     push(d_send, d_recv, (i, sib), d_at)
+    for way, second in enumerate((yn, xn)):
+        part = pl.ds(2 * way, 2)
+        arrived(rh_one.at[way, 1], h_one + 2 * way + 1)
+        gh[second, part] = (gh[second, part].astype(F32) + rh_one[way, 1].astype(F32)).astype(BF16)
+        push(gh.at[second, part], rh_two.at[way], (second, c), h_two + way)
+    lax.fori_loop(0, SIDE - UPPER, back_mine, 0)
 
     def kernel_gradient(t, carry):
         rows = d_pad[pl.ds(FRONT + PITCH + 1 - PITCH * lax.div(t, 3) - lax.rem(t, 3), SIDE * PITCH)]
@@ -839,65 +885,54 @@
 
     for dz in (1, 2, 3):
         push(channels_of(dz), back_into, (i, zdev(dz)), b_recv + z)
-    keep = pltpu.make_async_copy(channels_of(0), back_into, local_sem.at[1])
+    keep = pltpu.make_async_copy(channels_of(0), back_into, local_sem.at[UPPER])
     keep.start()
 
     sent.pop(0).wait_send()
     edge_rows[...] = jnp.zeros(edge_rows.shape, F32)
     lax.fori_loop(0, TAPS, kernel_gradient, 0)
-    arrived(gh.at[pl.ds(2 * (1 - k), 2)], gh_swap)
-    gh[pl.ds(2 * k, 2)] = jnp.where(
-        k == 0, gh_half[:, :, 0].astype(F32), gh_half[:, :, 1].astype(F32)
-    ).astype(BF16)
-
     def gk_at(line, dz):
         return gk.at[pl.ds(pl.multiple_of(chunk * (line * 4 + chip(dz)), 32), chunk)]
 
-    def gh_at(line, dz):
-        return gh.at[line, chip(dz)]
-
-    order = (1, 2, 3, 0)
     ways = {1: (xn, yn), 2: (yn, xn), 3: (xn, yn), 0: (yn, xn)}
-    one_at = {dz: new_recv(4) for dz in order}
-    two_at = {dz: new_recv(2) for dz in order}
-    z_at = new_recv(8)
+    one_at = {dz: new_recv(2) for dz in (3, 2, 1, 0)}
+    two_at = {dz: new_recv() for dz in (3, 2, 1, 0)}
+    z_at = new_recv(4)
 
     def start_one(dz):
         first, second = ways[dz]
         push(gk_at(dg, dz), rk_one.at[dz, 1], (first, c), one_at[dz] + 1)
-        push(gh_at(dg, dz), rh_one.at[dz, 1], (first, c), one_at[dz] + 3)
         push(gk_at(first, dz), rk_one.at[dz, 0], (first, c), one_at[dz])
-        push(gh_at(first, dz), rh_one.at[dz, 0], (first, c), one_at[dz] + 2)
 
     def start_two(dz):
         first, second = ways[dz]
         arrived(rk_one.at[dz, 1], one_at[dz] + 1)
-        arrived(rh_one.at[dz, 1], one_at[dz] + 3)
-        into_k, into_h = gk_at(second, dz), gh_at(second, dz)
+        into_k = gk_at(second, dz)
         into_k[...] = (into_k[...].astype(F32) + rk_one[dz, 1].astype(F32)).astype(BF16)
-        into_h[...] = (into_h[...].astype(F32) + rh_one[dz, 1].astype(F32)).astype(BF16)
         push(into_k, rk_two.at[dz], (second, c), two_at[dz])
-        push(into_h, rh_two.at[dz], (second, c), two_at[dz] + 1)
 
     def plane_done(dz):
         arrived(rk_one.at[dz, 0], one_at[dz])
-        arrived(rh_one.at[dz, 0], one_at[dz] + 2)
         arrived(rk_two.at[dz], two_at[dz])
-        arrived(rh_two.at[dz], two_at[dz] + 1)
-        into_k, into_h = gk_at(i, dz), gh_at(i, dz)
+        into_k = gk_at(i, dz)
         sum_k = into_k[...].astype(F32) + rk_one[dz, 0].astype(F32) + rk_two[dz].astype(F32)
-        sum_h = into_h[...].astype(F32) + rh_one[dz, 0].astype(F32) + rh_two[dz].astype(F32)
         if dz == 0:
-            return sum_k, sum_h
+            return sum_k
         into_k[...] = sum_k.astype(BF16)
-        into_h[...] = sum_h.astype(BF16)
         push(into_k, rk_z.at[z], (i, zdev(dz)), z_at + z)
-        push(into_h, rh_z.at[z], (i, zdev(dz)), z_at + 4 + z)
         return None
 
-    for dz in order:
-        start_one(dz)
-    finish_edges = wide_sum(2, edge_rows[...], size=edge_rows.shape[0])
+    start_one(3)
+    start_one(2)
+    for way in (0, 1):
+        part = pl.ds(2 * way, 2)
+        arrived(rh_one.at[way, 0], h_one + 2 * way)
+        arrived(rh_two.at[way], h_two + way)
+        sum_h = gh[i, part].astype(F32) + rh_one[way, 0].astype(F32) + rh_two[way].astype(F32)
+        h_sum[part] = sum_h
+        gh[i, part] = sum_h.astype(BF16)
+    for dz in (3, 2, 1):
+        push(gh.at[i, chip(dz)], rh_z.at[z], (i, zdev(dz)), h_z + z)
 
     keep.wait()
     for dz in (1, 2, 3):
@@ -920,8 +955,11 @@
     finish = small_sum(
         1, jnp.concatenate([d_gain, d_bias, jnp.zeros((6, 128), F32)], axis=0)
     )
-    start_two(1)
+    start_two(3)
     start_two(2)
+    start_one(1)
+    start_one(0)
+    finish_edges = wide_sum(2, edge_rows[...])
     totals_one = finish()
     g_bn_one[...] = jnp.where(k == 0, totals_one[0:2, :own_ch], totals_one[0:2, own_ch:])
     scale_one = gain_one * inv_one
@@ -956,10 +994,8 @@
     g_at = new_recv()
     push(go_send, go_recv, (i, sib), g_at)
     g_one[...] = jnp.where(k == 0, low, high)
-    plane_done(1)
+    plane_done(3)
     plane_done(2)
-    start_two(3)
-    start_two(0)
     arrived(go_recv, g_at)
     part = own_ch // 2
     ga_send[0] = (g_one[...] + go_recv[...].astype(F32)).astype(BF16)
@@ -967,6 +1003,8 @@
     upper, lower = pl.ds(0, part), pl.ds(part, part)
     push(ga_send.at[0, upper], ga_recv.at[0, upper], (xn, c), first_at)
     push(ga_send.at[0, lower], ga_recv.at[0, lower], (yn, c), first_at + 1)
+    start_two(1)
+    start_two(0)
     arrived(ga_recv.at[0, upper], first_at)
     arrived(ga_recv.at[0, lower], first_at + 1)
     ga_send[1] = (ga_send[0].astype(F32) + ga_recv[0].astype(F32)).astype(BF16)
@@ -974,8 +1012,8 @@
     push(ga_send.at[1, lower], ga_recv.at[1, lower], (xn, c), second_at + 1)
 
     edges = finish_edges()
-    plane_done(3)
-    sum_k, sum_h = plane_done(0)
+    plane_done(1)
+    sum_k = plane_done(0)
 
     arrived(ga_recv.at[1, upper], second_at)
     arrived(ga_recv.at[1, lower], second_at + 1)
@@ -990,12 +1028,26 @@
         )
     offset = pl.multiple_of(row_at - width * tap, 32)
     sum_k = sum_k + ranked[pl.ds(offset, chunk), :]
+    sum_h = h_sum[z]
     for dz in (1, 2, 3):
         arrived(rk_z.at[chip(dz)], z_at + chip(dz))
-        arrived(rh_z.at[chip(dz)], z_at + 4 + chip(dz))
+        arrived(rh_z.at[chip(dz)], h_z + chip(dz))
         sum_k = sum_k + rk_z[chip(dz)].astype(F32)
         sum_h = sum_h + rh_z[chip(dz)].astype(F32)
-    g_head[...] = sum_h
+    head_flat[...] = sum_h
+    g_head[...] = jnp.zeros(g_head.shape, F32)
+    for r in range(head_rows):
+        first, shift = divmod(classes * r, 128)
+        rows = jnp.concatenate(
+            [head_flat[r : r + 1, 128 * j : 128 * j + 128] for j in range(8)], axis=0
+        )
+        if shift:
+            rows = pltpu.roll(rows, shift, 1)
+        count = min(8, g_head.shape[0] - first)
+        g_head[first : first + count, :] += jnp.where(lane >= shift, rows, 0.0)[:count]
+        count = min(8, g_head.shape[0] - first - 1)
+        if shift:
+            g_head[first + 1 : first + 1 + count, :] += jnp.where(lane < shift, rows, 0.0)[:count]
     last_send[...] = sum_k
     l_at = new_recv()
     theirs = last_send.at[pl.ds(pl.multiple_of(block * (1 - k), 16), block)]
@@ -1021,8 +1073,8 @@
 
 
 def update_kernel(rates, *refs):
-    take, give = refs[:20], refs[20:]
-    rate_one, rate_bn_one, rate_two, rate_bn_two = rates
+    take, give = refs[:24], refs[24:]
+    rate_one, rate_bn_one, rate_two, rate_bn_two, rate_head = rates
     w, g, m, v, mask, rank = (r[...] for r in take[:6])
     results = sparse_update(w, g * mask.astype(F32), m, v, mask, rank, rate_one)
     for ref, value in zip(give[:5], results):
@@ -1031,12 +1083,15 @@
     results = sparse_update(w, g * mask.astype(F32), m, v, mask, rank, rate_two)
     for ref, value in zip(give[5:10], results):
         ref[...] = value
-    w, g, m, v = (r[...] for r in take[12:16])
-    for ref, value in zip(give[10:13], dense_update(w, g, m, v, rate_bn_one)):
-        ref[...] = value
-    w, g, m, v = (r[...] for r in take[16:20])
-    for ref, value in zip(give[13:16], dense_update(w, g, m, v, rate_bn_two)):
-        ref[...] = value
+
+    @pl.when(pl.program_id(0) == 0)
+    def _():
+        for n, rate in enumerate((rate_bn_one, rate_bn_two, rate_head)):
+            w, g, m, v = (r[...] for r in take[12 + 4 * n : 16 + 4 * n])
+            results = dense_update(w, g, m, v, rate)
+            for ref, value in zip(give[10 + 3 * n : 13 + 3 * n], results):
+                ref[...] = value
+        give[19][...] = results[0].astype(BF16)
 
 
 def fast_shards(
@@ -1060,9 +1115,7 @@
     block = w_two.shape[0] // width
     chunk = 2 * block
     flat = (w_two.shape[0] // 128, 128)
-    headp = jnp.pad(
-        w_head.astype(BF16).reshape(head_rows, classes), ((0, 0), (0, lanes - classes))
-    )
+    top = [a.reshape(-1, 128) for a in (w_head, mom_head, avg_head)]
     one = [a.T for a in (w_one, mom_one, avg_one, mask_one, rank_one_in)]
     two = [a.reshape(flat) for a in (w_two, mom_two, avg_two, mask_two, rank_two)]
     vmem = pl.BlockSpec(memory_space=pltpu.VMEM)
@@ -1075,7 +1128,7 @@
         out_shape=(
             shape((own_ch, cin), F32),
             shape(flat, F32),
-            shape((head_rows, lanes), F32),
+            shape(top[0].shape, F32),
             shape((2, own_ch), F32),
             shape((2, width), F32),
             shape((1, 128), F32),
@@ -1100,21 +1153,21 @@
             v((UPPER, SIDE, group, chip_ch), BF16),
             v((2, 8, 128), F32),
             v((4, 8, 128), F32),
-            v((2, 2, 8, 128), F32),
-            v((2, 4, 8, 128), F32),
-            v((3, 4, 16, half), F32),
-            v((3, 4, 16, half), F32),
+            v((2, 8, 8, 128), F32),
+            v((3, 16, 16, half), F32),
             v((2, 8, half), F32),
             v((2, per_chip, lanes), F32),
             v((2, 4, 2, head_rows, lanes), BF16),
             v((TAPS * width, half), BF16),
             v((4, 4, head_rows, lanes), BF16),
             v((4, 2, chunk, half), BF16),
-            v((4, 2, head_rows, lanes), BF16),
+            v((2, 2, 2, head_rows, lanes), BF16),
+            v((4, chunk, half), BF16),
+            v((2, 2, head_rows, lanes), BF16),
             v((4, chunk, half), BF16),
             v((4, head_rows, lanes), BF16),
-            v((4, chunk, half), BF16),
-            v((4, head_rows, lanes), BF16),
+            v((4, head_rows, lanes), F32),
+            v((head_rows, lanes), F32),
             v((chunk, half), F32),
             v((block, half), F32),
             v((16, half), F32),
@@ -1126,9 +1179,9 @@
             v((2, own_ch, cin), BF16),
             v((2, own_ch, cin), BF16),
             pltpu.SemaphoreType.DMA((UPPER,)),
-            pltpu.SemaphoreType.DMA((2,)),
-            pltpu.SemaphoreType.DMA((150,)),
-            pltpu.SemaphoreType.DMA((150,)),
+            pltpu.SemaphoreType.DMA((UPPER + 1,)),
+            pltpu.SemaphoreType.DMA((SEMS,)),
+            pltpu.SemaphoreType.DMA((SEMS,)),
         ],
         compiler_params=pltpu.CompilerParams(
             collective_id=0, has_side_effects=True, vmem_limit_bytes=56 << 20
@@ -1144,7 +1197,7 @@
         first_norm_params,
         two[0],
         two[3],
-        headp,
+        top[0],
         second_norm_params,
     )
     root = math.sqrt(images)
@@ -1153,33 +1206,33 @@
     two_spec = pl.BlockSpec((flat[0] // steps, 128), lambda n: (n, 0))
     bno_spec = pl.BlockSpec((2, own_ch), lambda n: (0, 0))
     bnt_spec = pl.BlockSpec((2, width), lambda n: (0, 0))
+    top_spec = pl.BlockSpec(top[0].shape, lambda n: (0, 0))
     f_one, f_two = shape(one[0].shape, F32), shape(flat, F32)
     new = pl.pallas_call(
-        functools.partial(update_kernel, (1.3 * root, 8.0 * root, 0.25 * root, root)),
+        functools.partial(update_kernel, (1.3 * root, 8.0 * root, 0.25 * root, root, 40.0)),
         grid=(steps,),
-        in_specs=[one_spec] * 6 + [two_spec] * 6 + [bno_spec] * 4 + [bnt_spec] * 4,
-        out_specs=[one_spec] * 5 + [two_spec] * 5 + [bno_spec] * 3 + [bnt_spec] * 3,
+        in_specs=[one_spec] * 6 + [two_spec] * 6 + [bno_spec] * 4 + [bnt_spec] * 4 + [top_spec] * 4,
+        out_specs=[one_spec] * 5 + [two_spec] * 5 + [bno_spec] * 3 + [bnt_spec] * 3 + [top_spec] * 4,
         out_shape=[f_one] * 3 + [shape(f_one.shape, jnp.int32), shape(f_one.shape, BF16)]
         + [f_two] * 3 + [shape(flat, jnp.int32), shape(flat, BF16)]
-        + [shape((2, own_ch), F32)] * 3 + [shape((2, width), F32)] * 3,
-        compiler_params=pltpu.CompilerParams(vmem_limit_bytes=32 << 20),
+        + [shape((2, own_ch), F32)] * 3 + [shape((2, width), F32)] * 3
+        + [shape(top[0].shape, F32)] * 3 + [shape(top[0].shape, BF16)],
+        compiler_params=pltpu.CompilerParams(vmem_limit_bytes=56 << 20),
         name="update",
     )(
         one[0], g_one, one[1], one[2], one[3], one[4],
         two[0], g_two, two[1], two[2], two[3], two[4],
         first_norm_params, g_bn_one, mom_bn_one, avg_bn_one,
         second_norm_params, g_bn_two, mom_bn_two, avg_bn_two,
-    )
-    g_head = g_head[:, :classes].reshape(-1)
-    top_head = dense_update(w_head, g_head, mom_head, avg_head, 40.0)
+        top[0], g_head, top[1], top[2],
+    )
     return (
         loss[0, 0],
         *(a.T for a in new[:5]),
         *new[10:13],
         *(a.reshape(-1) for a in new[5:10]),
         *new[13:16],
-        *top_head,
-        top_head[0].astype(BF16),
+        *(a.reshape(-1) for a in new[16:20]),
     )
 
 

time: 147 us -> 125 us (0.85)
  Pallas kernels: 132 us -> 122 us
  local copies, waits for them, and re-layouts: 7.3 us -> 0 us
  other arithmetic: 4.63 us -> 0 us
    pallas_call x1, Pallas kernels: 129 us -> 117 us  [fast_shards(): pl.pallas_call(functools.partial(step_kernel, (group, per_chip, classes,...]
    unnamed x42 -> x0, local copies, waits for them, and re-layouts: 3.43 us -> none
    pallas_call x1, Pallas kernels: 2.41 us -> 5.63 us  [fast_shards(): pl.pallas_call(functools.partial(update_kernel, (1.3 * root, 8.0 * root,...]
    convert_element_type x2 -> x0, other arithmetic: 3.13 us -> none  [the longest x1 1.61 us: fast_shards(): w_head.astype(BF16).reshape(head_rows, classes)]
    reshape x2 -> x0, local copies, waits for them, and re-layouts: 2.43 us -> none  [the longest x1 1.49 us: fast_shards(): w_head.astype(BF16).reshape(head_rows, classes)]
    add x1 -> x0, other arithmetic: 1.5 us -> none  [dense_update(): return (moved, velocity, 0.5 * average + 0.5 * moved)]
where the time goes in v3:
time: 125 us
  Pallas kernels  122 us (98%)
  between operations  2.42 us (2%)
    pallas_call x1, Pallas kernels, fast_shards(): pl.pallas_call(functools.partial(step_kernel, (group, per_chip, classes,...  117 us
    pallas_call x1, Pallas kernels, fast_shards(): pl.pallas_call(functools.partial(update_kernel, (1.3 * root, 8.0 * root,...  5.63 us

profile of v3, /device:TPU:1, one launch (start us, length us, event | category | flops | bytes accessed | tf_op | source)
XLA Modules:
  0.0 124.6 jit_solution(9805369331324756749)
XLA Ops:
  0.7 116.6 %step.1 = (f32[64,2048]{1,0:T(8,128)}, f32[576,128]{1,0:T(8,128)}, f32[125,128]{1,0:T(8,128)}, f32[2,64]{1,0:T(2,128)}, f32[2,512]{1,0:T(2,128)}, /*index=5*/f32[1,128]{1,0:T(1,128)}) custom-call(bf16[49,64,2048]{2,1,0:T(8,128)(2,1)} %bitcast.30, s32[1,64]{1,0:T(1,128)} %place.1, s32[8]{0:T(128)} %labels.1, s32[8]{0:T(128)} %loss_wt.1, f32[64,2048]{1,0:T(8,128)} %bitcast.31, ...), custom_call_target="tpu_custom_call" | custom-call | tf_op jit(solution)/shard_map/step/pallas_call | solution.py:1126
  117.2 5.6 %update.1 = (f32[64,2048]{1,0:T(8,128)}, f32[64,2048]{1,0:T(8,128)}, f32[64,2048]{1,0:T(8,128)}, s32[64,2048]{1,0:T(8,128)}, bf16[64,2048]{1,0:T(8,128)(2,1)}, /...) custom-call(f32[64,2048]{1,0:T(8,128)} %bitcast.32, ...), custom_call_target="tpu_custom_call" | custom-call | tf_op jit(solution)/shard_map/update/pallas_call | solution.py:1211

commit v4 on v3

--- a/solution.py
+++ b/solution.py
@@ -287,7 +287,7 @@
 UPPER = (SIDE + 1) // 2
 PITCH = SIDE + 1
 FRONT = 2 * PITCH
-SEMS = 240
+SEMS = 92
 
 
 def silu_pair(value):
@@ -319,22 +319,32 @@
 def step_kernel(
     sizes,
     images,
-    place,
-    labels,
-    loss_wt,
-    w_one,
-    mask_one,
-    norm_one,
-    w_two,
-    mask_two,
-    w_head,
-    norm_two,
+    place_in,
+    labels_in,
+    loss_wt_in,
+    w_one_in,
+    mask_one_in,
+    norm_one_in,
+    w_two_in,
+    mask_two_in,
+    w_head_in,
+    norm_two_in,
     g_one,
     g_two,
     g_head,
     g_bn_one,
     g_bn_two,
     loss,
+    w_one,
+    mask_one,
+    w_two,
+    mask_two,
+    w_head,
+    norm_one,
+    norm_two,
+    place,
+    labels,
+    loss_wt,
     feats,
     filt,
     kern,
@@ -377,6 +387,7 @@
     go_recv,
     ga_send,
     ga_recv,
+    load_sem,
     image_sem,
     local_sem,
     send,
@@ -430,6 +441,28 @@
         sent.append(copy)
         return copy
 
+    def push_all(copies, size_of, to):
+        at = next(next_send)
+        for src, dst, device in copies:
+            pltpu.make_async_remote_copy(
+                src_ref=src,
+                dst_ref=dst,
+                send_sem=send.at[at],
+                recv_sem=recv.at[to],
+                device_id=device,
+                device_id_type=MESH,
+            ).start()
+        group_copy = pltpu.make_async_remote_copy(
+            src_ref=size_of,
+            dst_ref=size_of,
+            send_sem=send.at[at],
+            recv_sem=recv.at[to],
+            device_id=(i, sib),
+            device_id_type=MESH,
+        )
+        sent.append(group_copy)
+        return group_copy
+
     def arrived(dst, at):
         pltpu.make_async_remote_copy(
             src_ref=dst,
@@ -445,14 +478,36 @@
             images.at[pl.ds(SIDE * (h0 + r), SIDE)], feats.at[pl.ds(SIDE * r, SIDE)], image_sem.at[r]
         )
 
+    barrier = pltpu.get_barrier_semaphore()
+    same_core = [(o, zdev(dz)) for o in (i, *lines) for dz in (0, 1, 2, 3)][1:]
+    plane = [(i, sib)] + [(o, d) for o in lines for d in (c, sib)]
+    others = plane + same_core[:3]
+    for device in others:
+        pl.semaphore_signal(barrier, inc=1, device_id=device, device_id_type=MESH)
+    loads = [
+        pltpu.make_async_copy(src, dst, load_sem.at[n])
+        for n, (src, dst) in enumerate(
+            (
+                (w_two_in, w_two),
+                (mask_two_in, mask_two),
+                (w_one_in, w_one),
+                (mask_one_in, mask_one),
+                (norm_one_in, norm_one),
+                (labels_in, labels),
+                (loss_wt_in, loss_wt),
+                (w_head_in, w_head),
+                (norm_two_in, norm_two),
+                (place_in, place),
+            )
+        )
+    ]
+    for copy in loads:
+        copy.start()
     for r in range(UPPER):
         image_copy(r).start()
 
-    act_in[0] = jnp.zeros(act_in.shape[1:], BF16)
-    for r in range(SIDE + 1, act_in.shape[0]):
-        act_in[r] = jnp.zeros(act_in.shape[1:], BF16)
-    for r in range(1, SIDE + 1):
-        act_in[r, 0] = jnp.zeros(act_in.shape[2:], BF16)
+    loads[0].wait()
+    loads[1].wait()
     chunk_at = pl.multiple_of(chunk * (i * 4 + z), 32)
     block_at = pl.multiple_of(chunk_at + block * k, 16)
     parts = [
@@ -463,9 +518,103 @@
     high = jnp.concatenate(parts[2:], axis=1).astype(BF16)
     kern[pl.ds(block_at, block), :] = jnp.where(k == 0, low.astype(F32), high.astype(F32)).astype(BF16)
     gk[pl.ds(0, block), :] = jnp.where(k == 0, high.astype(F32), low.astype(F32)).astype(BF16)
+    for copy in loads[2:7]:
+        copy.wait()
     own_at = pl.multiple_of(own_ch * k, 16)
     filt[pl.ds(own_at, own_ch), :] = (w_one[...] * mask_one[...].astype(F32)).astype(BF16)
     lane = lax.broadcasted_iota(jnp.int32, (1, 128), 1)
+    norms = norm_one[...]
+    nothing = jnp.zeros_like(norms)
+    placed = jnp.where(
+        k == 0, jnp.concatenate([norms, nothing], axis=1), jnp.concatenate([nothing, norms], axis=1)
+    )
+    label_row, weight_row = jnp.zeros((1, 128), F32), jnp.zeros((1, 128), F32)
+    for j in range(labels.shape[0]):
+        here = lane == labels.shape[0] * c + j
+        label_row = jnp.where(here, labels[j].astype(F32), label_row)
+        weight_row = jnp.where(here, loss_wt[j].astype(F32), weight_row)
+    early[0] = jnp.concatenate(
+        [placed, label_row, weight_row, jnp.zeros((4, 128), F32)], axis=0
+    )
+
+    pl.semaphore_wait(barrier, len(others))
+
+    k_sib, f_sib, e_sib = new_recv(), new_recv(), new_recv()
+    push(gk.at[pl.ds(0, block)], kern.at[pl.ds(block_at, block)], (i, sib), k_sib)
+    push(filt.at[pl.ds(own_at, own_ch)], filt.at[pl.ds(own_at, own_ch)], (i, sib), f_sib)
+    push(early.at[0], early.at[1], (i, sib), e_sib)
+
+    k_recv = new_recv(32)
+
+    def kern_at(line, dz, u):
+        at = chunk * (line * 4 + chip(dz)) + block * (k if u == 0 else 1 - k)
+        return kern.at[pl.ds(pl.multiple_of(at, 16), block)]
+
+    def forward(line, dz, u, *devices):
+        for device in devices:
+            at = k_recv + 2 * (line * 4 + chip(dz)) + u
+            push(kern_at(line, dz, u), kern_at(line, dz, u), device, at)
+
+    def landed(line, dz, u):
+        arrived(kern_at(line, dz, u), k_recv + 2 * (line * 4 + chip(dz)) + u)
+
+    def relay(line, dz, u, *devices):
+        landed(line, dz, u)
+        forward(line, dz, u, *devices)
+
+    to_x, to_y = (xn, c), (yn, c)
+    to_z = [(i, zdev(dz)) for dz in (1, 2, 3)]
+    forward(i, 0, 0, to_x, to_y, *to_z)
+    act_in[0] = jnp.zeros(act_in.shape[1:], BF16)
+    for r in range(SIDE + 1, act_in.shape[0]):
+        act_in[r] = jnp.zeros(act_in.shape[1:], BF16)
+    for r in range(1, SIDE + 1):
+        act_in[r, 0] = jnp.zeros(act_in.shape[2:], BF16)
+    other_block_at = pl.multiple_of(chunk_at + block * (1 - k), 16)
+    arrived(kern.at[pl.ds(other_block_at, block)], k_sib)
+    forward(i, 0, 1, to_x, to_y, *to_z)
+    arrived(early.at[1], e_sib)
+    both = early[0] + early[1]
+    info[z] = both
+    i_recv = new_recv()
+    push_all([(info.at[z], info.at[z], device) for device in to_z], info.at[pl.ds(0, 3)], i_recv)
+    other_at = pl.multiple_of(own_ch * (1 - k), 16)
+    arrived(filt.at[pl.ds(other_at, own_ch)], f_sib)
+
+    def first_conv(r, carry):
+        sums, squares = carry
+        image_copy(r).wait()
+        rows = feats[pl.ds(SIDE * r, SIDE)].reshape(rows_a, feats.shape[2])
+        out = matmul_nt(rows, filt[...])
+        z_one[pl.ds(pl.multiple_of(rows_a * r, 64), rows_a), :] = out
+        counted = jnp.where((r == 0) & (k == 1), 0.0, 1.0)
+        return (
+            sums + counted * jnp.sum(out, axis=0, keepdims=True),
+            squares + counted * jnp.sum(out * out, axis=0, keepdims=True),
+        )
+
+    zero_row = jnp.zeros((1, chip_ch), F32)
+    sums, squares = lax.fori_loop(0, UPPER, first_conv, (zero_row, zero_row))
+
+    def small_sum(turn, rows):
+        own = 2 * i + k
+        tiles[turn, own] = rows
+        at = new_recv()
+        tile, all_others = tiles.at[turn, own], tiles.at[turn, pl.ds(0, 7)]
+        push_all([(tile, tile, device) for device in plane], all_others, at)
+
+        def finish():
+            arrived(all_others, at)
+            result = tiles[turn, 0]
+            for n in range(1, 8):
+                result = result + tiles[turn, n]
+            return result
+
+        return finish
+
+    finish = small_sum(0, jnp.concatenate([sums, squares, jnp.zeros((6, 128), F32)], axis=0))
+    for copy in loads[7:]:
+        copy.wait()
     for r in range(head_rows):
         first, shift = divmod(classes * r, 128)
         taken = -(-(shift + classes) // 128)
@@ -479,111 +628,9 @@
             head_flat[r : r + 1, 128 * j : 128 * j + 128] = rows[j : j + 1]
     head_lane = lax.broadcasted_iota(jnp.int32, (head_rows, 1024), 1)
     head[i, z, k] = jnp.where(head_lane < classes, head_flat[...], 0.0).astype(BF16)
-    norms = norm_one[...]
-    nothing = jnp.zeros_like(norms)
-    placed = jnp.where(
-        k == 0, jnp.concatenate([norms, nothing], axis=1), jnp.concatenate([nothing, norms], axis=1)
-    )
-    label_row, weight_row = jnp.zeros((1, 128), F32), jnp.zeros((1, 128), F32)
-    for j in range(labels.shape[0]):
-        here = lane == labels.shape[0] * c + j
-        label_row = jnp.where(here, labels[j].astype(F32), label_row)
-        weight_row = jnp.where(here, loss_wt[j].astype(F32), weight_row)
-    early[0] = jnp.concatenate(
-        [placed, label_row, weight_row, jnp.zeros((4, 128), F32)], axis=0
-    )
-
-    barrier = pltpu.get_barrier_semaphore()
-    same_core = [(o, zdev(dz)) for o in (i, *lines) for dz in (0, 1, 2, 3)][1:]
-    plane = [(i, sib)] + [(o, d) for o in lines for d in (c, sib)]
-    others = same_core + [plane[0]] + [p for p in plane[1:] if p[1] is sib]
-    for device in others:
-        pl.semaphore_signal(barrier, inc=1, device_id=device, device_id_type=MESH)
-    pl.semaphore_wait(barrier, len(others))
-
-    k_sib, f_sib, e_sib = new_recv(), new_recv(), new_recv()
-    push(gk.at[pl.ds(0, block)], kern.at[pl.ds(block_at, block)], (i, sib), k_sib)
-    push(filt.at[pl.ds(own_at, own_ch)], filt.at[pl.ds(own_at, own_ch)], (i, sib), f_sib)
-    push(early.at[0], early.at[1], (i, sib), e_sib)
-
-    k_recv, h_recv = new_recv(16), new_recv(16)
-
-    def kern_at(line, dz):
-        return kern.at[pl.ds(pl.multiple_of(chunk * (line * 4 + chip(dz)), 32), chunk)]
-
-    def head_at(line, dz):
-        return head.at[line, chip(dz), k]
-
-    def number(line, dz):
-        return line * 4 + chip(dz)
-
-    def forward(line, dz, device):
-        push(kern_at(line, dz), kern_at(line, dz), device, k_recv + number(line, dz))
-
-    def landed(line, dz):
-        arrived(kern_at(line, dz), k_recv + number(line, dz))
-
-    def head_forward(line, dz, device):
-        push(head_at(line, dz), head_at(line, dz), device, h_recv + number(line, dz))
-
-    def head_landed(line, dz):
-        arrived(head_at(line, dz), h_recv + number(line, dz))
-
-    other_block_at = pl.multiple_of(chunk_at + block * (1 - k), 16)
-    arrived(kern.at[pl.ds(other_block_at, block)], k_sib)
-    forward(i, 0, (xn, c))
-    forward(i, 0, (yn, c))
-    for dz in (1, 2, 3):
-        forward(i, 0, (i, zdev(dz)))
-    arrived(early.at[1], e_sib)
-    both = early[0] + early[1]
-    info[z] = both
-    i_recv = new_recv(4)
-    for dz in (1, 2, 3):
-        push(info.at[z], info.at[z], (i, zdev(dz)), i_recv + z)
-    other_at = pl.multiple_of(own_ch * (1 - k), 16)
-    arrived(filt.at[pl.ds(other_at, own_ch)], f_sib)
-
-    def first_conv(r, carry):
-        sums, squares = carry
-        image_copy(r).wait()
-        rows = feats[pl.ds(SIDE * r, SIDE)].reshape(rows_a, feats.shape[2])
-        out = matmul_nt(rows, filt[...])
-        z_one[pl.ds(pl.multiple_of(rows_a * r, 64), rows_a), :] = out
-        counted = jnp.where((r == 0) & (k == 1), 0.0, 1.0)
-        return (
-            sums + counted * jnp.sum(out, axis=0, keepdims=True),
-            squares + counted * jnp.sum(out * out, axis=0, keepdims=True),
-        )
-
-    zero_row = jnp.zeros((1, chip_ch), F32)
-    sums, squares = lax.fori_loop(0, UPPER, first_conv, (zero_row, zero_row))
-
-    def small_sum(turn, rows):
-        own = 2 * i + k
-        tiles[turn, own] = rows
-        at = new_recv(8)
-        for device in plane:
-            push(tiles.at[turn, own], tiles.at[turn, own], device, at + own)
-
-        def finish():
-            for line in (i, *lines):
-                arrived(tiles.at[turn, 2 * line + 1 - k], at + 2 * line + 1 - k)
-                if line is not i:
-                    arrived(tiles.at[turn, 2 * line + k], at + 2 * line + k)
-            result = tiles[turn, 0]
-            for n in range(1, 8):
-                result = result + tiles[turn, n]
-            return result
-
-        return finish
-
-    finish = small_sum(0, jnp.concatenate([sums, squares, jnp.zeros((6, 128), F32)], axis=0))
-    landed(i, 1)
-    forward(i, 1, (xn, c))
-    forward(i, 1, (yn, c))
-    landed(xn, 0)
-    forward(xn, 0, (yn, c))
+    relay(i, 1, 0, to_x, to_y)
+    relay(xn, 0, 0, to_y)
+    relay(xn, 0, 1, to_y)
     totals = finish()
     mean_one = totals[0:1] / count_all
     inv_one = lax.rsqrt(totals[1:2] / count_all - mean_one * mean_one + EPS)
@@ -595,11 +642,9 @@
         value, grade = silu_pair(gain_one * hat + bias_one)
         act_out[r] = value.astype(BF16).reshape(SIDE, group, chip_ch)
 
-    a_recv = new_recv(4 * UPPER)
-
-    def into(r, chip_id):
+    def into(row, chip_id):
         return act_in.at[
-            1 + h0 + r, pl.ds(1, SIDE), :, pl.ds(pl.multiple_of(chip_ch * chip_id, 128), chip_ch)
+            1 + row, pl.ds(1, SIDE), :, pl.ds(pl.multiple_of(chip_ch * chip_id, 128), chip_ch)
         ]
 
     def images_of(ref, dz):
@@ -608,51 +653,116 @@
     def images_in_row(ref, r, dz):
         return ref.at[r, :, pl.ds(pl.multiple_of(per_chip * chip(dz), 16), per_chip), :]
 
-    out_copies, kept = [], []
+    def row_copies(r):
+        return [
+            (images_in_row(act_out, r + k, dz), into(UPPER * k + r, z), to_z[dz - 1])
+            for dz in (3, 2, 1)
+        ]
+
+    def keep_row(r, n):
+        return pltpu.make_async_copy(
+            images_in_row(act_out, r, 0), into(h0 + r, z), local_sem.at[n]
+        )
+
+    relay(i, 2, 0, to_x, to_y)
+    relay(xn, 1, 0, to_y)
+    relay(i, 3, 0, to_x, to_y)
+    relay(i, 1, 1, to_x, to_y)
     for r in range(UPPER):
         first_act(r)
+    a_recv, a_more = new_recv(), new_recv()
+    common = SIDE - UPPER
+    out_copies = [
+        push_all(
+            [copy for r in range(common) for copy in row_copies(r)],
+            act_out.at[pl.ds(0, 3), :, pl.ds(0, 3 * per_chip)],
+            a_recv,
+        )
+    ]
+    more_send = next(next_send)
+
+    def more_copy(dz):
+        return pltpu.make_async_remote_copy(
+            src_ref=images_in_row(act_out, common, dz),
+            dst_ref=into(common, z),
+            send_sem=send.at[more_send],
+            recv_sem=recv.at[a_more],
+            device_id=to_z[dz - 1],
+            device_id_type=MESH,
+        )
+
+    more_size = act_out.at[0, :, pl.ds(0, 3 * per_chip)]
+    more_wait = pltpu.make_async_remote_copy(
+        src_ref=more_size,
+        dst_ref=more_size,
+        send_sem=send.at[more_send],
+        recv_sem=recv.at[a_more],
+        device_id=(i, sib),
+        device_id_type=MESH,
+    )
+
+    @pl.when(k == 0)
+    def _():
         for dz in (3, 2, 1):
-            out_copies.append(
-                push(images_in_row(act_out, r, dz), into(r, z), (i, zdev(dz)), a_recv + 4 * r + z)
-            )
-        kept.append(
-            pltpu.make_async_copy(images_in_row(act_out, r, 0), into(r, z), local_sem.at[r])
-        )
-        kept[-1].start()
-    landed(i, 2)
-    forward(i, 2, (xn, c))
-    forward(i, 2, (yn, c))
-    landed(xn, 1)
-    forward(xn, 1, (yn, c))
-    landed(i, 3)
-    forward(i, 3, (xn, c))
-    forward(i, 3, (yn, c))
-    landed(yn, 2)
-    forward(yn, 2, (xn, c))
-    landed(yn, 3)
-    forward(yn, 3, (xn, c))
-    head_forward(i, 0, (xn, c))
-    head_forward(i, 0, (yn, c))
-    for dz in (1, 2, 3):
-        head_forward(i, 0, (i, zdev(dz)))
+            more_copy(dz).start()
+        keep_row(common, common).start()
+
+    kept = [keep_row(r + k, r) for r in range(common)]
+    for copy in kept:
+        copy.start()
+    relay(yn, 2, 0, to_x)
+    relay(i, 2, 1, to_x, to_y)
+    relay(xn, 1, 1, to_y)
+    relay(yn, 3, 0, to_x)
+    relay(i, 3, 1, to_x, to_y)
+    relay(yn, 2, 1, to_x)
+    relay(yn, 3, 1, to_x)
+    hz_recv = new_recv()
+    own_head, line_head = head.at[i, z, k], head.at[i, :, k]
+    push_all([(own_head, own_head, device) for device in to_z], head.at[i, pl.ds(0, 3), k], hz_recv)
 
     for copy in kept:
         copy.wait()
-    for r in range(UPPER):
-        for dz in (1, 2, 3):
-            arrived(into(r, chip(dz)), a_recv + 4 * r + chip(dz))
-    a_sib = new_recv()
-    mine = act_in.at[pl.ds(1 + UPPER * k, SIDE - UPPER), pl.ds(1, SIDE)]
+    arrived(act_out.at[pl.ds(0, 3), :, pl.ds(0, 3 * per_chip)], a_recv)
+    a_sib, m_sib = new_recv(), new_recv()
+    mine = act_in.at[pl.ds(1 + UPPER * k, common), pl.ds(1, SIDE)]
     push(mine, mine, (i, sib), a_sib)
+    m_send = next(next_send)
+    middle = pltpu.make_async_remote_copy(
+        src_ref=act_in.at[1 + common, pl.ds(1, SIDE)],
+        dst_ref=act_in.at[1 + common, pl.ds(1, SIDE)],
+        send_sem=send.at[m_send],
+        recv_sem=recv.at[m_sib],
+        device_id=(i, sib),
+        device_id_type=MESH,
+    )
+
+    @pl.when(k == 0)
+    def _():
+        keep_row(common, common).wait()
+        more_wait.wait_recv()
+        middle.start()
+
     for line, dz in ((yn, 0), (yn, 1), (xn, 2), (xn, 3), (dg, 0), (dg, 1), (dg, 2), (dg, 3)):
-        landed(line, dz)
-    arrived(act_in.at[pl.ds(1 + UPPER * (1 - k), SIDE - UPPER), pl.ds(1, SIDE)], a_sib)
+        landed(line, dz, 0)
+        landed(line, dz, 1)
+    arrived(act_in.at[pl.ds(1 + UPPER * (1 - k), common), pl.ds(1, SIDE)], a_sib)
+
+    @pl.when(k == 1)
+    def _():
+        middle.wait_recv()
+
+    @pl.when(k == 0)
+    def _():
+        middle.wait_send()
+        more_wait.wait_send()
 
     def tap_of(t):
         return t // 3, t % 3
 
     def second_conv(h, carry):
-        sums, squares = carry
+        sums, squares, act_sums = carry
+        inner = act_in[h + 1].reshape(rows_c, width).astype(F32)
         out = jnp.zeros((rows_c, half), F32)
         for t in range(TAPS):
             up, left = tap_of(t)
@@ -666,33 +776,24 @@
         return (
             sums + jnp.sum(real, axis=0, keepdims=True),
             squares + jnp.sum(real * real, axis=0, keepdims=True),
+            act_sums + jnp.sum(inner, axis=0, keepdims=True),
         )
 
     zero_half = jnp.zeros((1, half), F32)
-    sums, squares = lax.fori_loop(0, SIDE, second_conv, (zero_half, zero_half))
-
-    def act_sum(h, carry):
-        rows = act_in[h + 1].reshape(rows_c, width).astype(F32)
-        return carry + jnp.sum(rows, axis=0, keepdims=True)
-
-    act_sums = lax.fori_loop(0, SIDE, act_sum, jnp.zeros((1, width), F32))
+    sums, squares, act_sums = lax.fori_loop(
+        0, SIDE, second_conv, (zero_half, zero_half, jnp.zeros((1, width), F32))
+    )
 
     def wide_sum(turn, rows):
         own, size = 4 * i + z, rows.shape[0]
         wide[turn, own, pl.ds(0, size)] = rows
-        at = new_recv(16)
-
-        def tile(number):
-            return wide.at[turn, number, pl.ds(0, size)]
-
-        for device in same_core[::-1]:
-            push(tile(own), tile(own), device, at + own)
+        at = new_recv()
+        tile = wide.at[turn, own, pl.ds(0, size)]
+        all_others = wide.at[turn, pl.ds(0, 15), pl.ds(0, size)]
+        push_all([(tile, tile, device) for device in same_core[::-1]], all_others, at)
 
         def finish():
-            for line in (i, *lines):
-                for dz in (0, 1, 2, 3):
-                    if not (line is i and dz == 0):
-                        arrived(tile(4 * line + chip(dz)), at + 4 * line + chip(dz))
+            arrived(all_others, at)
             result = wide[turn, 0, pl.ds(0, size)]
             for n in range(1, 16):
                 result = result + wide[turn, n, pl.ds(0, size)]
@@ -715,24 +816,21 @@
             axis=0,
         ),
     )
-    for dz in (1, 2, 3):
-        head_landed(i, dz)
-        head_forward(i, dz, (xn, c))
-        head_forward(i, dz, (yn, c))
-    inner = act_in[pl.ds(1, SIDE + 1)].reshape((SIDE + 1) * PITCH, per_chip, width)
-    inner = inner[1 : 1 + SIDE * PITCH].reshape(SIDE * rows_c, width)
-    act_t[pl.ds(0, width), :] = inner.T
+    hx_recv, hy_recv, hxy_recv, hyx_recv = new_recv(), new_recv(), new_recv(), new_recv()
+    arrived(head.at[i, pl.ds(0, 3), k], hz_recv)
+    push(line_head, line_head, to_x, hx_recv)
+    push(line_head, line_head, to_y, hy_recv)
     column = lax.broadcasted_iota(jnp.int32, (16, SIDE * rows_c), 1)
     is_real = lax.rem(lax.div(column, per_chip), PITCH) < SIDE
     act_t[pl.ds(width, 16), :] = jnp.where(is_real, 1.0, 0.0).astype(BF16)
     d_pad[pl.ds(0, FRONT)] = jnp.zeros((FRONT, per_chip, half), BF16)
     d_pad[pl.ds(FRONT + SIDE * PITCH, FRONT)] = jnp.zeros((FRONT, per_chip, half), BF16)
-    for dz in (0, 1):
-        head_landed(xn, dz)
-        head_forward(xn, dz, (yn, c))
-    for dz in (2, 3):
-        head_landed(yn, dz)
-        head_forward(yn, dz, (xn, c))
+    arrived(head.at[xn, :, k], hx_recv)
+    half_head = head.at[xn, pl.ds(0, 2), k]
+    push(half_head, half_head, to_y, hxy_recv)
+    arrived(head.at[yn, :, k], hy_recv)
+    half_head = head.at[yn, pl.ds(2, 2), k]
+    push(half_head, half_head, to_x, hyx_recv)
     totals_two = finish()
     total = totals_two[4:5, 0:1]
     mean_two = totals_two[0:1] / count_all
@@ -752,13 +850,12 @@
     pooled = lax.fori_loop(0, SIDE, second_act, jnp.zeros((per_chip, half), F32)) / PIX
     pooled_low = pooled.astype(BF16)
 
-    for line, dz in ((yn, 0), (yn, 1), (xn, 2), (xn, 3), (dg, 0), (dg, 1), (dg, 2), (dg, 3)):
-        head_landed(line, dz)
+    arrived(head.at[dg, pl.ds(0, 2), k], hxy_recv)
+    arrived(head.at[dg, pl.ds(2, 2), k], hyx_recv)
     hd_sib = new_recv()
     theirs = head.at[pl.ds(2 * (1 - k), 2), :, k]
     push(theirs, theirs, (i, sib), hd_sib)
-    for dz in (1, 2, 3):
-        arrived(info.at[chip(dz)], i_recv + chip(dz))
+    arrived(info.at[pl.ds(0, 3)], i_recv)
     slots = info[0] + info[1] + info[2] + info[3]
     arrived(head.at[pl.ds(2 * k, 2), :, 1 - k], hd_sib)
     head_half = head[pl.ds(2 * k, 2)].reshape(half, head.shape[4])
@@ -802,6 +899,11 @@
             [d_gain, d_bias, jnp.broadcast_to(partial, (1, half)), jnp.zeros((5, half), F32)], axis=0
         ),
     )
+    inner = act_in[pl.ds(1, SIDE + 1)].reshape((SIDE + 1) * PITCH, per_chip, width)
+    inner = inner[1 : 1 + SIDE * PITCH].reshape(SIDE * rows_c, width).astype(F32)
+    row = lax.broadcasted_iota(jnp.int32, (SIDE * rows_c, 1), 0)
+    inner = jnp.where(lax.rem(lax.div(row, per_chip), PITCH) < SIDE, inner - centre, 0.0)
+    act_t[pl.ds(0, width), :] = inner.astype(BF16).T
     gh_swap = new_recv()
     gh_half[...] = matmul_tn(pooled_low, d_logits).astype(BF16).reshape(gh_half.shape)
     push(gh_half.at[:, :, 1 - k], gh.at[pl.ds(2 * k, 2)], (i, sib), gh_swap)
@@ -868,23 +970,21 @@
         )
         edge = out[width : width + 1]
         edge_rows[pl.ds(t, 1)] = edge
-        gk[pl.ds(pl.multiple_of(width * t, 32), width), :] = (
-            out[:width] - rank_one(centre, edge)
-        ).astype(BF16)
+        gk[pl.ds(pl.multiple_of(width * t, 32), width), :] = out[:width].astype(BF16)
         return carry
 
     arrived(d_recv, d_at)
     for r in range(UPPER):
         d_send_r = d_act[h0 + r][:SIDE] + d_recv[r].astype(F32)
         d_recv[r] = d_send_r.astype(BF16)
-    b_recv = new_recv(4)
+    b_recv = new_recv()
     back_into = images_of(d_one, 0)
 
     def channels_of(dz):
         return d_recv.at[:, :, :, pl.ds(pl.multiple_of(chip_ch * chip(dz), 128), chip_ch)]
 
-    for dz in (1, 2, 3):
-        push(channels_of(dz), back_into, (i, zdev(dz)), b_recv + z)
+    back_size = d_one.at[:, :, pl.ds(0, 3 * per_chip)]
+    push_all([(channels_of(dz), back_into, to_z[dz - 1]) for dz in (3, 2, 1)], back_size, b_recv)
     keep = pltpu.make_async_copy(channels_of(0), back_into, local_sem.at[UPPER])
     keep.start()
 
@@ -935,8 +1035,7 @@
         push(gh.at[i, chip(dz)], rh_z.at[z], (i, zdev(dz)), h_z + z)
 
     keep.wait()
-    for dz in (1, 2, 3):
-        arrived(images_of(d_one, dz), b_recv + chip(dz))
+    arrived(back_size, b_recv)
 
     def first_back(r, carry):
         sums, products = carry
@@ -1119,8 +1218,7 @@
     one = [a.T for a in (w_one, mom_one, avg_one, mask_one, rank_one_in)]
     two = [a.reshape(flat) for a in (w_two, mom_two, avg_two, mask_two, rank_two)]
     vmem = pl.BlockSpec(memory_space=pltpu.VMEM)
-    smem = pl.BlockSpec(memory_space=pltpu.SMEM)
-    hbm = pl.BlockSpec(memory_space=pl.ANY)
+    hbm = pl.BlockSpec(memory_space=pltpu.HBM)
     v = pltpu.VMEM
     shape = jax.ShapeDtypeStruct
     g_one, g_two, g_head, g_bn_one, g_bn_two, loss = pl.pallas_call(
@@ -1133,9 +1231,19 @@
             shape((2, width), F32),
             shape((1, 128), F32),
         ),
-        in_specs=[hbm, vmem, smem, smem, vmem, vmem, vmem, vmem, vmem, vmem, vmem],
+        in_specs=[hbm] * 11,
         out_specs=[vmem] * 6,
         scratch_shapes=[
+            v((own_ch, cin), F32),
+            v((own_ch, cin), jnp.int32),
+            v(flat, F32),
+            v(flat, jnp.int32),
+            v(top[0].shape, F32),
+            v((2, own_ch), F32),
+            v((2, width), F32),
+            v((1, group), jnp.int32),
+            pltpu.SMEM((per_core,), jnp.int32),
+            pltpu.SMEM((per_core,), jnp.int32),
             v((UPPER * SIDE, group, cin), BF16),
             v((chip_ch, cin), BF16),
             v((TAPS * width, half), BF16),
@@ -1178,6 +1286,7 @@
             v((own_ch, cin), BF16),
             v((2, own_ch, cin), BF16),
             v((2, own_ch, cin), BF16),
+            pltpu.SemaphoreType.DMA((10,)),
             pltpu.SemaphoreType.DMA((UPPER,)),
             pltpu.SemaphoreType.DMA((UPPER + 1,)),
             pltpu.SemaphoreType.DMA((SEMS,)),
@@ -1201,7 +1310,7 @@
         second_norm_params,
     )
     root = math.sqrt(images)
-    steps = 4
+    steps = 2
     one_spec = pl.BlockSpec((own_ch // steps, cin), lambda n: (n, 0))
     two_spec = pl.BlockSpec((flat[0] // steps, 128), lambda n: (n, 0))
     bno_spec = pl.BlockSpec((2, own_ch), lambda n: (0, 0))

time: 125 us -> 107 us (0.86)
  Pallas kernels: 122 us -> 105 us
    pallas_call x1, Pallas kernels: 117 us -> 100 us  [fast_shards(): pl.pallas_call(functools.partial(step_kernel, (group, per_chip, classes,...]
where the time goes in v4:
time: 107 us
  Pallas kernels  105 us (98%)
  between operations  2.42 us (2%)
    pallas_call x1, Pallas kernels, fast_shards(): pl.pallas_call(functools.partial(step_kernel, (group, per_chip, classes,...  100 us
    pallas_call x1, Pallas kernels, fast_shards(): pl.pallas_call(functools.partial(update_kernel, (1.3 * root, 8.0 * root,...  4.56 us

profile of v4, /device:TPU:1, one launch (start us, length us, event | category | flops | bytes accessed | tf_op | source)
XLA Modules:
  0.0 107.2 jit_solution(9084021117681650182)
XLA Ops:
  0.7 100.2 %step.1 = (f32[64,2048]{1,0:T(8,128)}, f32[576,128]{1,0:T(8,128)}, f32[125,128]{1,0:T(8,128)}, f32[2,64]{1,0:T(2,128)}, f32[2,512]{1,0:T(2,128)}, /*index=5*/f32[1,128]{1,0:T(1,128)}) custom-call(bf16[49,64,2048]{2,1,0:T(8,128)(2,1)} %bitcast.30, s32[1,64]{1,0:T(1,128)} %place_in.1, s32[8]{0:T(128)} %labels_in.1, s32[8]{0:T(128)} %loss_wt_in.1, ...), custom_call_target="tpu_custom_call" | custom-call | tf_op jit(solution)/shard_map/step/pallas_call | solution.py:1224
  100.9 4.6 %update.1 = (f32[64,2048]{1,0:T(8,128)}, f32[64,2048]{1,0:T(8,128)}, f32[64,2048]{1,0:T(8,128)}, s32[64,2048]{1,0:T(8,128)}, bf16[64,2048]{1,0:T(8,128)(2,1)}, /...) custom-call(f32[64,2048]{1,0:T(8,128)} %bitcast.32, ...), custom_call_target="tpu_custom_call" | custom-call | tf_op jit(solution)/shard_map/update/pallas_call | solution.py:1320

commit v5 on v4

--- a/solution.py
+++ b/solution.py
@@ -287,7 +287,7 @@
 UPPER = (SIDE + 1) // 2
 PITCH = SIDE + 1
 FRONT = 2 * PITCH
-SEMS = 92
+SENDS, RECEIVES = 48, 95
 
 
 def silu_pair(value):
@@ -387,6 +387,9 @@
     go_recv,
     ga_send,
     ga_recv,
+    kern_t,
+    hat_t,
+    m_two,
     load_sem,
     image_sem,
     local_sem,
@@ -462,6 +465,26 @@
         )
         sent.append(group_copy)
         return group_copy
+
+    def start(at, to, src, dst, device):
+        pltpu.make_async_remote_copy(
+            src_ref=src,
+            dst_ref=dst,
+            send_sem=send.at[at],
+            recv_sem=recv.at[to],
+            device_id=device,
+            device_id_type=MESH,
+        ).start()
+
+    def size_wait(ref, at, to):
+        return pltpu.make_async_remote_copy(
+            src_ref=ref,
+            dst_ref=ref,
+            send_sem=send.at[at],
+            recv_sem=recv.at[to],
+            device_id=(i, sib),
+            device_id_type=MESH,
+        )
 
     def arrived(dst, at):
         pltpu.make_async_remote_copy(
@@ -550,10 +573,13 @@
         at = chunk * (line * 4 + chip(dz)) + block * (k if u == 0 else 1 - k)
         return kern.at[pl.ds(pl.multiple_of(at, 16), block)]
 
+    k_send, k_count = next(next_send), itertools.count(1)
+
     def forward(line, dz, u, *devices):
         for device in devices:
             at = k_recv + 2 * (line * 4 + chip(dz)) + u
-            push(kern_at(line, dz, u), kern_at(line, dz, u), device, at)
+            start(k_send, at, kern_at(line, dz, u), kern_at(line, dz, u), device)
+            next(k_count)
 
     def landed(line, dz, u):
         arrived(kern_at(line, dz, u), k_recv + 2 * (line * 4 + chip(dz)) + u)
@@ -564,7 +590,7 @@
 
     to_x, to_y = (xn, c), (yn, c)
     to_z = [(i, zdev(dz)) for dz in (1, 2, 3)]
-    forward(i, 0, 0, to_x, to_y, *to_z)
+    forward(i, 0, 0, to_x, to_y, *to_z[::-1])
     act_in[0] = jnp.zeros(act_in.shape[1:], BF16)
     for r in range(SIDE + 1, act_in.shape[0]):
         act_in[r] = jnp.zeros(act_in.shape[1:], BF16)
@@ -572,7 +598,7 @@
         act_in[r, 0] = jnp.zeros(act_in.shape[2:], BF16)
     other_block_at = pl.multiple_of(chunk_at + block * (1 - k), 16)
     arrived(kern.at[pl.ds(other_block_at, block)], k_sib)
-    forward(i, 0, 1, to_x, to_y, *to_z)
+    forward(i, 0, 1, to_x, to_y, *to_z[::-1])
     arrived(early.at[1], e_sib)
     both = early[0] + early[1]
     info[z] = both
@@ -594,7 +620,10 @@
         )
 
     zero_row = jnp.zeros((1, chip_ch), F32)
-    sums, squares = lax.fori_loop(0, UPPER, first_conv, (zero_row, zero_row))
+    so_far = lax.fori_loop(0, UPPER // 2, first_conv, (zero_row, zero_row))
+    relay(i, 1, 0, to_x, to_y)
+    relay(xn, 0, 0, to_y)
+    sums, squares = lax.fori_loop(UPPER // 2, UPPER, first_conv, so_far)
 
     def small_sum(turn, rows):
         own = 2 * i + k
@@ -628,9 +657,10 @@
             head_flat[r : r + 1, 128 * j : 128 * j + 128] = rows[j : j + 1]
     head_lane = lax.broadcasted_iota(jnp.int32, (head_rows, 1024), 1)
     head[i, z, k] = jnp.where(head_lane < classes, head_flat[...], 0.0).astype(BF16)
-    relay(i, 1, 0, to_x, to_y)
-    relay(xn, 0, 0, to_y)
     relay(xn, 0, 1, to_y)
+    relay(i, 2, 0, to_x, to_y)
+    relay(i, 1, 1, to_x, to_y)
+    relay(xn, 1, 0, to_y)
     totals = finish()
     mean_one = totals[0:1] / count_all
     inv_one = lax.rsqrt(totals[1:2] / count_all - mean_one * mean_one + EPS)
@@ -641,6 +671,17 @@
         hat = (z_one[at, :] - mean_one) * inv_one
         value, grade = silu_pair(gain_one * hat + bias_one)
         act_out[r] = value.astype(BF16).reshape(SIDE, group, chip_ch)
+        counted = jnp.where(k == 1, 0.0, 1.0) if r == 0 else 1.0
+        d_one[r] = (counted * hat).astype(BF16).reshape(SIDE, group, chip_ch)
+
+    def hat_products(first, last):
+        def step(n, carry):
+            at = pl.ds(pl.multiple_of(256 * n, 256), 256)
+            rows = feats[:, :, at].reshape(UPPER * rows_a, 256)
+            m_two[:, at] = jnp.dot(hat_t[...], rows, preferred_element_type=F32)
+            return carry
+
+        lax.fori_loop(first, last, step, 0)
 
     def into(row, chip_id):
         return act_in.at[
@@ -664,10 +705,6 @@
             images_in_row(act_out, r, 0), into(h0 + r, z), local_sem.at[n]
         )
 
-    relay(i, 2, 0, to_x, to_y)
-    relay(xn, 1, 0, to_y)
-    relay(i, 3, 0, to_x, to_y)
-    relay(i, 1, 1, to_x, to_y)
     for r in range(UPPER):
         first_act(r)
     a_recv, a_more = new_recv(), new_recv()
@@ -710,16 +747,26 @@
     kept = [keep_row(r + k, r) for r in range(common)]
     for copy in kept:
         copy.start()
-    relay(yn, 2, 0, to_x)
+    steps = feats.shape[2] // 256
+    relay(i, 3, 0, to_x, to_y)
     relay(i, 2, 1, to_x, to_y)
     relay(xn, 1, 1, to_y)
+    hat_t[pl.ds(0, chip_ch), :] = d_one[...].reshape(UPPER * rows_a, chip_ch).T
+    place_of = lax.broadcasted_iota(jnp.int32, (16, UPPER * rows_a), 1)
+    hat_t[pl.ds(chip_ch, 16), :] = jnp.where(
+        place_of < jnp.where(k == 1, rows_a, 0), 0.0, 1.0
+    ).astype(BF16)
+    relay(yn, 2, 0, to_x)
+    hat_products(0, steps // 4)
     relay(yn, 3, 0, to_x)
     relay(i, 3, 1, to_x, to_y)
+    hat_products(steps // 4, steps // 2)
     relay(yn, 2, 1, to_x)
     relay(yn, 3, 1, to_x)
     hz_recv = new_recv()
     own_head, line_head = head.at[i, z, k], head.at[i, :, k]
     push_all([(own_head, own_head, device) for device in to_z], head.at[i, pl.ds(0, 3), k], hz_recv)
+    hat_products(steps // 2, steps)
 
     for copy in kept:
         copy.wait()
@@ -746,6 +793,7 @@
     for line, dz in ((yn, 0), (yn, 1), (xn, 2), (xn, 3), (dg, 0), (dg, 1), (dg, 2), (dg, 3)):
         landed(line, dz, 0)
         landed(line, dz, 1)
+    sent.append(size_wait(kern.at[pl.ds(0, block * (next(k_count) - 1))], k_send, k_recv))
     arrived(act_in.at[pl.ds(1 + UPPER * (1 - k), common), pl.ds(1, SIDE)], a_sib)
 
     @pl.when(k == 1)
@@ -757,32 +805,47 @@
         middle.wait_send()
         more_wait.wait_send()
 
+    hx_recv, hy_recv, hxy_recv, hyx_recv = new_recv(), new_recv(), new_recv(), new_recv()
+    arrived(head.at[i, pl.ds(0, 3), k], hz_recv)
+    push(line_head, line_head, to_x, hx_recv)
+    push(line_head, line_head, to_y, hy_recv)
+
+    arrived(info.at[pl.ds(0, 3)], i_recv)
+    slots = info[0] + info[1] + info[2] + info[3]
+    gains = jnp.concatenate([info[n, 0:1] for n in range(4)], axis=1)
+    biases = jnp.concatenate([info[n, 1:2] for n in range(4)], axis=1)
+    spread = math.sqrt(3.0) * gains
+    centre = 2.0 / 3.0 * silu_pair(biases)[0] + 1.0 / 6.0 * (
+        silu_pair(biases + spread)[0] + silu_pair(biases - spread)[0]
+    )
+    centre = centre.astype(BF16).astype(F32)
+
     def tap_of(t):
         return t // 3, t % 3
 
+    def transpose_tap(t):
+        kern_t[pl.ds(pl.multiple_of(half * t, 256), half), :] = kern[
+            pl.ds(pl.multiple_of(width * t, 512), width), :
+        ].T
+
     def second_conv(h, carry):
-        sums, squares, act_sums = carry
-        inner = act_in[h + 1].reshape(rows_c, width).astype(F32)
-        out = jnp.zeros((rows_c, half), F32)
+        sums, squares = carry
+        transpose_tap(h)
+        rows = []
         for t in range(TAPS):
             up, left = tap_of(t)
-            wide = act_in[pl.ds(h + up, 2)].reshape(2 * PITCH, per_chip, width)
-            rows = wide[left : left + PITCH].reshape(rows_c, width)
-            out = out + jnp.dot(
-                rows, kern[pl.ds(width * t, width), :], preferred_element_type=F32
-            )
+            wide_rows = act_in[pl.ds(h + up, 2)].reshape(2 * PITCH, per_chip, width)
+            rows.append(wide_rows[left : left + PITCH].reshape(rows_c, width))
+        out = jnp.dot(jnp.concatenate(rows, axis=1), kern[...], preferred_element_type=F32)
         z_two[h] = out.reshape(PITCH, per_chip, half)
         real = out[: SIDE * per_chip]
         return (
             sums + jnp.sum(real, axis=0, keepdims=True),
             squares + jnp.sum(real * real, axis=0, keepdims=True),
-            act_sums + jnp.sum(inner, axis=0, keepdims=True),
         )
 
     zero_half = jnp.zeros((1, half), F32)
-    sums, squares, act_sums = lax.fori_loop(
-        0, SIDE, second_conv, (zero_half, zero_half, jnp.zeros((1, width), F32))
-    )
+    sums, squares = lax.fori_loop(0, SIDE, second_conv, (zero_half, zero_half))
 
     def wide_sum(turn, rows):
         own, size = 4 * i + z, rows.shape[0]
@@ -808,35 +871,39 @@
             [
                 sums,
                 squares,
-                act_sums[:, :half],
-                act_sums[:, half:],
                 jnp.broadcast_to(chip_weight, (1, half)),
-                jnp.zeros((3, half), F32),
+                jnp.zeros((5, half), F32),
             ],
             axis=0,
         ),
     )
-    hx_recv, hy_recv, hxy_recv, hyx_recv = new_recv(), new_recv(), new_recv(), new_recv()
-    arrived(head.at[i, pl.ds(0, 3), k], hz_recv)
-    push(line_head, line_head, to_x, hx_recv)
-    push(line_head, line_head, to_y, hy_recv)
-    column = lax.broadcasted_iota(jnp.int32, (16, SIDE * rows_c), 1)
-    is_real = lax.rem(lax.div(column, per_chip), PITCH) < SIDE
-    act_t[pl.ds(width, 16), :] = jnp.where(is_real, 1.0, 0.0).astype(BF16)
-    d_pad[pl.ds(0, FRONT)] = jnp.zeros((FRONT, per_chip, half), BF16)
-    d_pad[pl.ds(FRONT + SIDE * PITCH, FRONT)] = jnp.zeros((FRONT, per_chip, half), BF16)
     arrived(head.at[xn, :, k], hx_recv)
     half_head = head.at[xn, pl.ds(0, 2), k]
     push(half_head, half_head, to_y, hxy_recv)
     arrived(head.at[yn, :, k], hy_recv)
     half_head = head.at[yn, pl.ds(2, 2), k]
     push(half_head, half_head, to_x, hyx_recv)
+    for t in range(SIDE, TAPS):
+        transpose_tap(t)
+    inner = act_in[pl.ds(1, SIDE + 1)].reshape((SIDE + 1) * PITCH, per_chip, width)
+    inner = inner[1 : 1 + SIDE * PITCH].reshape(SIDE * rows_c, width).astype(F32)
+    row = lax.broadcasted_iota(jnp.int32, (SIDE * rows_c, 1), 0)
+    inner = jnp.where(lax.rem(lax.div(row, per_chip), PITCH) < SIDE, inner - centre, 0.0)
+    act_t[pl.ds(0, width), :] = inner.astype(BF16).T
+    column = lax.broadcasted_iota(jnp.int32, (16, SIDE * rows_c), 1)
+    is_real = lax.rem(lax.div(column, per_chip), PITCH) < SIDE
+    act_t[pl.ds(width, 16), :] = jnp.where(is_real, 1.0, 0.0).astype(BF16)
+    d_pad[pl.ds(0, FRONT)] = jnp.zeros((FRONT, per_chip, half), BF16)
+    d_pad[pl.ds(FRONT + SIDE * PITCH, FRONT)] = jnp.zeros((FRONT, per_chip, half), BF16)
+    arrived(head.at[dg, pl.ds(0, 2), k], hxy_recv)
+    arrived(head.at[dg, pl.ds(2, 2), k], hyx_recv)
+    hd_sib = new_recv()
+    theirs = head.at[pl.ds(2 * (1 - k), 2), :, k]
+    push(theirs, theirs, (i, sib), hd_sib)
     totals_two = finish()
-    total = totals_two[4:5, 0:1]
+    total = totals_two[2:3, 0:1]
     mean_two = totals_two[0:1] / count_all
     inv_two = lax.rsqrt(totals_two[1:2] / count_all - mean_two * mean_two + EPS)
-    centre = jnp.concatenate([totals_two[2:3], totals_two[3:4]], axis=1) / count_all
-    centre = centre.astype(BF16).astype(F32)
     norms_two = jnp.where(k == 0, norm_two[:, :half], norm_two[:, half:])
     gain_two, bias_two = norms_two[0:1], norms_two[1:2]
 
@@ -850,13 +917,6 @@
     pooled = lax.fori_loop(0, SIDE, second_act, jnp.zeros((per_chip, half), F32)) / PIX
     pooled_low = pooled.astype(BF16)
 
-    arrived(head.at[dg, pl.ds(0, 2), k], hxy_recv)
-    arrived(head.at[dg, pl.ds(2, 2), k], hyx_recv)
-    hd_sib = new_recv()
-    theirs = head.at[pl.ds(2 * (1 - k), 2), :, k]
-    push(theirs, theirs, (i, sib), hd_sib)
-    arrived(info.at[pl.ds(0, 3)], i_recv)
-    slots = info[0] + info[1] + info[2] + info[3]
     arrived(head.at[pl.ds(2 * k, 2), :, 1 - k], hd_sib)
     head_half = head[pl.ds(2 * k, 2)].reshape(half, head.shape[4])
     logit[0] = jnp.dot(pooled_low, head_half, preferred_element_type=F32)
@@ -899,11 +959,6 @@
             [d_gain, d_bias, jnp.broadcast_to(partial, (1, half)), jnp.zeros((5, half), F32)], axis=0
         ),
     )
-    inner = act_in[pl.ds(1, SIDE + 1)].reshape((SIDE + 1) * PITCH, per_chip, width)
-    inner = inner[1 : 1 + SIDE * PITCH].reshape(SIDE * rows_c, width).astype(F32)
-    row = lax.broadcasted_iota(jnp.int32, (SIDE * rows_c, 1), 0)
-    inner = jnp.where(lax.rem(lax.div(row, per_chip), PITCH) < SIDE, inner - centre, 0.0)
-    act_t[pl.ds(0, width), :] = inner.astype(BF16).T
     gh_swap = new_recv()
     gh_half[...] = matmul_tn(pooled_low, d_logits).astype(BF16).reshape(gh_half.shape)
     push(gh_half.at[:, :, 1 - k], gh.at[pl.ds(2 * k, 2)], (i, sib), gh_swap)
@@ -933,36 +988,6 @@
 
     lax.fori_loop(0, SIDE, second_grad, 0)
 
-    def back_conv(h):
-        out = jnp.zeros((rows_c, width), F32)
-        for t in range(TAPS):
-            up, left = tap_of(t)
-            rows = d_pad[pl.ds(PITCH * h + FRONT + PITCH + 1 - PITCH * up - left, PITCH)]
-            out = out + matmul_nt(rows.reshape(rows_c, half), kern[pl.ds(width * t, width), :])
-        return out.reshape(PITCH, per_chip, width)
-
-    s0 = (SIDE - UPPER) * (1 - k)
-
-    def back_theirs(r, carry):
-        out = back_conv(s0 + r)
-        d_act[s0 + r] = out
-        d_send[r] = out[:SIDE].astype(BF16)
-        return carry
-
-    def back_mine(r, carry):
-        d_act[UPPER * k + r] = back_conv(UPPER * k + r)
-        return carry
-
-    lax.fori_loop(0, UPPER, back_theirs, 0)
-    d_at = new_recv()
-    push(d_send, d_recv, (i, sib), d_at)
-    for way, second in enumerate((yn, xn)):
-        part = pl.ds(2 * way, 2)
-        arrived(rh_one.at[way, 1], h_one + 2 * way + 1)
-        gh[second, part] = (gh[second, part].astype(F32) + rh_one[way, 1].astype(F32)).astype(BF16)
-        push(gh.at[second, part], rh_two.at[way], (second, c), h_two + way)
-    lax.fori_loop(0, SIDE - UPPER, back_mine, 0)
-
     def kernel_gradient(t, carry):
         rows = d_pad[pl.ds(FRONT + PITCH + 1 - PITCH * lax.div(t, 3) - lax.rem(t, 3), SIDE * PITCH)]
         out = jnp.dot(
@@ -972,21 +997,6 @@
         edge_rows[pl.ds(t, 1)] = edge
         gk[pl.ds(pl.multiple_of(width * t, 32), width), :] = out[:width].astype(BF16)
         return carry
-
-    arrived(d_recv, d_at)
-    for r in range(UPPER):
-        d_send_r = d_act[h0 + r][:SIDE] + d_recv[r].astype(F32)
-        d_recv[r] = d_send_r.astype(BF16)
-    b_recv = new_recv()
-    back_into = images_of(d_one, 0)
-
-    def channels_of(dz):
-        return d_recv.at[:, :, :, pl.ds(pl.multiple_of(chip_ch * chip(dz), 128), chip_ch)]
-
-    back_size = d_one.at[:, :, pl.ds(0, 3 * per_chip)]
-    push_all([(channels_of(dz), back_into, to_z[dz - 1]) for dz in (3, 2, 1)], back_size, b_recv)
-    keep = pltpu.make_async_copy(channels_of(0), back_into, local_sem.at[UPPER])
-    keep.start()
 
     sent.pop(0).wait_send()
     edge_rows[...] = jnp.zeros(edge_rows.shape, F32)
@@ -998,18 +1008,20 @@
     one_at = {dz: new_recv(2) for dz in (3, 2, 1, 0)}
     two_at = {dz: new_recv() for dz in (3, 2, 1, 0)}
     z_at = new_recv(4)
+    r_send = next(next_send)
+    sent.append(size_wait(gk.at[pl.ds(0, 15 * chunk)], r_send, z_at))
 
     def start_one(dz):
         first, second = ways[dz]
-        push(gk_at(dg, dz), rk_one.at[dz, 1], (first, c), one_at[dz] + 1)
-        push(gk_at(first, dz), rk_one.at[dz, 0], (first, c), one_at[dz])
+        start(r_send, one_at[dz] + 1, gk_at(dg, dz), rk_one.at[dz, 1], (first, c))
+        start(r_send, one_at[dz], gk_at(first, dz), rk_one.at[dz, 0], (first, c))
 
     def start_two(dz):
         first, second = ways[dz]
         arrived(rk_one.at[dz, 1], one_at[dz] + 1)
         into_k = gk_at(second, dz)
         into_k[...] = (into_k[...].astype(F32) + rk_one[dz, 1].astype(F32)).astype(BF16)
-        push(into_k, rk_two.at[dz], (second, c), two_at[dz])
+        start(r_send, two_at[dz], into_k, rk_two.at[dz], (second, c))
 
     def plane_done(dz):
         arrived(rk_one.at[dz, 0], one_at[dz])
@@ -1019,11 +1031,78 @@
         if dz == 0:
             return sum_k
         into_k[...] = sum_k.astype(BF16)
-        push(into_k, rk_z.at[z], (i, zdev(dz)), z_at + z)
+        start(r_send, z_at + z, into_k, rk_z.at[z], to_z[dz - 1])
         return None
 
     start_one(3)
     start_one(2)
+
+    def back_conv(h):
+        rows = []
+        for t in range(TAPS):
+            up, left = tap_of(t)
+            at = PITCH * h + FRONT + PITCH + 1 - PITCH * up - left
+            rows.append(d_pad[pl.ds(at, PITCH)].reshape(rows_c, half))
+        out = jnp.dot(jnp.concatenate(rows, axis=1), kern_t[...], preferred_element_type=F32)
+        return out.reshape(PITCH, per_chip, width)[:SIDE]
+
+    d_at, d_send_at = new_recv(), next(next_send)
+
+    def back_theirs(r, carry):
+        out = back_conv(h0_other + r)
+        d_act[h0_other + r, pl.ds(0, SIDE)] = out
+        d_send[r] = out.astype(BF16)
+        start(d_send_at, d_at, d_send.at[r], d_recv.at[r], (i, sib))
+        return carry
+
+    def channels_of(r, dz):
+        return d_recv.at[r, :, :, pl.ds(pl.multiple_of(chip_ch * chip(dz), 128), chip_ch)]
+
+    def back_row(r, at, to):
+        d_recv[r] = (d_act[h0 + r, pl.ds(0, SIDE)] + d_recv[r].astype(F32)).astype(BF16)
+        for dz in (3, 2, 1):
+            start(at, to, channels_of(r, dz), images_in_row(d_one, r, 0), to_z[dz - 1])
+
+    h0_other = (SIDE - UPPER) * (1 - k)
+    lax.fori_loop(0, UPPER, back_theirs, 0)
+    for way, second in enumerate((yn, xn)):
+        part = pl.ds(2 * way, 2)
+        arrived(rh_one.at[way, 1], h_one + 2 * way + 1)
+        gh[second, part] = (gh[second, part].astype(F32) + rh_one[way, 1].astype(F32)).astype(BF16)
+        push(gh.at[second, part], rh_two.at[way], (second, c), h_two + way)
+    b_recv, b_more = new_recv(), new_recv()
+    b_send, b_more_send = next(next_send), next(next_send)
+
+    d_copy = size_wait(d_send, d_send_at, d_at)
+    sent.append(d_copy)
+    d_act[UPPER * k, pl.ds(0, SIDE)] = back_conv(UPPER * k)
+    d_copy.wait_recv()
+
+    def keep_back(r, n):
+        return pltpu.make_async_copy(
+            channels_of(r, 0), images_in_row(d_one, r, 0), local_sem.at[n]
+        )
+
+    @pl.when(k == 0)
+    def _():
+        back_row(common, b_more_send, b_more)
+        keep_back(common, common).start()
+
+    @pl.when(k == 1)
+    def _():
+        d_one[0] = jnp.zeros(d_one.shape[1:], BF16)
+
+    for r in range(common):
+        if r:
+            d_act[UPPER * k + r, pl.ds(0, SIDE)] = back_conv(UPPER * k + r)
+        back_row(r + k, b_send, b_recv)
+    kept = [keep_back(r + k, r) for r in range(common)]
+    for copy in kept:
+        copy.start()
+    back_copy = size_wait(d_one.at[pl.ds(0, 3), :, pl.ds(0, 3 * per_chip)], b_send, b_recv)
+    back_more = size_wait(d_one.at[0, :, pl.ds(0, 3 * per_chip)], b_more_send, b_more)
+    sent.append(back_copy)
+
     for way in (0, 1):
         part = pl.ds(2 * way, 2)
         arrived(rh_one.at[way, 0], h_one + 2 * way)
@@ -1034,8 +1113,20 @@
     for dz in (3, 2, 1):
         push(gh.at[i, chip(dz)], rh_z.at[z], (i, zdev(dz)), h_z + z)
 
-    keep.wait()
-    arrived(back_size, b_recv)
+    start_two(3)
+    start_two(2)
+    start_one(1)
+    start_one(0)
+    for copy in kept:
+        copy.wait()
+    back_copy.wait_recv()
+
+    @pl.when(k == 0)
+    def _():
+        keep_back(common, common).wait()
+        back_more.wait_recv()
+        back_more.wait_send()
+
 
     def first_back(r, carry):
         sums, products = carry
@@ -1054,15 +1145,14 @@
     finish = small_sum(
         1, jnp.concatenate([d_gain, d_bias, jnp.zeros((6, 128), F32)], axis=0)
     )
-    start_two(3)
-    start_two(2)
-    start_one(1)
-    start_one(0)
     finish_edges = wide_sum(2, edge_rows[...])
-    totals_one = finish()
-    g_bn_one[...] = jnp.where(k == 0, totals_one[0:2, :own_ch], totals_one[0:2, own_ch:])
+    start_two(1)
+    start_two(0)
+    plane_done(3)
+    plane_done(2)
     scale_one = gain_one * inv_one
-    shift_one, lean_one = totals_one[1:2] / count_all, totals_one[0:1] / count_all
+    near_count = count_all / 8
+    shift_near, lean_near = d_bias / near_count, d_gain / near_count
 
     def first_grad(r, carry):
         at = pl.ds(pl.multiple_of(rows_a * r, 64), rows_a)
@@ -1070,7 +1160,7 @@
         _, grade = silu_pair(gain_one * hat + bias_one)
         d_y = d_one[r].reshape(rows_a, chip_ch).astype(F32) * grade
         counted = jnp.where((r == 0) & (k == 1), 0.0, 1.0)
-        grad = (counted * scale_one) * (d_y - shift_one - hat * lean_one)
+        grad = (counted * scale_one) * (d_y - shift_near - hat * lean_near)
         act_out[r] = grad.astype(BF16).reshape(SIDE, group, chip_ch)
         return carry
 
@@ -1087,36 +1177,47 @@
         g_acc[:, at] = jnp.dot(grad_t[...], rows, preferred_element_type=F32)
         return carry
 
-    lax.fori_loop(0, feats.shape[2] // 256, first_weights, 0)
-    low, high = g_acc[:own_ch], g_acc[own_ch:]
-    go_send[...] = jnp.where(k == 0, high, low).astype(BF16)
-    g_at = new_recv()
-    push(go_send, go_recv, (i, sib), g_at)
-    g_one[...] = jnp.where(k == 0, low, high)
-    plane_done(3)
-    plane_done(2)
-    arrived(go_recv, g_at)
-    part = own_ch // 2
-    ga_send[0] = (g_one[...] + go_recv[...].astype(F32)).astype(BF16)
-    first_at, second_at = new_recv(2), new_recv(2)
+    part, columns = own_ch // 2, feats.shape[2] // 2
     upper, lower = pl.ds(0, part), pl.ds(part, part)
-    push(ga_send.at[0, upper], ga_recv.at[0, upper], (xn, c), first_at)
-    push(ga_send.at[0, lower], ga_recv.at[0, lower], (yn, c), first_at + 1)
-    start_two(1)
-    start_two(0)
-    arrived(ga_recv.at[0, upper], first_at)
-    arrived(ga_recv.at[0, lower], first_at + 1)
-    ga_send[1] = (ga_send[0].astype(F32) + ga_recv[0].astype(F32)).astype(BF16)
-    push(ga_send.at[1, upper], ga_recv.at[1, upper], (yn, c), second_at)
-    push(ga_send.at[1, lower], ga_recv.at[1, lower], (xn, c), second_at + 1)
+    sides = [slice(0, columns), slice(columns, 2 * columns)]
+    g_at, first_at, second_at = new_recv(2), new_recv(4), new_recv(4)
+    for n, side in enumerate(sides):
+        lax.fori_loop(columns // 256 * n, columns // 256 * (n + 1), first_weights, 0)
+        if n == 0:
+            totals_one = finish()
+            g_bn_one[...] = jnp.where(k == 0, totals_one[0:2, :own_ch], totals_one[0:2, own_ch:])
+            shift_rest = scale_one * (totals_one[1:2] / count_all - shift_near)
+            lean_rest = scale_one * (totals_one[0:1] / count_all - lean_near)
+            rest = jnp.concatenate([shift_rest, lean_rest, jnp.zeros((6, chip_ch), F32)], axis=0).T
+        g_all = (
+            g_acc[:, side]
+            - rest[:, 0:1] * m_two[chip_ch : chip_ch + 1, side]
+            - rest[:, 1:2] * m_two[:chip_ch, side]
+        )
+        low, high = g_all[:own_ch], g_all[own_ch:]
+        go_send[n] = jnp.where(k == 0, high, low).astype(BF16)
+        push(go_send.at[n], go_recv.at[n], (i, sib), g_at + n)
+        g_one[:, side] = jnp.where(k == 0, low, high)
+    for n, side in enumerate(sides):
+        arrived(go_recv.at[n], g_at + n)
+        ga_send[n] = (g_one[:, side] + go_recv[n].astype(F32)).astype(BF16)
+        push(ga_send.at[n, upper], ga_recv.at[n, upper], to_x, first_at + 2 * n)
+        push(ga_send.at[n, lower], ga_recv.at[n, lower], to_y, first_at + 2 * n + 1)
+    for n in (0, 1):
+        arrived(ga_recv.at[n, upper], first_at + 2 * n)
+        arrived(ga_recv.at[n, lower], first_at + 2 * n + 1)
+        ga_send[2 + n] = (ga_send[n].astype(F32) + ga_recv[n].astype(F32)).astype(BF16)
+        push(ga_send.at[2 + n, upper], ga_recv.at[2 + n, upper], to_y, second_at + 2 * n)
+        push(ga_send.at[2 + n, lower], ga_recv.at[2 + n, lower], to_x, second_at + 2 * n + 1)
 
     edges = finish_edges()
     plane_done(1)
     sum_k = plane_done(0)
 
-    arrived(ga_recv.at[1, upper], second_at)
-    arrived(ga_recv.at[1, lower], second_at + 1)
-    g_one[...] = ga_send[1].astype(F32) + ga_recv[1].astype(F32)
+    for n, side in enumerate(sides):
+        arrived(ga_recv.at[2 + n, upper], second_at + 2 * n)
+        arrived(ga_recv.at[2 + n, lower], second_at + 2 * n + 1)
+        g_one[:, side] = ga_send[2 + n].astype(F32) + ga_recv[2 + n].astype(F32)
 
     row_at = chunk * (i * 4 + z)
     tap = lax.div(row_at, width)
@@ -1282,15 +1383,18 @@
             v((2 * width, half), F32),
             v((chip_ch, UPPER * SIDE * group), BF16),
             v((chip_ch, cin), F32),
-            v((own_ch, cin), BF16),
-            v((own_ch, cin), BF16),
-            v((2, own_ch, cin), BF16),
-            v((2, own_ch, cin), BF16),
+            v((2, own_ch, cin // 2), BF16),
+            v((2, own_ch, cin // 2), BF16),
+            v((4, own_ch, cin // 2), BF16),
+            v((4, own_ch, cin // 2), BF16),
+            v((TAPS * half, width), BF16),
+            v((chip_ch + 16, UPPER * SIDE * group), BF16),
+            v((chip_ch + 16, cin), F32),
             pltpu.SemaphoreType.DMA((10,)),
             pltpu.SemaphoreType.DMA((UPPER,)),
             pltpu.SemaphoreType.DMA((UPPER + 1,)),
-            pltpu.SemaphoreType.DMA((SEMS,)),
-            pltpu.SemaphoreType.DMA((SEMS,)),
+            pltpu.SemaphoreType.DMA((SENDS,)),
+            pltpu.SemaphoreType.DMA((RECEIVES,)),
         ],
         compiler_params=pltpu.CompilerParams(
             collective_id=0, has_side_effects=True, vmem_limit_bytes=56 << 20

time: 107 us -> 101 us (0.944)
  Pallas kernels: 105 us -> 98.4 us
    pallas_call x1, Pallas kernels: 100 us -> 93.9 us  [fast_shards(): pl.pallas_call(functools.partial(step_kernel, (group, per_chip, classes,...]
where the time goes in v5:
time: 101 us
  Pallas kernels  98.4 us (97%)
  between operations  2.42 us (2%)
    pallas_call x1, Pallas kernels, fast_shards(): pl.pallas_call(functools.partial(step_kernel, (group, per_chip, classes,...  93.9 us
    pallas_call x1, Pallas kernels, fast_shards(): pl.pallas_call(functools.partial(update_kernel, (1.3 * root, 8.0 * root,...  4.56 us

profile of v5, /device:TPU:1, one launch (start us, length us, event | category | flops | bytes accessed | tf_op | source)
XLA Modules:
  0.0 100.9 jit_solution(3603234761028406553)
XLA Ops:
  0.7 93.9 %step.1 = (f32[64,2048]{1,0:T(8,128)}, f32[576,128]{1,0:T(8,128)}, f32[125,128]{1,0:T(8,128)}, f32[2,64]{1,0:T(2,128)}, f32[2,512]{1,0:T(2,128)}, /*index=5*/f32[1,128]{1,0:T(1,128)}) custom-call(bf16[49,64,2048]{2,1,0:T(8,128)(2,1)} %bitcast.30, s32[1,64]{1,0:T(1,128)} %place_in.1, s32[8]{0:T(128)} %labels_in.1, s32[8]{0:T(128)} %loss_wt_in.1, ...), custom_call_target="tpu_custom_call" | custom-call | tf_op jit(solution)/shard_map/step/pallas_call | solution.py:1325
  94.6 4.6 %update.1 = (f32[64,2048]{1,0:T(8,128)}, f32[64,2048]{1,0:T(8,128)}, f32[64,2048]{1,0:T(8,128)}, s32[64,2048]{1,0:T(8,128)}, bf16[64,2048]{1,0:T(8,128)(2,1)}, /...) custom-call(f32[64,2048]{1,0:T(8,128)} %bitcast.32, ...), custom_call_target="tpu_custom_call" | custom-call | tf_op jit(solution)/shard_map/update/pallas_call | solution.py:1424

commit v6 on v5

--- a/solution.py
+++ b/solution.py
@@ -287,7 +287,7 @@
 UPPER = (SIDE + 1) // 2
 PITCH = SIDE + 1
 FRONT = 2 * PITCH
-SENDS, RECEIVES = 48, 95
+SENDS, RECEIVES = 48, 102
 
 
 def silu_pair(value):
@@ -390,6 +390,8 @@
     kern_t,
     hat_t,
     m_two,
+    edge_plane,
+    edge_z,
     load_sem,
     image_sem,
     local_sem,
@@ -847,36 +849,32 @@
     zero_half = jnp.zeros((1, half), F32)
     sums, squares = lax.fori_loop(0, SIDE, second_conv, (zero_half, zero_half))
 
+    def folded(*rows):
+        parts = [row[:, n : n + 128] for row in rows for n in range(0, row.shape[1], 128)]
+        parts.append(jnp.zeros((8 - len(parts), 128), F32))
+        return jnp.concatenate(parts, axis=0)
+
+    def unfolded(tile, n):
+        return jnp.concatenate([tile[2 * n : 2 * n + 1], tile[2 * n + 1 : 2 * n + 2]], axis=1)
+
     def wide_sum(turn, rows):
-        own, size = 4 * i + z, rows.shape[0]
-        wide[turn, own, pl.ds(0, size)] = rows
+        own = 4 * i + z
+        wide[turn, own] = rows
         at = new_recv()
-        tile = wide.at[turn, own, pl.ds(0, size)]
-        all_others = wide.at[turn, pl.ds(0, 15), pl.ds(0, size)]
+        tile, all_others = wide.at[turn, own], wide.at[turn, pl.ds(0, 15)]
         push_all([(tile, tile, device) for device in same_core[::-1]], all_others, at)
 
         def finish():
             arrived(all_others, at)
-            result = wide[turn, 0, pl.ds(0, size)]
+            result = wide[turn, 0]
             for n in range(1, 16):
-                result = result + wide[turn, n, pl.ds(0, size)]
+                result = result + wide[turn, n]
             return result
 
         return finish
 
     chip_weight = jnp.sum(both[3:4], axis=1, keepdims=True)
-    finish = wide_sum(
-        0,
-        jnp.concatenate(
-            [
-                sums,
-                squares,
-                jnp.broadcast_to(chip_weight, (1, half)),
-                jnp.zeros((5, half), F32),
-            ],
-            axis=0,
-        ),
-    )
+    finish = wide_sum(0, folded(sums, squares, jnp.broadcast_to(chip_weight, (1, 128))))
     arrived(head.at[xn, :, k], hx_recv)
     half_head = head.at[xn, pl.ds(0, 2), k]
     push(half_head, half_head, to_y, hxy_recv)
@@ -889,10 +887,7 @@
     inner = inner[1 : 1 + SIDE * PITCH].reshape(SIDE * rows_c, width).astype(F32)
     row = lax.broadcasted_iota(jnp.int32, (SIDE * rows_c, 1), 0)
     inner = jnp.where(lax.rem(lax.div(row, per_chip), PITCH) < SIDE, inner - centre, 0.0)
-    act_t[pl.ds(0, width), :] = inner.astype(BF16).T
-    column = lax.broadcasted_iota(jnp.int32, (16, SIDE * rows_c), 1)
-    is_real = lax.rem(lax.div(column, per_chip), PITCH) < SIDE
-    act_t[pl.ds(width, 16), :] = jnp.where(is_real, 1.0, 0.0).astype(BF16)
+    act_t[...] = inner.astype(BF16).T
     d_pad[pl.ds(0, FRONT)] = jnp.zeros((FRONT, per_chip, half), BF16)
     d_pad[pl.ds(FRONT + SIDE * PITCH, FRONT)] = jnp.zeros((FRONT, per_chip, half), BF16)
     arrived(head.at[dg, pl.ds(0, 2), k], hxy_recv)
@@ -901,9 +896,9 @@
     theirs = head.at[pl.ds(2 * (1 - k), 2), :, k]
     push(theirs, theirs, (i, sib), hd_sib)
     totals_two = finish()
-    total = totals_two[2:3, 0:1]
-    mean_two = totals_two[0:1] / count_all
-    inv_two = lax.rsqrt(totals_two[1:2] / count_all - mean_two * mean_two + EPS)
+    total = totals_two[4:5, 0:1]
+    mean_two = unfolded(totals_two, 0) / count_all
+    inv_two = lax.rsqrt(unfolded(totals_two, 1) / count_all - mean_two * mean_two + EPS)
     norms_two = jnp.where(k == 0, norm_two[:, :half], norm_two[:, half:])
     gain_two, bias_two = norms_two[0:1], norms_two[1:2]
 
@@ -953,12 +948,7 @@
 
     d_bias, d_gain = lax.fori_loop(0, SIDE, second_back, (zero_half, zero_half))
 
-    finish = wide_sum(
-        1,
-        jnp.concatenate(
-            [d_gain, d_bias, jnp.broadcast_to(partial, (1, half)), jnp.zeros((5, half), F32)], axis=0
-        ),
-    )
+    finish = wide_sum(1, folded(d_gain, d_bias, jnp.broadcast_to(partial, (1, 128))))
     gh_swap = new_recv()
     gh_half[...] = matmul_tn(pooled_low, d_logits).astype(BF16).reshape(gh_half.shape)
     push(gh_half.at[:, :, 1 - k], gh.at[pl.ds(2 * k, 2)], (i, sib), gh_swap)
@@ -972,12 +962,12 @@
         push(gh.at[dg, part], rh_one.at[way, 1], (first, c), h_one + 2 * way + 1)
         push(gh.at[first, part], rh_one.at[way, 0], (first, c), h_one + 2 * way)
     totals_back = finish()
-    loss[...] = totals_back[2:3, :128]
+    loss[...] = totals_back[4:5]
     wide_sib[0] = totals_back
     bn_at = new_recv()
     push(wide_sib.at[0], wide_sib.at[1], (i, sib), bn_at)
     scale = gain_two * inv_two
-    shift_two, lean_two = totals_back[1:2] / count_all, totals_back[0:1] / count_all
+    shift_two, lean_two = unfolded(totals_back, 1) / count_all, unfolded(totals_back, 0) / count_all
 
     def second_grad(h, carry):
         grad = scale * (slope[h] - shift_two - z_two[h] * lean_two)
@@ -988,44 +978,77 @@
 
     lax.fori_loop(0, SIDE, second_grad, 0)
 
-    def kernel_gradient(t, carry):
-        rows = d_pad[pl.ds(FRONT + PITCH + 1 - PITCH * lax.div(t, 3) - lax.rem(t, 3), SIDE * PITCH)]
-        out = jnp.dot(
-            act_t[...], rows.reshape(SIDE * rows_c, half), preferred_element_type=F32
-        )
-        edge = out[width : width + 1]
-        edge_rows[pl.ds(t, 1)] = edge
-        gk[pl.ds(pl.multiple_of(width * t, 32), width), :] = out[:width].astype(BF16)
-        return carry
+    def shifted(t):
+        at = FRONT + PITCH + 1 - PITCH * lax.div(t, 3) - lax.rem(t, 3)
+        return d_pad[pl.ds(at, SIDE * PITCH)].reshape(SIDE * rows_c, half)
+
+    def kernel_gradient(line):
+        def granule(n, carry):
+            at = 4 * chunk * line + 128 * n
+            tap = lax.div(at, width)
+            rows = act_t[pl.ds(pl.multiple_of(at - width * tap, 128), 128), :]
+            gk[pl.ds(pl.multiple_of(at, 128), 128), :] = jnp.dot(
+                rows, shifted(tap), preferred_element_type=F32
+            ).astype(BF16)
+            return carry
+
+        lax.fori_loop(0, 4 * chunk // 128, granule, 0)
+
+    def edge_sums():
+        maps = d_pad[pl.ds(FRONT, SIDE * PITCH)].astype(F32).reshape(SIDE, PITCH, per_chip, half)
+        across = jnp.sum(maps[:, :SIDE], axis=1)
+        for left, rows in enumerate((across - maps[:, 0], across, across - maps[:, SIDE - 1])):
+            down = jnp.sum(rows, axis=0)
+            for up, part in enumerate((down - rows[0], down, down - rows[SIDE - 1])):
+                t = 3 * up + left
+                edge_rows[t : t + 1] = jnp.sum(part, axis=0, keepdims=True)
 
     sent.pop(0).wait_send()
-    edge_rows[...] = jnp.zeros(edge_rows.shape, F32)
-    lax.fori_loop(0, TAPS, kernel_gradient, 0)
     def gk_at(line, dz):
         return gk.at[pl.ds(pl.multiple_of(chunk * (line * 4 + chip(dz)), 32), chunk)]
 
-    ways = {1: (xn, yn), 2: (yn, xn), 3: (xn, yn), 0: (yn, xn)}
-    one_at = {dz: new_recv(2) for dz in (3, 2, 1, 0)}
-    two_at = {dz: new_recv() for dz in (3, 2, 1, 0)}
+    whole, first_half, second_half = (0, chunk), (0, block), (block, block)
+    units = {
+        3: ((whole, xn, yn),),
+        2: ((whole, yn, xn),),
+        1: ((first_half, xn, yn), (second_half, yn, xn)),
+        0: ((first_half, xn, yn), (second_half, yn, xn)),
+    }
+    one_at = {dz: new_recv(2 * len(units[dz])) for dz in units}
+    two_at = {dz: new_recv(len(units[dz])) for dz in units}
     z_at = new_recv(4)
     r_send = next(next_send)
     sent.append(size_wait(gk.at[pl.ds(0, 15 * chunk)], r_send, z_at))
 
-    def start_one(dz):
-        first, second = ways[dz]
-        start(r_send, one_at[dz] + 1, gk_at(dg, dz), rk_one.at[dz, 1], (first, c))
-        start(r_send, one_at[dz], gk_at(first, dz), rk_one.at[dz, 0], (first, c))
+    def rows_of(ref, part):
+        return ref.at[pl.ds(part[0], part[1])]
+
+    def gk_part(line, dz, part):
+        at = chunk * (line * 4 + chip(dz)) + part[0]
+        return gk.at[pl.ds(pl.multiple_of(at, 16), part[1])]
+
+    def start_far(dz):
+        for n, (part, first, second) in enumerate(units[dz]):
+            into_part = rows_of(rk_one.at[dz, 1], part)
+            start(r_send, one_at[dz] + 2 * n + 1, gk_part(dg, dz, part), into_part, (first, c))
+
+    def start_near(dz):
+        for n, (part, first, second) in enumerate(units[dz]):
+            into_part = rows_of(rk_one.at[dz, 0], part)
+            start(r_send, one_at[dz] + 2 * n, gk_part(first, dz, part), into_part, (first, c))
 
     def start_two(dz):
-        first, second = ways[dz]
-        arrived(rk_one.at[dz, 1], one_at[dz] + 1)
-        into_k = gk_at(second, dz)
-        into_k[...] = (into_k[...].astype(F32) + rk_one[dz, 1].astype(F32)).astype(BF16)
-        start(r_send, two_at[dz], into_k, rk_two.at[dz], (second, c))
+        for n, (part, first, second) in enumerate(units[dz]):
+            came = rows_of(rk_one.at[dz, 1], part)
+            arrived(came, one_at[dz] + 2 * n + 1)
+            into_k = gk_part(second, dz, part)
+            into_k[...] = (into_k[...].astype(F32) + came[...].astype(F32)).astype(BF16)
+            start(r_send, two_at[dz] + n, into_k, rows_of(rk_two.at[dz], part), (second, c))
 
     def plane_done(dz):
-        arrived(rk_one.at[dz, 0], one_at[dz])
-        arrived(rk_two.at[dz], two_at[dz])
+        for n, (part, first, second) in enumerate(units[dz]):
+            arrived(rows_of(rk_one.at[dz, 0], part), one_at[dz] + 2 * n)
+            arrived(rows_of(rk_two.at[dz], part), two_at[dz] + n)
         into_k = gk_at(i, dz)
         sum_k = into_k[...].astype(F32) + rk_one[dz, 0].astype(F32) + rk_two[dz].astype(F32)
         if dz == 0:
@@ -1033,9 +1056,6 @@
         into_k[...] = sum_k.astype(BF16)
         start(r_send, z_at + z, into_k, rk_z.at[z], to_z[dz - 1])
         return None
-
-    start_one(3)
-    start_one(2)
 
     def back_conv(h):
         rows = []
@@ -1065,6 +1085,9 @@
 
     h0_other = (SIDE - UPPER) * (1 - k)
     lax.fori_loop(0, UPPER, back_theirs, 0)
+    kernel_gradient(dg)
+    start_far(3)
+    start_far(2)
     for way, second in enumerate((yn, xn)):
         part = pl.ds(2 * way, 2)
         arrived(rh_one.at[way, 1], h_one + 2 * way + 1)
@@ -1102,6 +1125,10 @@
     back_copy = size_wait(d_one.at[pl.ds(0, 3), :, pl.ds(0, 3 * per_chip)], b_send, b_recv)
     back_more = size_wait(d_one.at[0, :, pl.ds(0, 3 * per_chip)], b_more_send, b_more)
     sent.append(back_copy)
+    kernel_gradient(xn)
+    start_near(3)
+    kernel_gradient(yn)
+    start_near(2)
 
     for way in (0, 1):
         part = pl.ds(2 * way, 2)
@@ -1115,8 +1142,12 @@
 
     start_two(3)
     start_two(2)
-    start_one(1)
-    start_one(0)
+    for dz in (1, 0):
+        start_far(dz)
+        start_near(dz)
+    kernel_gradient(i)
+    edge_rows[...] = jnp.zeros(edge_rows.shape, F32)
+    edge_sums()
     for copy in kept:
         copy.wait()
     back_copy.wait_recv()
@@ -1145,7 +1176,13 @@
     finish = small_sum(
         1, jnp.concatenate([d_gain, d_bias, jnp.zeros((6, 128), F32)], axis=0)
     )
-    finish_edges = wide_sum(2, edge_rows[...])
+    edge_at, edge_z_at = new_recv(), new_recv()
+    edge_plane[i] = edge_rows[...]
+    push_all(
+        [(edge_plane.at[i], edge_plane.at[i], (line, c)) for line in lines],
+        edge_plane.at[pl.ds(0, 3)],
+        edge_at,
+    )
     start_two(1)
     start_two(0)
     plane_done(3)
@@ -1203,6 +1240,12 @@
         ga_send[n] = (g_one[:, side] + go_recv[n].astype(F32)).astype(BF16)
         push(ga_send.at[n, upper], ga_recv.at[n, upper], to_x, first_at + 2 * n)
         push(ga_send.at[n, lower], ga_recv.at[n, lower], to_y, first_at + 2 * n + 1)
+    plane_done(1)
+    arrived(edge_plane.at[pl.ds(0, 3)], edge_at)
+    edge_z[z] = edge_plane[0] + edge_plane[1] + edge_plane[2] + edge_plane[3]
+    push_all(
+        [(edge_z.at[z], edge_z.at[z], device) for device in to_z], edge_z.at[pl.ds(0, 3)], edge_z_at
+    )
     for n in (0, 1):
         arrived(ga_recv.at[n, upper], first_at + 2 * n)
         arrived(ga_recv.at[n, lower], first_at + 2 * n + 1)
@@ -1210,8 +1253,8 @@
         push(ga_send.at[2 + n, upper], ga_recv.at[2 + n, upper], to_y, second_at + 2 * n)
         push(ga_send.at[2 + n, lower], ga_recv.at[2 + n, lower], to_x, second_at + 2 * n + 1)
 
-    edges = finish_edges()
-    plane_done(1)
+    arrived(edge_z.at[pl.ds(0, 3)], edge_z_at)
+    edges = edge_z[0] + edge_z[1] + edge_z[2] + edge_z[3]
     sum_k = plane_done(0)
 
     for n, side in enumerate(sides):
@@ -1262,11 +1305,13 @@
         )
 
     arrived(wide_sib.at[1], bn_at)
-    own_bn, other_bn = wide_sib[0], wide_sib[1]
+    own_bn, other_bn = (
+        jnp.concatenate([unfolded(wide_sib[n], 0), unfolded(wide_sib[n], 1)], axis=0) for n in (0, 1)
+    )
     g_bn_two[...] = jnp.where(
         k == 0,
-        jnp.concatenate([own_bn[0:2], other_bn[0:2]], axis=1),
-        jnp.concatenate([other_bn[0:2], own_bn[0:2]], axis=1),
+        jnp.concatenate([own_bn, other_bn], axis=1),
+        jnp.concatenate([other_bn, own_bn], axis=1),
     )
     for copy in sent:
         copy.wait_send()
@@ -1355,7 +1400,7 @@
             v((SIDE, PITCH, per_chip, half), F32),
             v((SIDE, PITCH, per_chip, half), F32),
             v((2 * FRONT + SIDE * PITCH, per_chip, half), BF16),
-            v((width + 16, SIDE * PITCH * per_chip), BF16),
+            v((width, SIDE * PITCH * per_chip), BF16),
             v((SIDE, PITCH, per_chip, width), F32),
             v((UPPER, SIDE, per_chip, width), BF16),
             v((UPPER, SIDE, per_chip, width), BF16),
@@ -1363,8 +1408,8 @@
             v((2, 8, 128), F32),
             v((4, 8, 128), F32),
             v((2, 8, 8, 128), F32),
-            v((3, 16, 16, half), F32),
-            v((2, 8, half), F32),
+            v((2, 16, 8, 128), F32),
+            v((2, 8, 128), F32),
             v((2, per_chip, lanes), F32),
             v((2, 4, 2, head_rows, lanes), BF16),
             v((TAPS * width, half), BF16),
@@ -1390,6 +1435,8 @@
             v((TAPS * half, width), BF16),
             v((chip_ch + 16, UPPER * SIDE * group), BF16),
             v((chip_ch + 16, cin), F32),
+            v((4, 16, half), F32),
+            v((4, 16, half), F32),
             pltpu.SemaphoreType.DMA((10,)),
             pltpu.SemaphoreType.DMA((UPPER,)),
             pltpu.SemaphoreType.DMA((UPPER + 1,)),

time: 101 us -> 97.6 us (0.966)
  Pallas kernels: 98.4 us -> 95 us
    pallas_call x1, Pallas kernels: 93.9 us -> 90.4 us  [fast_shards(): pl.pallas_call(functools.partial(step_kernel, (group, per_chip, classes,...]
where the time goes in v6:
time: 97.6 us; the launch traced here: 97.4 us
  Pallas kernels  95 us (97%)
  between operations  2.42 us (2%)
    pallas_call x1, Pallas kernels, fast_shards(): pl.pallas_call(functools.partial(step_kernel, (group, per_chip, classes,...  90.4 us
    pallas_call x1, Pallas kernels, fast_shards(): pl.pallas_call(functools.partial(update_kernel, (1.3 * root, 8.0 * root,...  4.56 us

profile of v6, /device:TPU:1, one launch (start us, length us, event | category | flops | bytes accessed | tf_op | source)
XLA Modules:
  0.0 97.4 jit_solution(15693770413953649096)
XLA Ops:
  0.7 90.4 %step.1 = (f32[64,2048]{1,0:T(8,128)}, f32[576,128]{1,0:T(8,128)}, f32[125,128]{1,0:T(8,128)}, f32[2,64]{1,0:T(2,128)}, f32[2,512]{1,0:T(2,128)}, /*index=5*/f32[1,128]{1,0:T(1,128)}) custom-call(bf16[49,64,2048]{2,1,0:T(8,128)(2,1)} %bitcast.30, s32[1,64]{1,0:T(1,128)} %place_in.1, s32[8]{0:T(128)} %labels_in.1, s32[8]{0:T(128)} %loss_wt_in.1, ...), custom_call_target="tpu_custom_call" | custom-call | tf_op jit(solution)/shard_map/step/pallas_call | solution.py:1370
  91.1 4.6 %update.1 = (f32[64,2048]{1,0:T(8,128)}, f32[64,2048]{1,0:T(8,128)}, f32[64,2048]{1,0:T(8,128)}, s32[64,2048]{1,0:T(8,128)}, bf16[64,2048]{1,0:T(8,128)(2,1)}, /...) custom-call(f32[64,2048]{1,0:T(8,128)} %bitcast.32, ...), custom_call_target="tpu_custom_call" | custom-call | tf_op jit(solution)/shard_map/update/pallas_call | solution.py:1471

commit v7 on v6

--- a/solution.py
+++ b/solution.py
@@ -992,7 +992,7 @@
             ).astype(BF16)
             return carry
 
-        lax.fori_loop(0, 4 * chunk // 128, granule, 0)
+        lax.fori_loop(0, 4 * chunk // 128, granule, 0, unroll=3)
 
     def edge_sums():
         maps = d_pad[pl.ds(FRONT, SIDE * PITCH)].astype(F32).reshape(SIDE, PITCH, per_chip, half)
@@ -1057,22 +1057,26 @@
         start(r_send, z_at + z, into_k, rk_z.at[z], to_z[dz - 1])
         return None
 
-    def back_conv(h):
-        rows = []
-        for t in range(TAPS):
-            up, left = tap_of(t)
-            at = PITCH * h + FRONT + PITCH + 1 - PITCH * up - left
-            rows.append(d_pad[pl.ds(at, PITCH)].reshape(rows_c, half))
-        out = jnp.dot(jnp.concatenate(rows, axis=1), kern_t[...], preferred_element_type=F32)
-        return out.reshape(PITCH, per_chip, width)[:SIDE]
+    def back_conv(h, count):
+        lines_in = []
+        for n in range(count):
+            rows = []
+            for t in range(TAPS):
+                up, left = tap_of(t)
+                at = PITCH * (h + n) + FRONT + PITCH + 1 - PITCH * up - left
+                rows.append(d_pad[pl.ds(at, PITCH)].reshape(rows_c, half))
+            lines_in.append(jnp.concatenate(rows, axis=1))
+        out = jnp.dot(jnp.concatenate(lines_in, axis=0), kern_t[...], preferred_element_type=F32)
+        return out.reshape(count, PITCH, per_chip, width)[:, :SIDE]
 
     d_at, d_send_at = new_recv(), next(next_send)
 
-    def back_theirs(r, carry):
-        out = back_conv(h0_other + r)
-        d_act[h0_other + r, pl.ds(0, SIDE)] = out
-        d_send[r] = out.astype(BF16)
-        start(d_send_at, d_at, d_send.at[r], d_recv.at[r], (i, sib))
+    def back_theirs(n, carry):
+        at = pl.ds(2 * n, 2)
+        out = back_conv(h0_other + 2 * n, 2)
+        d_act[pl.ds(h0_other + 2 * n, 2), pl.ds(0, SIDE)] = out
+        d_send[at] = out.astype(BF16)
+        start(d_send_at, d_at, d_send.at[at], d_recv.at[at], (i, sib))
         return carry
 
     def channels_of(r, dz):
@@ -1084,7 +1088,7 @@
             start(at, to, channels_of(r, dz), images_in_row(d_one, r, 0), to_z[dz - 1])
 
     h0_other = (SIDE - UPPER) * (1 - k)
-    lax.fori_loop(0, UPPER, back_theirs, 0)
+    lax.fori_loop(0, UPPER // 2, back_theirs, 0)
     kernel_gradient(dg)
     start_far(3)
     start_far(2)
@@ -1098,7 +1102,7 @@
 
     d_copy = size_wait(d_send, d_send_at, d_at)
     sent.append(d_copy)
-    d_act[UPPER * k, pl.ds(0, SIDE)] = back_conv(UPPER * k)
+    d_act[pl.ds(UPPER * k, 2), pl.ds(0, SIDE)] = back_conv(UPPER * k, 2)
     d_copy.wait_recv()
 
     def keep_back(r, n):
@@ -1116,8 +1120,8 @@
         d_one[0] = jnp.zeros(d_one.shape[1:], BF16)
 
     for r in range(common):
-        if r:
-            d_act[UPPER * k + r, pl.ds(0, SIDE)] = back_conv(UPPER * k + r)
+        if r == 2:
+            d_act[UPPER * k + r, pl.ds(0, SIDE)] = back_conv(UPPER * k + r, 1)[0]
         back_row(r + k, b_send, b_recv)
     kept = [keep_back(r + k, r) for r in range(common)]
     for copy in kept:

time: 97.6 us -> 95.8 us (0.982)
  Pallas kernels: 95 us -> 93.3 us
    pallas_call x1, Pallas kernels: 90.4 us -> 88.7 us  [fast_shards(): pl.pallas_call(functools.partial(step_kernel, (group, per_chip, classes,...]
where the time goes in v7:
time: 95.8 us; the launch traced here: 95.7 us
  Pallas kernels  93.3 us (97%)
  between operations  2.42 us (3%)
    pallas_call x1, Pallas kernels, fast_shards(): pl.pallas_call(functools.partial(step_kernel, (group, per_chip, classes,...  88.7 us
    pallas_call x1, Pallas kernels, fast_shards(): pl.pallas_call(functools.partial(update_kernel, (1.3 * root, 8.0 * root,...  4.56 us

profile of v7, /device:TPU:1, one launch (start us, length us, event | category | flops | bytes accessed | tf_op | source)
XLA Modules:
  0.0 95.7 jit_solution(4689620449804430204)
XLA Ops:
  0.7 88.7 %step.1 = (f32[64,2048]{1,0:T(8,128)}, f32[576,128]{1,0:T(8,128)}, f32[125,128]{1,0:T(8,128)}, f32[2,64]{1,0:T(2,128)}, f32[2,512]{1,0:T(2,128)}, /*index=5*/f32[1,128]{1,0:T(1,128)}) custom-call(bf16[49,64,2048]{2,1,0:T(8,128)(2,1)} %bitcast.30, s32[1,64]{1,0:T(1,128)} %place_in.1, s32[8]{0:T(128)} %labels_in.1, s32[8]{0:T(128)} %loss_wt_in.1, ...), custom_call_target="tpu_custom_call" | custom-call | tf_op jit(solution)/shard_map/step/pallas_call | solution.py:1374
  89.4 4.6 %update.1 = (f32[64,2048]{1,0:T(8,128)}, f32[64,2048]{1,0:T(8,128)}, f32[64,2048]{1,0:T(8,128)}, s32[64,2048]{1,0:T(8,128)}, bf16[64,2048]{1,0:T(8,128)(2,1)}, /...) custom-call(f32[64,2048]{1,0:T(8,128)} %bitcast.32, ...), custom_call_target="tpu_custom_call" | custom-call | tf_op jit(solution)/shard_map/update/pallas_call | solution.py:1475
